TPU v7x, 32 devices: a whole 2x2x4 slice. The times are simulated.
32 devices in a mesh: frames: 2 (over y), patches: 16 (over z, x, core).
Axes of the slice: x: 2, y: 2, z: 4, core: 2. Of those that a mesh axis runs over, the one named last changes fastest.
Arguments:
- tokens: bfloat16 [18, 1536, 1152], P('frames', 'patches'), may hold values from -6 to 6
- cotangent: bfloat16 [18, 1536, 1152], P('frames', 'patches'), may hold values from -6 to 6
- caption: bfloat16 [4, 120, 1152], replicated, may hold values from -6 to 6
- null_embed: bfloat16 [120, 1152], replicated, may hold values from -6 to 6
- timesteps: int32 [4], replicated, may hold values from 0 to 999
- null_mask: int32 [4], replicated, may hold values from 0 to 1, as said below
- bucket_sizes: int32 [4], replicated, may hold values from 1 to 576, 1536 in all
- patch_mask: int32 [1536], P('patches'), may hold values 0 or 1
- frame_counts: int32 [2], P('frames'), may hold values from 1 to 9, 17 in all
- table: bfloat16 [6, 1152], replicated, may hold values from -3 to 3
- time_proj: bfloat16 [256, 6912], P('patches', 'frames'), may hold values from -0.375 to 0.375
- self_qkv: bfloat16 [1152, 3456], P('patches', 'frames'), may hold values from -0.1875 to 0.1875
- self_out: bfloat16 [1152, 1152], P('patches', 'frames'), may hold values from -0.25 to 0.25
- cross_q: bfloat16 [1152, 1152], P('patches', 'frames'), may hold values from -0.1875 to 0.1875
- cross_kv: bfloat16 [1152, 2304], P('patches', 'frames'), may hold values from -0.1875 to 0.1875
- cross_out: bfloat16 [1152, 1152], P('patches', 'frames'), may hold values from -0.75 to 0.75
- mlp_in: bfloat16 [1152, 4608], P('patches', 'frames'), may hold values from -0.1875 to 0.1875
- mlp_out: bfloat16 [4608, 1152], P('patches', 'frames'), may hold values from -0.09375 to 0.09375
- biases: bfloat16 [7, 1152], replicated, may hold values from -3 to 3
- hidden_bias: bfloat16 [4608], replicated, may hold values from -3 to 3
Outputs:
- block_out: bfloat16 [18, 1536, 1152], P('frames', 'patches')
- input_grad: float32 [18, 1536, 1152], P('frames', 'patches')
- caption_grad: float32 [4, 120, 1152], replicated
- null_grad: float32 [120, 1152], replicated
- table_grad: float32 [6, 1152], replicated
- time_proj_grad: float32 [256, 6912], P('patches', 'frames')
- self_qkv_grad: float32 [1152, 3456], P('patches', 'frames')
- self_out_grad: float32 [1152, 1152], P('patches', 'frames')
- cross_q_grad: float32 [1152, 1152], P('patches', 'frames')
- cross_kv_grad: float32 [1152, 2304], P('patches', 'frames')
- cross_out_grad: float32 [1152, 1152], P('patches', 'frames')
- mlp_in_grad: float32 [1152, 4608], P('patches', 'frames')
- mlp_out_grad: float32 [4608, 1152], P('patches', 'frames')
- biases_grad: float32 [7, 1152], replicated
- hidden_bias_grad: float32 [4608], replicated
Inputs may be any that keep to these rules, and one draw needn't show every extreme that they name: `null_mask`: at least one clip and at most 2 clips take the null caption. `frame_counts`: the counts sum to 17; index i of frames holds the frames after those of lower indices. `bucket_sizes`: the sizes sum to 1536; clip c takes the positions after those of lower clips.
All inputs are finite; a program needn't handle non-finite values. No bound on the sum of `patch_mask` or of `frame_counts` on one device may be relied on, other than what follows from the above.
Results may differ from a plain program's by a relative error of at most 0.028.
Values may be sent and summed in bfloat16 or wider, within the bound.
A program may use at most 384 MiB of HBM per device.

v0:
```python
from functools import partial
import math

import jax
import jax.numpy as jnp
from jax import lax
from jax.sharding import PartitionSpec as P

HEADS = 16


HIGH = lax.Precision.HIGHEST


def with_halo(shard, sides, width):
    for axis, dim in sides:
        count, length = (lax.axis_size(axis), shard.shape[dim])
        up = [(i, (i + 1) % count) for i in range(count - 1)]
        down = [(j, i) for i, j in up]
        last = lax.slice_in_dim(shard, length - width, length, axis=dim)
        initial = lax.slice_in_dim(shard, 0, width, axis=dim)
        before = lax.ppermute(last, axis, up)
        after = lax.ppermute(initial, axis, down)
        shard = jnp.concatenate([before, shard, after], axis=dim)
    return shard


def layer_norm(values):
    mean = jnp.mean(values, axis=-1, keepdims=True)
    centered = values - mean
    variance = jnp.mean(centered * centered, axis=-1, keepdims=True)
    return centered * lax.rsqrt(variance + 1e-06)


def modulate(values, shift, scale):
    return layer_norm(values) * (1.0 + scale) + shift


def time_features(timesteps, width):
    half = width // 2
    freqs = jnp.exp(-math.log(10000.0) * jnp.arange(half, dtype=jnp.float32) / half)
    angles = timesteps.astype(jnp.float32)[:, None] * freqs[None, :]
    return jnp.concatenate([jnp.cos(angles), jnp.sin(angles)], axis=1)


def gelu_tanh(values):
    return jax.nn.gelu(values, approximate=True)


def forward_dot(left, right):
    return jnp.dot(left, right, preferred_element_type=jnp.float32)


def outer_sum(left, right):
    return jnp.einsum("rd,re->de", left, right, preferred_element_type=jnp.float32)


def times_transposed(grad, weight):
    return jnp.einsum("re,de->rd", grad, weight, preferred_element_type=jnp.float32)


def round_trip(values):
    return lax.optimization_barrier(values.astype(jnp.bfloat16)).astype(jnp.float32)


def gather_forward(shards):
    row_parts = (
        lax.all_gather(shards[0], "patches", axis=0, tiled=True),
        lax.all_gather(shards[1], "patches", axis=0, tiled=True),
        lax.all_gather(shards[2], "patches", axis=0, tiled=True),
        lax.all_gather(shards[3], "patches", axis=0, tiled=True),
        lax.all_gather(shards[4], "patches", axis=0, tiled=True),
        lax.all_gather(shards[5], "patches", axis=0, tiled=True),
        lax.all_gather(shards[6], "patches", axis=0, tiled=True),
        lax.all_gather(shards[7], "patches", axis=0, tiled=True),
    )
    return (
        lax.all_gather(row_parts[0], "frames", axis=1, tiled=True),
        lax.all_gather(row_parts[1], "frames", axis=1, tiled=True),
        lax.all_gather(row_parts[2], "frames", axis=1, tiled=True),
        lax.all_gather(row_parts[3], "frames", axis=1, tiled=True),
        lax.all_gather(row_parts[4], "frames", axis=1, tiled=True),
        lax.all_gather(row_parts[5], "frames", axis=1, tiled=True),
        lax.all_gather(row_parts[6], "frames", axis=1, tiled=True),
        lax.all_gather(row_parts[7], "frames", axis=1, tiled=True),
    )


def gather_backward(shards):
    row_parts = (
        lax.all_gather(shards[0], "patches", axis=0, tiled=True),
        lax.all_gather(shards[1], "patches", axis=0, tiled=True),
        lax.all_gather(shards[2], "patches", axis=0, tiled=True),
        lax.all_gather(shards[3], "patches", axis=0, tiled=True),
        lax.all_gather(shards[4], "patches", axis=0, tiled=True),
        lax.all_gather(shards[5], "patches", axis=0, tiled=True),
        lax.all_gather(shards[6], "patches", axis=0, tiled=True),
        lax.all_gather(shards[7], "patches", axis=0, tiled=True),
    )
    return (
        lax.all_gather(row_parts[0], "frames", axis=1, tiled=True),
        lax.all_gather(row_parts[1], "frames", axis=1, tiled=True),
        lax.all_gather(row_parts[2], "frames", axis=1, tiled=True),
        lax.all_gather(row_parts[3], "frames", axis=1, tiled=True),
        lax.all_gather(row_parts[4], "frames", axis=1, tiled=True),
        lax.all_gather(row_parts[5], "frames", axis=1, tiled=True),
        lax.all_gather(row_parts[6], "frames", axis=1, tiled=True),
        lax.all_gather(row_parts[7], "frames", axis=1, tiled=True),
    )


def self_attend(queries, keys_vals, key_mask, heads):
    frames, patches, width = queries.shape
    head_dim = width // heads
    query_heads = queries.reshape(frames, patches, heads, head_dim)
    key_heads = keys_vals[..., :width].reshape(frames + 2, patches, heads, head_dim)
    value_heads = keys_vals[..., width:].reshape(frames + 2, patches, heads, head_dim)
    scores = jnp.einsum("sphd,tphd->phst", query_heads, key_heads, precision=HIGH) * head_dim ** (
        -0.5
    )
    scores = jnp.where(key_mask[None, None], scores, -1000000000.0)
    probs = jax.nn.softmax(scores, axis=-1)
    mixed = jnp.einsum("phst,tphd->sphd", probs, value_heads, precision=HIGH)
    return mixed.reshape(frames, patches, width)


def body(
    tokens,
    cotangent,
    caption,
    null_embed,
    timesteps,
    null_mask,
    bucket_sizes,
    patch_mask,
    frame_counts,
    table,
    time_proj,
    self_qkv,
    self_out,
    cross_q,
    cross_kv,
    cross_out,
    mlp_in,
    mlp_out,
    biases,
    hidden_bias,
):
    f32 = jnp.float32
    bf16 = jnp.bfloat16
    frames, patches, width = tokens.shape
    heads = HEADS
    head_dim = width // heads
    scale = head_dim ** (-0.5)
    clips = caption.shape[0]
    cap_len = caption.shape[1]
    row_count = frames * patches
    count = frame_counts[0]
    frame_index = lax.axis_index("frames")
    patch_index = lax.axis_index("patches")
    shards = (time_proj, self_qkv, self_out, cross_q, cross_kv, cross_out, mlp_in, mlp_out)
    weights = gather_forward(shards)
    full_time, full_qkv, full_out, full_q, full_kv, full_cross_out, full_in, full_mlp_out = weights
    bias_f = biases.astype(f32)
    bias_hidden = hidden_bias.astype(f32)
    patch_ids = patch_index * patches + jnp.arange(patches, dtype=jnp.int32)
    bucket_ends = jnp.cumsum(bucket_sizes)
    clip_ids = jnp.sum((patch_ids[:, None] >= bucket_ends[None, :]).astype(jnp.int32), axis=1)
    onehot = (clip_ids[:, None] == jnp.arange(clips, dtype=jnp.int32)[None, :]).astype(f32)
    slot_ids = jnp.arange(frames, dtype=jnp.int32)
    valid = (slot_ids < count)[:, None] & (patch_mask[None, :] == 1)
    features = time_features(timesteps, full_time.shape[0]).astype(bf16)
    modulation = table.astype(f32) + forward_dot(features, full_time).reshape(clips, 6, width)
    per_patch = jnp.einsum("pc,ckd->pkd", onehot, modulation, precision=HIGH)
    shift_a = per_patch[:, 0]
    scale_a = per_patch[:, 1]
    gate_a = per_patch[:, 2]
    shift_m = per_patch[:, 3]
    scale_m = per_patch[:, 4]
    gate_m = per_patch[:, 5]
    inputs_f = tokens.astype(f32)
    normed_a, modulate_a_vjp = jax.vjp(modulate, inputs_f, shift_a, scale_a)
    normed_r = normed_a.astype(bf16).reshape(row_count, width)
    qkv_bias = jnp.concatenate([bias_f[0], jnp.zeros((width,), f32), bias_f[1]])
    qkv_r = (
        (forward_dot(normed_r, full_qkv) + qkv_bias)
        .astype(bf16)
        .reshape(frames, patches, 3 * width)
    )
    queries_r = qkv_r[..., :width]
    keyval_r = qkv_r[..., width:]
    last_kv = lax.dynamic_index_in_dim(keyval_r, count - 1, 0, keepdims=False)
    edges = jnp.stack([keyval_r[0], last_kv])
    outer_kv = with_halo(edges, (("frames", 0),), 1)
    keys_all = jnp.concatenate([outer_kv[0:1], keyval_r, outer_kv[3:4]], axis=0)
    prev_ok = frame_index > 0
    next_ok = frame_index < lax.axis_size("frames") - 1
    query_slot = slot_ids[:, None]
    key_place = jnp.arange(frames + 2, dtype=jnp.int32)[None, :]
    key_slot = key_place - 1
    slot_keys = (
        (key_place >= 1)
        & (key_place <= frames)
        & (jnp.abs(key_slot - query_slot) <= 1)
        & (key_slot < count)
    )
    prev_keys = (key_place == 0) & (query_slot == 0) & prev_ok
    next_keys = (key_place == frames + 1) & (query_slot == count - 1) & next_ok
    key_mask = slot_keys | prev_keys | next_keys
    attn_in, attend_vjp = jax.vjp(
        partial(self_attend, key_mask=key_mask, heads=heads),
        queries_r.astype(f32),
        keys_all.astype(f32),
    )
    attn_r = attn_in.astype(bf16).reshape(row_count, width)
    attn_out = (forward_dot(attn_r, full_out) + bias_f[2]).reshape(frames, patches, width)
    resid_a = inputs_f + gate_a * attn_out
    captions_used = jnp.where(null_mask[:, None, None] == 1, null_embed[None], caption).reshape(
        clips * cap_len, width
    )
    kv_bias = jnp.concatenate([jnp.zeros((width,), f32), bias_f[4]])
    cross_kv_r = (forward_dot(captions_used, full_kv) + kv_bias).astype(bf16)
    cross_keys = cross_kv_r[:, :width].reshape(clips * cap_len, heads, head_dim)
    cross_vals = cross_kv_r[:, width:].reshape(clips * cap_len, heads, head_dim)
    resid_a_r = resid_a.astype(bf16).reshape(row_count, width)
    cross_queries = (
        (forward_dot(resid_a_r, full_q) + bias_f[3])
        .astype(bf16)
        .reshape(row_count, heads, head_dim)
    )
    token_clip = jnp.broadcast_to(clip_ids[None, :], (frames, patches)).reshape(row_count)
    key_clip = jnp.repeat(jnp.arange(clips, dtype=jnp.int32), cap_len)
    same_clip = token_clip[:, None] == key_clip[None, :]
    scores = (
        jnp.einsum("rhd,khd->rhk", cross_queries, cross_keys, preferred_element_type=f32) * scale
    )
    scores = jnp.where(same_clip[:, None, :], scores, -1000000000.0)
    probs = jax.nn.softmax(scores, axis=-1)
    probs_r = probs.astype(bf16)
    cross_mix = (
        jnp.einsum("rhk,khd->rhd", probs_r, cross_vals, preferred_element_type=f32)
        .astype(bf16)
        .reshape(row_count, width)
    )
    cross_res = forward_dot(cross_mix, full_cross_out) + bias_f[5]
    resid_c = resid_a + cross_res.reshape(frames, patches, width)
    normed_m, modulate_m_vjp = jax.vjp(modulate, resid_c, shift_m, scale_m)
    normed_m_r = normed_m.astype(bf16).reshape(row_count, width)
    pre_act = forward_dot(normed_m_r, full_in) + bias_hidden
    activ, gelu_vjp = jax.vjp(gelu_tanh, pre_act)
    activ_r = activ.astype(bf16)
    mlp_res = (forward_dot(activ_r, full_mlp_out) + bias_f[6]).reshape(frames, patches, width)
    final = resid_c + gate_m * mlp_res
    block_out = jnp.where(valid[:, :, None], final, 0.0).astype(bf16)
    weights = gather_backward(shards)
    full_time, full_qkv, full_out, full_q, full_kv, full_cross_out, full_in, full_mlp_out = weights
    grad_final = jnp.where(valid[:, :, None], cotangent.astype(f32), 0.0)
    grad_gate_m = jnp.sum(grad_final * mlp_res, axis=0)
    grad_mlp_r = (gate_m * grad_final).astype(bf16).reshape(row_count, width)
    bias_mo_grad = jnp.sum(grad_mlp_r.astype(f32), axis=0)
    mlp_out_grad = outer_sum(activ_r, grad_mlp_r)
    grad_act = times_transposed(grad_mlp_r, full_mlp_out)
    grad_pre_r = gelu_vjp(grad_act)[0].astype(bf16)
    bias_hidden_grad = jnp.sum(grad_pre_r.astype(f32), axis=0)
    mlp_in_grad = outer_sum(normed_m_r, grad_pre_r)
    grad_norm_m = times_transposed(grad_pre_r, full_in).reshape(frames, patches, width)
    resid_c_part, grad_shift_m, grad_scale_m = modulate_m_vjp(grad_norm_m)
    grad_resid_c = grad_final + resid_c_part
    grad_cross_r = grad_resid_c.astype(bf16).reshape(row_count, width)
    bias_co_grad = jnp.sum(grad_cross_r.astype(f32), axis=0)
    cross_out_grad = outer_sum(cross_mix, grad_cross_r)
    grad_mix_r = (
        times_transposed(grad_cross_r, full_cross_out)
        .astype(bf16)
        .reshape(row_count, heads, head_dim)
    )
    grad_probs = jnp.einsum("rhd,khd->rhk", grad_mix_r, cross_vals, preferred_element_type=f32)
    grad_vals = jnp.einsum("rhk,rhd->khd", probs_r, grad_mix_r, preferred_element_type=f32)
    grad_scores_r = (
        probs * (grad_probs - jnp.sum(grad_probs * probs, axis=-1, keepdims=True))
    ).astype(bf16)
    grad_cq = (
        jnp.einsum("rhk,khd->rhd", grad_scores_r, cross_keys, preferred_element_type=f32) * scale
    )
    grad_cq_r = grad_cq.astype(bf16).reshape(row_count, width)
    grad_keys = (
        jnp.einsum("rhk,rhd->khd", grad_scores_r, cross_queries, preferred_element_type=f32) * scale
    )
    bias_cq_grad = jnp.sum(grad_cq_r.astype(f32), axis=0)
    cross_q_grad = outer_sum(resid_a_r, grad_cq_r)
    grad_resid_a = grad_resid_c + times_transposed(grad_cq_r, full_q).reshape(
        frames, patches, width
    )
    cross_kv_part = jnp.concatenate(
        [grad_keys.reshape(clips * cap_len, width), grad_vals.reshape(clips * cap_len, width)],
        axis=1,
    )
    grad_gate_a = jnp.sum(grad_resid_a * attn_out, axis=0)
    grad_attn_r = (gate_a * grad_resid_a).astype(bf16).reshape(row_count, width)
    bias_o_grad = jnp.sum(grad_attn_r.astype(f32), axis=0)
    self_out_grad = outer_sum(attn_r, grad_attn_r)
    grad_attn_in = round_trip(times_transposed(grad_attn_r, full_out)).reshape(
        frames, patches, width
    )
    grad_queries, grad_keys_all = attend_vjp(grad_attn_in)
    returns = jnp.stack([grad_keys_all[0], grad_keys_all[frames + 1]])
    back_kv = with_halo(returns.astype(jnp.bfloat16), (("frames", 0),), 1).astype(returns.dtype)
    first_slot = (slot_ids == 0)[:, None, None]
    last_slot = (slot_ids == count - 1)[:, None, None]
    grad_kv = (
        grad_keys_all[1 : frames + 1]
        + jnp.where(first_slot, back_kv[0][None], 0.0)
        + jnp.where(last_slot, back_kv[3][None], 0.0)
    )
    grad_qkv_r = (
        jnp.concatenate([grad_queries, grad_kv], axis=-1).astype(bf16).reshape(row_count, 3 * width)
    )
    bias_q_grad = jnp.sum(grad_qkv_r[:, :width].astype(f32), axis=0)
    bias_v_grad = jnp.sum(grad_qkv_r[:, 2 * width :].astype(f32), axis=0)
    self_qkv_grad = outer_sum(normed_r, grad_qkv_r)
    grad_norm_a = times_transposed(grad_qkv_r, full_qkv).reshape(frames, patches, width)
    input_part, grad_shift_a, grad_scale_a = modulate_a_vjp(grad_norm_a)
    input_grad = grad_resid_a + input_part
    per_patch_grad = jnp.stack(
        [grad_shift_a, grad_scale_a, grad_gate_a, grad_shift_m, grad_scale_m, grad_gate_m], axis=1
    )
    mod_part = jnp.einsum("pc,pkd->ckd", onehot, per_patch_grad, precision=HIGH)
    bias_part = jnp.stack(
        [
            bias_q_grad,
            bias_v_grad,
            bias_o_grad,
            bias_cq_grad,
            jnp.zeros((width,), f32),
            bias_co_grad,
            bias_mo_grad,
        ]
    )
    kv_total, bias_total, hidden_total, mod_total = lax.psum(
        (cross_kv_part, bias_part, bias_hidden_grad, mod_part), ("frames", "patches")
    )
    kv_total_r = kv_total.astype(bf16)
    bias_cv_grad = jnp.sum(kv_total_r[:, width:].astype(f32), axis=0)
    bias_rows_ids = jnp.arange(bias_total.shape[0], dtype=jnp.int32)
    biases_grad = bias_total + jnp.where((bias_rows_ids == 4)[:, None], bias_cv_grad[None, :], 0.0)
    cross_kv_full = outer_sum(captions_used, kv_total_r)
    caption_rows = times_transposed(kv_total_r, full_kv).reshape(clips, cap_len, width)
    dropped = (null_mask == 1)[:, None, None]
    caption_grad = jnp.where(dropped, 0.0, caption_rows)
    null_grad = jnp.sum(jnp.where(dropped, caption_rows, 0.0), axis=0)
    table_grad = jnp.sum(mod_total, axis=0)
    time_full = jnp.dot(features.astype(f32).T, mod_total.reshape(clips, 6 * width), precision=HIGH)
    time_proj_grad = lax.dynamic_slice(
        time_full,
        (patch_index * time_proj.shape[0], frame_index * time_proj.shape[1]),
        time_proj.shape,
    )
    cross_kv_grad = lax.dynamic_slice(
        cross_kv_full,
        (patch_index * cross_kv.shape[0], frame_index * cross_kv.shape[1]),
        cross_kv.shape,
    )
    grads = (self_qkv_grad, self_out_grad, cross_q_grad, cross_out_grad, mlp_in_grad, mlp_out_grad)
    row_sums = (
        lax.psum_scatter(
            grads[0].astype(jnp.bfloat16), "patches", scatter_dimension=0, tiled=True
        ).astype(jnp.float32),
        lax.psum_scatter(
            grads[1].astype(jnp.bfloat16), "patches", scatter_dimension=0, tiled=True
        ).astype(jnp.float32),
        lax.psum_scatter(
            grads[2].astype(jnp.bfloat16), "patches", scatter_dimension=0, tiled=True
        ).astype(jnp.float32),
        lax.psum_scatter(
            grads[3].astype(jnp.bfloat16), "patches", scatter_dimension=0, tiled=True
        ).astype(jnp.float32),
        lax.psum_scatter(
            grads[4].astype(jnp.bfloat16), "patches", scatter_dimension=0, tiled=True
        ).astype(jnp.float32),
        lax.psum_scatter(
            grads[5].astype(jnp.bfloat16), "patches", scatter_dimension=0, tiled=True
        ).astype(jnp.float32),
    )
    col_sums = (
        lax.psum_scatter(
            row_sums[0].astype(jnp.bfloat16), "frames", scatter_dimension=1, tiled=True
        ).astype(jnp.float32),
        lax.psum_scatter(
            row_sums[1].astype(jnp.bfloat16), "frames", scatter_dimension=1, tiled=True
        ).astype(jnp.float32),
        lax.psum_scatter(
            row_sums[2].astype(jnp.bfloat16), "frames", scatter_dimension=1, tiled=True
        ).astype(jnp.float32),
        lax.psum_scatter(
            row_sums[3].astype(jnp.bfloat16), "frames", scatter_dimension=1, tiled=True
        ).astype(jnp.float32),
        lax.psum_scatter(
            row_sums[4].astype(jnp.bfloat16), "frames", scatter_dimension=1, tiled=True
        ).astype(jnp.float32),
        lax.psum_scatter(
            row_sums[5].astype(jnp.bfloat16), "frames", scatter_dimension=1, tiled=True
        ).astype(jnp.float32),
    )
    qkv_shard, out_shard, q_shard, cross_out_shard, in_shard, mlp_out_shard = col_sums
    return (
        block_out,
        input_grad,
        caption_grad,
        null_grad,
        table_grad,
        time_proj_grad,
        qkv_shard,
        out_shard,
        q_shard,
        cross_kv_grad,
        cross_out_shard,
        in_shard,
        mlp_out_shard,
        biases_grad,
        hidden_total,
    )


def solution(mesh):
    return jax.shard_map(
        body,
        mesh=mesh,
        in_specs=(
            P("frames", "patches", None),
            P("frames", "patches", None),
            P(),
            P(),
            P(),
            P(),
            P(),
            P("patches"),
            P("frames"),
            P(),
            P("patches", "frames"),
            P("patches", "frames"),
            P("patches", "frames"),
            P("patches", "frames"),
            P("patches", "frames"),
            P("patches", "frames"),
            P("patches", "frames"),
            P("patches", "frames"),
            P(),
            P(),
        ),
        out_specs=(
            P("frames", "patches", None),
            P("frames", "patches", None),
            P(),
            P(),
            P(),
            P("patches", "frames"),
            P("patches", "frames"),
            P("patches", "frames"),
            P("patches", "frames"),
            P("patches", "frames"),
            P("patches", "frames"),
            P("patches", "frames"),
            P("patches", "frames"),
            P(),
            P(),
        ),
        check_vma=False,
    )
```

profile of v0, /device:TPU:0, one launch (start us, length us, event | category | flops | bytes accessed | tf_op | source)
XLA Modules:
  0.0 1997.0 jit_solution(14520827129864487830)
XLA Ops:
  11.9 41.3 %all-gather.17.cloned.1.call-done = bf16[256,3456]{1,0:T(8,128)(2,1)} async-done(((bf16[16,3456]{1,0:T(8,128)(2,1)}), bf16[256,3456]{1,0:T(8,128)(2,1)}) %all-gather.17.cloned.1.call-update) | async-done | bytes 1769488 | tf_op jit(solution)/shard_map/all_gather | solution.py:68
  54.1 43.4 %all-gather.29.cloned.1.call-done = bf16[1152,1152]{1,0:T(8,128)(2,1)} async-done(((bf16[72,1152]{1,0:T(8,128)(2,1)}), bf16[1152,1152]{1,0:T(8,128)(2,1)}) %all-gather.29.cloned.1.call-update) | async-done | bytes 2654224 | tf_op jit(solution)/shard_map/all_gather | solution.py:72
  97.5 51.2 %all-gather.21.cloned.1.call-done = bf16[1152,1728]{1,0:T(8,128)(2,1)} async-done(((bf16[72,1728]{1,0:T(8,128)(2,1)}), bf16[1152,1728]{1,0:T(8,128)(2,1)}) %all-gather.21.cloned.1.call-update) | async-done | bytes 3981328 | tf_op jit(solution)/shard_map/all_gather | solution.py:69
  155.1 33.4 %all-gather.25.cloned.1.call-done = bf16[1152,576]{1,0:T(8,128)(2,1)} async-done(((bf16[72,576]{1,0:T(8,128)(2,1)}), bf16[1152,576]{1,0:T(8,128)(2,1)}) %all-gather.25.cloned.1.call-update) | async-done | bytes 1327120 | tf_op jit(solution)/shard_map/all_gather | solution.py:70
  191.2 37.5 %all-gather.33.cloned.1.call-done = bf16[1152,576]{1,0:T(8,128)(2,1)} async-done(((bf16[72,576]{1,0:T(8,128)(2,1)}), bf16[1152,576]{1,0:T(8,128)(2,1)}) %all-gather.33.cloned.1.call-update) | async-done | bytes 1327120 | tf_op jit(solution)/shard_map/all_gather | solution.py:71
  231.4 37.5 %all-gather.37.cloned.1.call-done = bf16[1152,576]{1,0:T(8,128)(2,1)} async-done(((bf16[72,576]{1,0:T(8,128)(2,1)}), bf16[1152,576]{1,0:T(8,128)(2,1)}) %all-gather.37.cloned.1.call-update) | async-done | bytes 1327120 | tf_op jit(solution)/shard_map/all_gather | solution.py:73
  271.7 54.6 %all-gather.41.cloned.1.call-done = bf16[1152,2304]{1,0:T(8,128)(2,1)} async-done(((bf16[72,2304]{1,0:T(8,128)(2,1)}), bf16[1152,2304]{1,0:T(8,128)(2,1)}) %all-gather.41.cloned.1.call-update) | async-done | bytes 5308432 | tf_op jit(solution)/shard_map/all_gather | solution.py:74
  333.4 42.4 %all-gather.19.cloned.1.call-done = bf16[256,6912]{1,0:T(8,128)(2,1)} async-done(((bf16[256,3456]{1,0:T(8,128)(2,1)}), bf16[256,6912]{1,0:T(8,128)(2,1)}) %all-gather.19.cloned.1.call-update) | async-done | bytes 3538960 | tf_op jit(solution)/shard_map/all_gather | solution.py:78
  385.6 52.3 %all-gather.45.cloned.1.call-done = bf16[4608,576]{1,0:T(8,128)(2,1)} async-done(((bf16[288,576]{1,0:T(8,128)(2,1)}), bf16[4608,576]{1,0:T(8,128)(2,1)}) %all-gather.45.cloned.1.call-update) | async-done | bytes 5308432 | tf_op jit(solution)/shard_map/all_gather | solution.py:75
  446.2 61.1 %all-gather.31.cloned.1.call-done = bf16[1152,2304]{1,0:T(8,128)(2,1)} async-done(((bf16[1152,1152]{1,0:T(8,128)(2,1)}), bf16[1152,2304]{1,0:T(8,128)(2,1)}) %all-gather.31.cloned.1.call-update) | async-done | bytes 5308432 | tf_op jit(solution)/shard_map/all_gather | solution.py:82
  514.1 94.5 %all-gather.23.cloned.1.call-done = bf16[1152,3456]{0,1:T(8,128)(2,1)} async-done(((bf16[1152,1728]{0,1:T(8,128)(2,1)}), bf16[1152,3456]{0,1:T(8,128)(2,1)}) %all-gather.23.cloned.1.call-update) | async-done | bytes 7962640 | tf_op jit(solution)/shard_map/all_gather | solution.py:79
  608.6 11.2 add_convert_fusion
  654.8 10.8 copy.157
  677.6 11.0 copy.159
  688.6 11.0 copy.158
  699.6 10.4 fusion.16
  720.4 17.9 convert_bitcast_fusion.1
  781.4 16.1 fusion.95
  797.5 12.9 fusion.56
  821.5 51.6 %all-gather.43.cloned.1.call-done = bf16[1152,4608]{1,0:T(8,128)(2,1)} async-done(((bf16[1152,2304]{1,0:T(8,128)(2,1)}), bf16[1152,4608]{1,0:T(8,128)(2,1)}) %all-gather.43.cloned.1.call-update) | async-done | bytes 10616848 | tf_op jit(solution)/shard_map/all_gather | solution.py:84
  873.1 17.2 fusion.96
  890.4 115.1 %all-gather.47.cloned.1.call-done = bf16[4608,1152]{0,1:T(8,128)(2,1)} async-done(((bf16[4608,576]{0,1:T(8,128)(2,1)}), bf16[4608,1152]{0,1:T(8,128)(2,1)}) %all-gather.47.cloned.1.call-update) | async-done | bytes 10616848 | tf_op jit(solution)/shard_map/all_gather | solution.py:85
  1005.5 24.1 %convert_reduce_fusion = (f32[4608]{0:T(1024)}, bf16[864,4608]{1,0:T(8,128)(2,1)S(1)}) fusion(f32[864,4608]{1,0:T(8,128)} %fusion.96, f32[4608]{0:T(1024)S(1)} %copy-done.67, bf16[864,1152]{1,0:T(8,128)(2,1)S(1)} %bitcast.232, bf16[4608,1152]{0,1:T(8,128)(2,1)} %all-gather.47.cloned.1.call-done), kind=kOutput, calls=%fused_computation.21 | convolution fusion | flops 9264508928 | bytes 36532224 | tf_op jit(solution)/shard_map/re,de->rd/dot_general | solution.py:59
  1029.6 10.4 fusion.97
  1042.5 20.4 %convolution_add_fusion.1 = f32[864,1152]{1,0:T(8,128)} fusion(bf16[4608,1152]{0,1:T(8,128)(2,1)} %all-gather.47.cloned.1.call-done, f32[1152]{0:T(1024)S(1)} %copy-done.79, f32[864,4608]{1,0:T(8,128)} %fusion.96, f32[4608]{0:T(1024)S(1)} %copy-done.67), kind=kOutput, calls=%fused_computation.78 | convolution fusion | flops 9213751296 | bytes 30546432 | tf_op jit(solution)/shard_map/dot_general | solution.py:51
  1090.0 20.6 %fusion.1 = (f32[864,16]{0,1:T(8,128)S(1)}, f32[16,480,864]{2,1,0:T(8,128)}) fusion(f32[864,16,480]{0,2,1:T(8,128)} %get-tuple-element.70, f32[864,16]{0,1:T(8,128)S(1)} %copy-done.60, bf16[480,16,72]{0,2,1:T(8,128)(2,1)S(1)} %bitcast.245, bf16[864,16,72]{0,2,1:T(8,128)(2,1)} %bitcast.230), kind=kOutput, calls=%fused_computation.3 | convolution fusion | flops 975407616 | bytes 56291328 | tf_op jit(solution)/shard_map/rhd,khd->rhk/dot_general | solution.py:277
  1110.6 23.9 %fusion.3 = bf16[864,16,480]{0,2,1:T(8,128)(2,1)} fusion(f32[16,480,864]{2,1,0:T(8,128)} %get-tuple-element.72, f32[864,16]{0,1:T(8,128)S(1)} %get-tuple-element.71, f32[864,16,480]{0,2,1:T(8,128)} %get-tuple-element.70, f32[864,16]{0,1:T(8,128)S(1)} %copy-done.60), kind=kLoop, calls=%fused_computation.5 | loop fusion | flops 26542080 | bytes 66465792 | tf_op jit(solution)/shard_map/convert_element_type | solution.py:281
  1180.1 14.7 multiply_reduce_fusion
  1199.7 25.4 %convolution_bitcast_fusion.2 = f32[11,96,16,72]{3,0,2,1:T(8,128)} fusion(bf16[9,96,16,72]{3,0,2,1:T(8,128)(2,1)S(1)} %bitcast.203, f32[96,16,9,11]{3,2,1,0:T(8,128)S(1)} %get-tuple-element.75, f32[96,16,9]{2,1,0:T(8,128)S(1)} %neg.13, f32[96,16,9]{2,1,0:T(8,128)S(1)} %copy-done.31, pred[9,11]{1,0:T(8,128)(4,1)S(1)} %copy-done.72, ...), kind=kOutput, calls=%fused_computation.80 | convolution fusion | flops 132599808 | bytes 8239203 | tf_op jit(solution)/shard_map/transpose(jvp(sphd,tphd->phst))/dot_general | solution.py:118
  1225.1 11.5 copy.180
  1243.0 22.9 %fusion.43 = f32[11,96,16,72]{3,0,2,1:T(8,128)} fusion(f32[96,16,9]{2,1,0:T(8,128)} %copy-done.29, bf16[96,16,72,9]{2,1,0,3:T(8,128)(2,1)} %bitcast.226, f32[96,16,9,11]{3,2,1,0:T(8,128)} %get-tuple-element.68, f32[96,16,9]{2,1,0:T(8,128)S(1)} %copy-done.28, pred[9,11]{1,0:T(8,128)(4,1)S(1)} %copy-done.72), kind=kOutput, calls=%fused_computation.79 | convolution fusion | flops 131991552 | bytes 7575651 | tf_op jit(solution)/shard_map/transpose(jvp(phst,tphd->sphd))/dot_general | solution.py:123
  1265.9 11.3 copy.176
  1307.1 19.7 convert_reduce_fusion.1
  1344.3 10.9 fusion.12
  1356.7 20.3 %convolution_convert_fusion = bf16[4608,1152]{1,0:T(8,128)(2,1)} fusion(bf16[864,1152]{1,0:T(8,128)(2,1)S(1)} %bitcast.233, f32[864,4608]{1,0:T(8,128)} %fusion.96, f32[4608]{0:T(1024)S(1)} %copy-done.68), kind=kOutput, calls=%fused_computation.11 | convolution fusion | flops 9218064384 | bytes 28551168 | tf_op jit(solution)/shard_map/rd,re->de/dot_general | solution.py:55
  1378.6 16.7 convolution_convert_fusion.1
  1397.2 13.5 fusion.50
  1421.2 14.8 fusion.31
  1456.7 21.8 %reduce-scatter.47.cloned.1.call-done = bf16[72,3456]{1,0:T(8,128)(2,1)} async-done(((bf16[1152,3456]{1,0:T(8,128)(2,1)}), bf16[72,3456]{1,0:T(8,128)(2,1)}) %reduce-scatter.47.cloned.1.call-update) | async-done | bytes 497680
  1480.8 143.1 %all-reduce.12 = (bf16[480,2304]{0,1:T(8,128)(2,1)S(1)}, f32[7,1152]{1,0:T(8,128)S(1)}, f32[4608]{0:T(1024)}) all-reduce(f32[480,2304]{0,1:T(8,128)} %pad_maximum_fusion.2, f32[7,1152]{1,0:T(8,128)S(1)} %stack.58, f32[4608]{0:T(1024)} %get-tuple-element.31), channel_id=1, replica_groups=mesh['frames'=2,'patches'=16] {'frames','patches'}, use_global_device_ids=true, to_apply=%region_16.17 | all-reduce | flops 1118592 | bytes 6736896 | tf_op jit(solution)/shard_map/psum | solution.py:339
  1646.5 110.4 %reduce-scatter.31.cloned.1.call-done = bf16[72,4608]{1,0:T(8,128)(2,1)} async-done(((bf16[1152,4608]{1,0:T(8,128)(2,1)}), bf16[72,4608]{1,0:T(8,128)(2,1)}) %reduce-scatter.31.cloned.1.call-update) | async-done | bytes 663568 | tf_op jit(solution)/shard_map/reduce_scatter | solution.py:377
  1761.6 121.7 %all-reduce.11.cloned.1.call-done = f32[4,6,1152]{2,0,1:T(4,128)} async-done(((f32[4,6,1152]{2,0,1:T(4,128)}), f32[4,6,1152]{2,0,1:T(4,128)}) %all-reduce.11.cloned.1.call-update) | async-done | bytes 110608 | tf_op jit(solution)/shard_map/psum | solution.py:339
  1888.7 10.3 reduce-scatter.43.cloned.1.call-done
  1900.7 13.1 reduce-scatter.41.cloned.1.call-done
  1915.6 13.0 reduce-scatter.39.cloned.1.call-done
  1930.3 18.9 reduce-scatter.37.cloned.1.call-done
  1951.3 18.8 reduce-scatter.45.cloned.1.call-done
  1972.2 16.3 reduce-scatter.33.cloned.1.call-done
  (423 shorter events, 377.4 us)
Async XLA Ops:
  7.2 46.1 %all-gather.17.cloned.1.call-start = ((), (), s32[]{:S(2)}) async-start(), calls=%async_computation.12 | async-start | bytes 1880064 | tf_op jit(solution)/shard_map/all_gather | solution.py:68
  7.9 89.5 %all-gather.29.cloned.1.call-start = ((), (), s32[]{:S(2)}) async-start(), calls=%async_computation.18 | async-start | bytes 2820096 | tf_op jit(solution)/shard_map/all_gather | solution.py:72
  8.7 140.0 %all-gather.21.cloned.1.call-start = ((), (), s32[]{:S(2)}) async-start(), calls=%async_computation.14 | async-start | bytes 4386816 | tf_op jit(solution)/shard_map/all_gather | solution.py:69
  9.4 179.1 %all-gather.25.cloned.1.call-start = ((), (), s32[]{:S(2)}) async-start(), calls=%async_computation.16 | async-start | bytes 1566720 | tf_op jit(solution)/shard_map/all_gather | solution.py:70
  10.0 218.8 %all-gather.33.cloned.1.call-start = ((), (), s32[]{:S(2)}) async-start(), calls=%async_computation.20 | async-start | bytes 1566720 | tf_op jit(solution)/shard_map/all_gather | solution.py:71
  10.6 258.4 %all-gather.37.cloned.1.call-start = ((), (), s32[]{:S(2)}) async-start(), calls=%async_computation.22 | async-start | bytes 1566720 | tf_op jit(solution)/shard_map/all_gather | solution.py:73
  11.1 315.2 %all-gather.41.cloned.1.call-start = ((), (), s32[]{:S(2)}) async-start(), calls=%async_computation.24 | async-start | bytes 5640192 | tf_op jit(solution)/shard_map/all_gather | solution.py:74
  11.9 364.0 %all-gather.19.cloned.1.call-start = ((), (), s32[]{:S(2)}) async-start(), calls=%async_computation.13 | async-start | bytes 5308416 | tf_op jit(solution)/shard_map/all_gather | solution.py:78
  53.3 384.6 %all-gather.45.cloned.1.call-start = ((), (), s32[]{:S(2)}) async-start(), calls=%async_computation.26 | async-start | bytes 6266880 | tf_op jit(solution)/shard_map/all_gather | solution.py:75
  54.0 453.3 %all-gather.31.cloned.1.call-start = ((), (), s32[]{:S(2)}) async-start(), calls=%async_computation.19 | async-start | bytes 7962624 | tf_op jit(solution)/shard_map/all_gather | solution.py:82
  97.5 511.2 %all-gather.23.cloned.1.call-start = ((), (), s32[]{:S(2)}) async-start(), calls=%async_computation.15 | async-start | bytes 11943936 | tf_op jit(solution)/shard_map/all_gather | solution.py:79
  155.1 605.8 %all-gather.27.cloned.1.call-start = ((), (), s32[]{:S(2)}) async-start(), calls=%async_computation.17 | async-start | bytes 3981312 | tf_op jit(solution)/shard_map/all_gather | solution.py:80
  191.2 579.5 %all-gather.35.cloned.1.call-start = ((), (), s32[]{:S(2)}) async-start(), calls=%async_computation.21 | async-start | bytes 3981312 | tf_op jit(solution)/shard_map/all_gather | solution.py:81
  231.4 579.0 %all-gather.39.cloned.1.call-start = ((), (), s32[]{:S(2)}) async-start(), calls=%async_computation.23 | async-start | bytes 3981312 | tf_op jit(solution)/shard_map/all_gather | solution.py:83
  271.6 56.1 %copy-start.73 = (bf16[4608]{0:T(1024)(128)(2,1)S(1)}, bf16[4608]{0:T(1024)(128)(2,1)}, u32[]{:S(2)}) copy-start(bf16[4608]{0:T(1024)(128)(2,1)} %param.39) | copy-start | bytes 27652
  271.6 56.7 %copy-start.69 = (bf16[6,1152]{1,0:T(8,128)(2,1)S(1)}, bf16[6,1152]{1,0:T(8,128)(2,1)}, u32[]{:S(2)}) copy-start(bf16[6,1152]{1,0:T(8,128)(2,1)} %param.29) | copy-start | bytes 41476
  271.6 56.7 %copy-start.70 = (bf16[7,1152]{1,0:T(8,128)(2,1)S(1)}, bf16[7,1152]{1,0:T(8,128)(2,1)}, u32[]{:S(2)}) copy-start(bf16[7,1152]{1,0:T(8,128)(2,1)} %param.38) | copy-start | bytes 48388
  271.6 57.5 %copy-start.2 = (bf16[9,96,1152]{2,1,0:T(8,128)(2,1)S(1)}, bf16[9,96,1152]{2,1,0:T(8,128)(2,1)}, u32[]{:S(2)}) copy-start(bf16[9,96,1152]{2,1,0:T(8,128)(2,1)} %param.20) | copy-start | bytes 5971972
  271.6 57.8 %copy-start.93 = (s32[4]{0:T(128)S(1)}, s32[4]{0:T(128)}, u32[]{:S(2)}) copy-start(s32[4]{0:T(128)} %param.25) | copy-start | bytes 52
  271.7 57.8 %copy-start.94 = (s32[96]{0:T(128)S(1)}, s32[96]{0:T(128)}, u32[]{:S(2)}) copy-start(s32[96]{0:T(128)} %param.27) | copy-start | bytes 1156
  271.7 601.4 %all-gather.43.cloned.1.call-start = ((), (), s32[]{:S(2)}) async-start(), calls=%async_computation.25 | async-start | bytes 15925248 | tf_op jit(solution)/shard_map/all_gather | solution.py:84
  326.4 679.1 %all-gather.47.cloned.1.call-start = ((), (), s32[]{:S(2)}) async-start(), calls=%async_computation.27 | async-start | bytes 15925248 | tf_op jit(solution)/shard_map/all_gather | solution.py:85
  329.8 389.7 %copy-start.71 = (pred[9,11]{1,0:T(8,128)(4,1)}, pred[9,11]{1,0:T(8,128)(4,1)S(1)}, u32[]{:S(2)}) copy-start(pred[9,11]{1,0:T(8,128)(4,1)S(1)} %fusion.67) | copy-start | bytes 301
  446.1 61.2 %copy-start.46 = (bf16[4,120,1152]{2,1,0:T(8,128)(2,1)S(1)}, bf16[4,120,1152]{2,1,0:T(8,128)(2,1)}, u32[]{:S(2)}) copy-start(bf16[4,120,1152]{2,1,0:T(8,128)(2,1)} %broadcast_select_fusion.1) | copy-start | bytes 3317764
  446.1 973.1 %reduce-scatter.53.cloned.1.call-start = ((), (), s32[]{:S(2)}) async-start(), calls=%async_computation.40 | async-start | bytes 2820096
  623.8 41.8 %collective-permute-start.1 = (bf16[1,96,2304]{2,1,0:T(8,128)(2,1)}, bf16[1,96,2304]{2,1,0:T(8,128)(2,1)}, u32[]{:S(2)}, u32[]{:S(2)}) collective-permute-start(bf16[1,96,2304]{2,1,0:T(8,128)(2,1)} %slice.121), channel_id=1, source_target_pairs={{16,0},{17,1},{18,2},{19,3},{20,4},{21,5},{22,6},{23,7},{24,8},{25... | collective-permute-start | bytes 1327112 | tf_op jit(solution)/shard_map/ppermute | solution.py:23
  634.0 33.7 %collective-permute-start = (bf16[1,96,2304]{2,1,0:T(8,128)(2,1)}, bf16[1,96,2304]{2,1,0:T(8,128)(2,1)}, u32[]{:S(2)}, u32[]{:S(2)}) collective-permute-start(bf16[1,96,2304]{2,1,0:T(8,128)(2,1)} %copy.153), channel_id=1, source_target_pairs={{0,16},{1,17},{2,18},{3,19},{4,20},{5,21},{6,22},{7,23},{8,24},{9,... | collective-permute-start | bytes 1327112 | tf_op jit(solution)/shard_map/ppermute | solution.py:22
  644.7 136.7 %copy-start.18 = (bf16[480,1152]{0,1:T(8,128)(2,1)}, bf16[480,1152]{0,1:T(8,128)(2,1)S(1)}, u32[]{:S(2)}) copy-start(bf16[480,1152]{0,1:T(8,128)(2,1)S(1)} %copy.163) | copy-start | bytes 3317764
  873.1 132.4 %copy-start.34 = (bf16[9,96,1152]{2,1,0:T(8,128)(2,1)S(1)}, bf16[9,96,1152]{2,1,0:T(8,128)(2,1)}, u32[]{:S(2)}) copy-start(bf16[9,96,1152]{2,1,0:T(8,128)(2,1)} %get-tuple-element.34) | copy-start | bytes 5971972
  873.1 132.4 %copy-start.67 = (f32[4608]{0:T(1024)S(1)}, f32[4608]{0:T(1024)}, u32[]{:S(2)}) copy-start(f32[4608]{0:T(1024)} %convert_element_type.204) | copy-start | bytes 55300
  1078.8 357.1 %reduce-scatter.51.cloned.1.call-start = ((), (), s32[]{:S(2)}) async-start(), calls=%async_computation.39 | async-start | bytes 2820096
  1242.9 205.1 %reduce-scatter.49.cloned.1.call-start = ((), (), s32[]{:S(2)}) async-start(), calls=%async_computation.38 | async-start | bytes 2820096
  1295.3 41.3 %collective-permute-start.2 = (bf16[1,96,2304]{2,1,0:T(8,128)(2,1)S(1)}, bf16[1,96,2304]{2,1,0:T(8,128)(2,1)}, u32[]{:S(2)}, u32[]{:S(2)}) collective-permute-start(bf16[1,96,2304]{2,1,0:T(8,128)(2,1)S(1)} %get-tuple-element.45), channel_id=1, source_target_pairs={{0,16},{1,17},{2,18},{3,19},{4,20},{5,21},{6,22},{7,23},{8,24},{9,... | collective-permute-start | bytes 1327112 | tf_op jit(solution)/shard_map/ppermute | solution.py:22
  1298.6 38.1 %collective-permute-start.3 = (bf16[1,96,2304]{2,1,0:T(8,128)(2,1)}, bf16[1,96,2304]{2,1,0:T(8,128)(2,1)}, u32[]{:S(2)}, u32[]{:S(2)}) collective-permute-start(bf16[1,96,2304]{2,1,0:T(8,128)(2,1)} %get-tuple-element.46), channel_id=1, source_target_pairs={{16,0},{17,1},{18,2},{19,3},{20,4},{21,5},{22,6},{23,7},{24,8},{25... | collective-permute-start | bytes 1327112 | tf_op jit(solution)/shard_map/ppermute | solution.py:23
  1307.1 171.3 %reduce-scatter.47.cloned.1.call-start = ((), (), s32[]{:S(2)}) async-start(), calls=%async_computation.37 | async-start | bytes 8460288
  1355.2 278.1 %reduce-scatter.35.cloned.1.call-start = ((), (), s32[]{:S(2)}) async-start(), calls=%async_computation.31 | async-start | bytes 11280384 | tf_op jit(solution)/shard_map/reduce_scatter | solution.py:380
  1377.0 379.9 %reduce-scatter.31.cloned.1.call-start = ((), (), s32[]{:S(2)}) async-start(), calls=%async_computation.29 | async-start | bytes 11280384 | tf_op jit(solution)/shard_map/reduce_scatter | solution.py:377
  1395.3 488.0 %all-reduce.11.cloned.1.call-start = ((), (), s32[]{:S(2)}) async-start(), calls=%async_computation.28 | async-start | bytes 221184 | tf_op jit(solution)/shard_map/psum | solution.py:339
  1419.2 479.8 %reduce-scatter.43.cloned.1.call-start = ((), (), s32[]{:S(2)}) async-start(), calls=%async_computation.35 | async-start | bytes 442368
  1421.1 492.7 %reduce-scatter.41.cloned.1.call-start = ((), (), s32[]{:S(2)}) async-start(), calls=%async_computation.34 | async-start | bytes 442368
  1437.8 490.8 %reduce-scatter.39.cloned.1.call-start = ((), (), s32[]{:S(2)}) async-start(), calls=%async_computation.33 | async-start | bytes 442368
  1449.9 499.4 %reduce-scatter.37.cloned.1.call-start = ((), (), s32[]{:S(2)}) async-start(), calls=%async_computation.32 | async-start | bytes 1327104
  1480.7 155.0 %copy-start.47 = (bf16[4,120,1152]{2,1,0:T(8,128)(2,1)S(1)}, bf16[4,120,1152]{2,1,0:T(8,128)(2,1)}, u32[]{:S(2)}) copy-start(bf16[4,120,1152]{2,1,0:T(8,128)(2,1)} %broadcast_select_fusion.1) | copy-start | bytes 3317764
  1480.7 489.4 %reduce-scatter.45.cloned.1.call-start = ((), (), s32[]{:S(2)}) async-start(), calls=%async_computation.36 | async-start | bytes 1327104
  1635.6 352.8 %reduce-scatter.33.cloned.1.call-start = ((), (), s32[]{:S(2)}) async-start(), calls=%async_computation.30 | async-start | bytes 995328 | tf_op jit(solution)/shard_map/reduce_scatter | solution.py:397
  1639.5 119.0 %copy-start.88 = (pred[4]{0:T(512)(128)(4,1)S(1)}, pred[4]{0:T(512)(128)(4,1)}, u32[]{:S(2)}) copy-start(pred[4]{0:T(512)(128)(4,1)} %copy-done.87) | copy-start | bytes 16
  1646.5 236.9 %copy-start.75 = (bf16[4,128]{1,0:T(4,128)(2,1)S(1)}, bf16[4,128]{1,0:T(4,128)(2,1)}, u32[]{:S(2)}) copy-start(bf16[4,128]{1,0:T(4,128)(2,1)} %copy-done.74) | copy-start | bytes 3076
  1646.5 236.9 %copy-start.77 = (bf16[4,128]{1,0:T(4,128)(2,1)S(1)}, bf16[4,128]{1,0:T(4,128)(2,1)}, u32[]{:S(2)}) copy-start(bf16[4,128]{1,0:T(4,128)(2,1)} %copy-done.76) | copy-start | bytes 3076
  (86 other events, 1005.6 us)
Sparse Core Ops, SparseCore 0:
  10.2 43.0 all-gather.16
  55.4 41.9 all-gather.28
  99.7 48.9 all-gather.20
  150.7 37.8 all-gather.24
  190.5 38.1 all-gather.32
  230.8 38.1 all-gather.36
  271.1 55.1 all-gather.40
  327.9 47.9 all-gather.18
  378.1 59.7 all-gather.44
  439.3 67.9 all-gather.30
  509.4 99.1 all-gather.22
  610.0 48.8 all-gather.26
  660.5 39.3 all-gather.34
  701.3 39.3 all-gather.38
  742.2 130.9 all-gather.42
  874.5 130.9 all-gather.46
  1078.9 63.8 reduce-scatter.52
  1243.0 64.0 reduce-scatter.50
  1311.1 63.1 reduce-scatter.48
  1378.7 99.6 reduce-scatter.46
  1482.5 150.7 reduce-scatter.34
  1637.3 119.5 reduce-scatter.30
  1763.1 120.2 all-reduce.10
  1886.0 12.8 reduce-scatter.42
  1901.8 12.0 reduce-scatter.40
  1916.5 12.0 reduce-scatter.38
  1930.7 18.4 reduce-scatter.36
  1951.5 18.5 reduce-scatter.44
  1972.3 16.0 reduce-scatter.32
where the time goes:
time: 2010 us; the launch traced here: 2000 us
  waiting for transfers between devices  1080 us (54%)
  matrix products  422 us (21%)
  local copies, waits for them, and re-layouts  228 us (11%)
  blocking collectives  143 us (7%)
  other arithmetic  99.3 us (5%)
    psum x1, blocking collectives, body(): lax.psum((cross_kv_part, bias_part, bias_hidden_grad, mod_part), ('frames...  143 us
    psum x1, waiting for transfers between devices, body(): lax.psum((cross_kv_part, bias_part, bias_hidden_grad, mod_part), ('frames...  122 us
    all_gather x1, waiting for transfers between devices, gather_forward(): lax.all_gather(row_parts[7], 'frames', axis=1, tiled=True)  115 us
    reduce_scatter x1, waiting for transfers between devices, body(): lax.psum_scatter(grads[4].astype(jnp.bfloat16), 'patches', scatter_dimens...  110 us
    unnamed x38, waiting for transfers between devices  101 us
    all_gather x1, waiting for transfers between devices, gather_forward(): lax.all_gather(row_parts[1], 'frames', axis=1, tiled=True)  94.5 us
    dot_general x8, matrix products, forward_dot(): return jnp.dot(left, right, preferred_element_type=jnp.float32)  76.4 us
    dot_general x7, matrix products, times_transposed(): jnp.einsum('re,de->rd', grad, weight, preferred_element_type=jnp.float32)  75.2 us
  transfers between devices with their start and end apart: 33, of which 23 were waited for; matrix products, arithmetic and copies ran while one was open for 33% of the time, Pallas kernels for 0%

commit v1 on v0

--- a/solution.py
+++ b/solution.py
@@ -4,9 +4,12 @@
 import jax
 import jax.numpy as jnp
 from jax import lax
+from jax.experimental import pallas as pl
+from jax.experimental.pallas import tpu as pltpu
 from jax.sharding import PartitionSpec as P
 
 HEADS = 16
+MESH = pl.DeviceIdType.MESH
 
 
 HIGH = lax.Precision.HIGHEST
@@ -86,26 +89,307 @@
     )
 
 
-def gather_backward(shards):
-    row_parts = (
-        lax.all_gather(shards[0], "patches", axis=0, tiled=True),
-        lax.all_gather(shards[1], "patches", axis=0, tiled=True),
-        lax.all_gather(shards[2], "patches", axis=0, tiled=True),
-        lax.all_gather(shards[3], "patches", axis=0, tiled=True),
-        lax.all_gather(shards[4], "patches", axis=0, tiled=True),
-        lax.all_gather(shards[5], "patches", axis=0, tiled=True),
-        lax.all_gather(shards[6], "patches", axis=0, tiled=True),
-        lax.all_gather(shards[7], "patches", axis=0, tiled=True),
-    )
+class Place:
+    def __init__(self):
+        self.y=lax.axis_index("frames"); p=lax.axis_index("patches")
+        self.z=p//4; self.x=lax.rem(p//2,2); self.c=lax.rem(p,2)
+    def dev(self,y=None,z=None,x=None,c=None):
+        y=self.y if y is None else y; z=self.z if z is None else z
+        x=self.x if x is None else x; c=self.c if c is None else c
+        return (y,(z*2+x)*2+c)
+    def zoff(self,d): return lax.rem(self.z+d,4)
+
+def barrier(pos):
+    bar=pltpu.get_barrier_semaphore()
+    peers=[pos.dev(z=pos.zoff(d)) for d in (1,2,3)]+[pos.dev(x=1-pos.x),pos.dev(y=1-pos.y),pos.dev(c=1-pos.c)]
+    for t in peers: pl.semaphore_signal(bar,inc=1,device_id=t,device_id_type=MESH)
+    pl.semaphore_wait(bar,6)
+
+N_AG=9
+class Gather:
+    def __init__(self,pos,shard,full,send,recv,first):
+        self.pos=pos; self.shard=shard; self.full=full; self.send=send; self.recv=recv; self.first=first
+    def _rc(self,i,src,dst,dev):
+        return pltpu.make_async_remote_copy(src_ref=src,dst_ref=dst,send_sem=self.send.at[i],recv_sem=self.recv.at[i],device_id=dev,device_id_type=MESH)
+    def _copies(self):
+        p=self.pos; F=self.full; y,z,x,c=p.y,p.z,p.x,p.c
+        cs=[]
+        mine=F.at[y,z,x,c]
+        for d in (1,2,3):
+            cs.append(self._rc(d-1,self.shard,mine,p.dev(z=p.zoff(d))))
+        line=F.at[y,:,x,c]
+        if self.first=="x":
+            cs.append(self._rc(3,line,line,p.dev(x=1-x)))
+            plane=F.at[y,:,:,c]
+            cs.append(self._rc(4,plane,plane,p.dev(y=1-y)))
+            got1=F.at[y,:,1-x,c]; got2=F.at[1-y,:,:,c]
+        else:
+            cs.append(self._rc(3,line,line,p.dev(y=1-y)))
+            plane=F.at[:,:,x,c]
+            cs.append(self._rc(4,plane,plane,p.dev(x=1-x)))
+            got1=F.at[1-y,:,x,c]; got2=F.at[:,:,1-x,c]
+        o=p.dev(c=1-c)
+        cs.append(self._rc(5,line,line,o)); cs.append(self._rc(6,got1,got1,o)); cs.append(self._rc(7,got2,got2,o))
+        return cs
+    def start(self):
+        self.cs=self._copies()
+        p=self.pos
+        for i in (0,1,2): self.cs[i].start()
+        self.loc=pltpu.make_async_copy(self.shard,self.full.at[p.y,p.z,p.x,p.c],self.send.at[8])
+        self.loc.start()
+    def step1(self):
+        self.loc.wait()
+        for i in (0,1,2): self.cs[i].wait_recv()
+        self.cs[3].start(); self.cs[5].start()
+    def step2(self):
+        self.cs[3].wait_recv(); self.cs[4].start(); self.cs[6].start()
+    def step3(self):
+        self.cs[4].wait_recv(); self.cs[7].start()
+    def finish(self):
+        for i in (5,6,7): self.cs[i].wait_recv()
+        for i in range(8): self.cs[i].wait_send()
+
+N_RS=6
+class Scatter:
+    def __init__(self,pos,part,out,bufs,send,recv,first):
+        self.pos=pos; self.part=part; self.out=out; self.send=send; self.recv=recv; self.first=first
+        self.own,self.r1,self.r2,self.r3,self.r4=bufs
+    def _rc(self,i,src,dst,dev):
+        return pltpu.make_async_remote_copy(src_ref=src,dst_ref=dst,send_sem=self.send.at[i],recv_sem=self.recv.at[i],device_id=dev,device_id_type=MESH)
+    def start(self):
+        p=self.pos
+        self.loc=pltpu.make_async_copy(self.part.at[:,:,:,p.c],self.own,self.send.at[6])
+        self.cc=self._rc(0,self.part.at[:,:,:,1-p.c],self.r1,p.dev(c=1-p.c))
+        self.loc.start(); self.cc.start()
+    def step1(self):
+        p=self.pos; own=self.own
+        self.loc.wait(); self.cc.wait_recv()
+        def body(i,_):
+            f,r=i//8,lax.rem(i,8); z,x=r//2,lax.rem(r,2)
+            own[f,z,x]=(own[f,z,x].astype(jnp.float32)+self.r1[f,z,x].astype(jnp.float32)).astype(jnp.bfloat16)
+            return 0
+        lax.fori_loop(0,16,body,0)
+        if self.first=="y": self.c1=self._rc(1,own.at[1-p.y],self.r2,p.dev(y=1-p.y))
+        else: self.c1=self._rc(1,own.at[:,:,1-p.x],self.r2,p.dev(x=1-p.x))
+        self.c1.start()
+    def step2(self):
+        p=self.pos; own=self.own
+        self.c1.wait_recv()
+        def body(i,_):
+            if self.first=="y": f,z,x=p.y,i//2,lax.rem(i,2); a,b=z,x
+            else: f,z,x=i//4,lax.rem(i,4),p.x; a,b=f,z
+            own[f,z,x]=(own[f,z,x].astype(jnp.float32)+self.r2[a,b].astype(jnp.float32)).astype(jnp.bfloat16)
+            return 0
+        lax.fori_loop(0,8,body,0)
+        if self.first=="y": self.c2=self._rc(2,own.at[p.y,:,1-p.x],self.r3,p.dev(x=1-p.x))
+        else: self.c2=self._rc(2,own.at[1-p.y,:,p.x],self.r3,p.dev(y=1-p.y))
+        self.c2.start()
+    def step3(self):
+        p=self.pos; own=self.own
+        self.c2.wait_recv()
+        def body(z,_):
+            own[p.y,z,p.x]=(own[p.y,z,p.x].astype(jnp.float32)+self.r3[z].astype(jnp.float32)).astype(jnp.bfloat16)
+            return 0
+        lax.fori_loop(0,4,body,0)
+        self.cz=[self._rc(2+d,own.at[p.y,p.zoff(d),p.x],self.r4.at[d-1],p.dev(z=p.zoff(d))) for d in (1,2,3)]
+        for c in self.cz: c.start()
+    def step4(self):
+        p=self.pos
+        for c in self.cz: c.wait_recv()
+        f32=jnp.float32
+        self.out[...]=((self.own[p.y,p.z,p.x].astype(f32)+self.r4[0].astype(f32))+(self.r4[1].astype(f32)+self.r4[2].astype(f32)))
+    def finish(self):
+        for c in [self.cc,self.c1,self.c2]+self.cz: c.wait_send()
+def scatter_bufs(R,C,first):
+    bf=jnp.bfloat16
+    return [pltpu.VMEM((2,4,2,R,C),bf),pltpu.VMEM((2,4,2,R,C),bf),
+      pltpu.VMEM((4,2,R,C) if first=="y" else (2,4,R,C),bf),pltpu.VMEM((4,R,C),bf),pltpu.VMEM((3,R,C),bf)]
+
+
+def part_of(ref, rows, cols, lead):
+    index = [slice(None)] * lead
+    index.append(pl.ds(*rows) if rows else slice(None))
+    index.append(pl.ds(*cols) if cols else slice(None))
+    return ref.at[tuple(index)]
+
+
+def gather_kernel(units, count, *refs):
+    shards, fulls = refs[:count], refs[count : 2 * count]
+    send, recv = refs[2 * count :]
+    pos = Place()
+    barrier(pos)
+    work = [
+        Gather(
+            pos,
+            part_of(shards[a], r, c, 0),
+            part_of(fulls[a], r, c, 4),
+            send.at[k],
+            recv.at[k],
+            first,
+        )
+        for k, (a, r, c, first) in enumerate(units)
+    ]
+    for unit in work:
+        unit.start()
+    total = len(work)
+    for t in range(total + 2):
+        if t < total:
+            work[t].step1()
+        if 0 <= t - 1 < total:
+            work[t - 1].step2()
+        if 0 <= t - 2 < total:
+            work[t - 2].step3()
+    for unit in work:
+        unit.finish()
+
+
+def gather_call(shards, units, ident):
+    count = len(shards)
+    return pl.pallas_call(
+        partial(gather_kernel, units, count),
+        out_shape=[jax.ShapeDtypeStruct((2, 4, 2, 2) + s.shape, s.dtype) for s in shards],
+        in_specs=[pl.BlockSpec(memory_space=pl.ANY)] * count,
+        out_specs=[pl.BlockSpec(memory_space=pl.ANY)] * count,
+        scratch_shapes=[
+            pltpu.SemaphoreType.DMA((len(units), N_AG)),
+            pltpu.SemaphoreType.DMA((len(units), 8)),
+        ],
+        compiler_params=pltpu.CompilerParams(collective_id=ident, has_side_effects=True),
+        name="gather",
+    )(*shards)
+
+
+def scatter_kernel(units, count, *refs):
+    parts, outs = refs[:count], refs[count : 2 * count]
+    rest = refs[2 * count :]
+    send, recv = rest[-2:]
+    pos = Place()
+    barrier(pos)
+    work = [
+        Scatter(
+            pos,
+            part_of(parts[a], r, c, 4),
+            part_of(outs[a], r, c, 0),
+            rest[5 * k : 5 * k + 5],
+            send.at[k],
+            recv.at[k],
+            first,
+        )
+        for k, (a, r, c, first) in enumerate(units)
+    ]
+    total = len(work)
+    for unit in work:
+        unit.start()
+    for t in range(total + 3):
+        if t < total:
+            work[t].step1()
+        if 0 <= t - 1 < total:
+            work[t - 1].step2()
+        if 0 <= t - 2 < total:
+            work[t - 2].step3()
+        if 0 <= t - 3 < total:
+            work[t - 3].step4()
+    for unit in work:
+        unit.finish()
+
+
+def scatter_call(parts, units, ident):
+    count = len(parts)
+    scratch = []
+    for a, r, c, first in units:
+        rows, cols = parts[a].shape[-2:]
+        scratch += scatter_bufs(r[1] if r else rows, c[1] if c else cols, first)
+    return pl.pallas_call(
+        partial(scatter_kernel, units, count),
+        out_shape=[jax.ShapeDtypeStruct(p.shape[-2:], jnp.float32) for p in parts],
+        in_specs=[pl.BlockSpec(memory_space=pl.ANY)] * count,
+        out_specs=[pl.BlockSpec(memory_space=pltpu.VMEM)] * count,
+        scratch_shapes=scratch
+        + [
+            pltpu.SemaphoreType.DMA((len(units), 7)),
+            pltpu.SemaphoreType.DMA((len(units), N_RS)),
+        ],
+        compiler_params=pltpu.CompilerParams(
+            collective_id=ident, has_side_effects=True, vmem_limit_bytes=60 * 2**20
+        ),
+        name="scatter",
+    )(*parts)
+
+
+GATHER_UNITS = (
+    (0, None, (0, 1152), "x"),
+    (0, None, (1152, 1152), "y"),
+    (1, None, None, "x"),
+    (4, None, None, "y"),
+    (2, None, (0, 1152), "x"),
+    (2, None, (1152, 1152), "y"),
+    (3, (0, 144), None, "x"),
+    (3, (144, 144), None, "y"),
+)
+
+
+def fast_gather(self_qkv, self_out, cross_q, cross_kv, cross_out, mlp_in, mlp_out):
+    first = jnp.concatenate([self_qkv, self_out], axis=1)
+    second = jnp.concatenate([cross_q, cross_out], axis=1)
+    got = gather_call([first, second, mlp_in, mlp_out, cross_kv], GATHER_UNITS, 0)
+    got = [g.reshape(2, -1, g.shape[-1]) for g in got]
+    qkv_cols = self_qkv.shape[1]
+    q_cols = cross_q.shape[1]
+
+    def whole(array, low, high):
+        return jnp.concatenate([array[0, :, low:high], array[1, :, low:high]], axis=1)
+
     return (
-        lax.all_gather(row_parts[0], "frames", axis=1, tiled=True),
-        lax.all_gather(row_parts[1], "frames", axis=1, tiled=True),
-        lax.all_gather(row_parts[2], "frames", axis=1, tiled=True),
-        lax.all_gather(row_parts[3], "frames", axis=1, tiled=True),
-        lax.all_gather(row_parts[4], "frames", axis=1, tiled=True),
-        lax.all_gather(row_parts[5], "frames", axis=1, tiled=True),
-        lax.all_gather(row_parts[6], "frames", axis=1, tiled=True),
-        lax.all_gather(row_parts[7], "frames", axis=1, tiled=True),
+        whole(got[0], 0, qkv_cols),
+        whole(got[0], qkv_cols, got[0].shape[-1]),
+        whole(got[1], 0, q_cols),
+        whole(got[4], 0, cross_kv.shape[1]),
+        whole(got[1], q_cols, got[1].shape[-1]),
+        whole(got[2], 0, mlp_in.shape[1]),
+        whole(got[3], 0, mlp_out.shape[1]),
+    )
+
+
+def blocks_of(grad):
+    grad = grad.astype(jnp.bfloat16)
+    rows, cols = grad.shape
+    return grad.reshape(16, rows // 16, 2, cols // 2).transpose(2, 0, 1, 3).reshape(
+        2, 4, 2, 2, rows // 16, cols // 2
+    )
+
+
+def fast_scatter(qkv, out, q, cross_out, mlp_in, mlp_out):
+    (in_shard, mlp_out_shard) = scatter_call(
+        [blocks_of(mlp_in), blocks_of(mlp_out)],
+        (
+            (0, None, (0, 1152), "x"),
+            (0, None, (1152, 1152), "y"),
+            (1, (0, 144), None, "x"),
+            (1, (144, 144), None, "y"),
+        ),
+        1,
+    )
+    first = jnp.concatenate([blocks_of(qkv), blocks_of(out)], axis=-1)
+    second = jnp.concatenate([blocks_of(q), blocks_of(cross_out)], axis=-1)
+    first, second = scatter_call(
+        [first, second],
+        (
+            (0, None, (0, 1152), "x"),
+            (0, None, (1152, 1152), "y"),
+            (1, None, (0, 640), "x"),
+            (1, None, (640, 512), "y"),
+        ),
+        2,
+    )
+    cut = qkv.shape[1] // 2
+    half = q.shape[1] // 2
+    return (
+        first[:, :cut],
+        first[:, cut:],
+        second[:, :half],
+        second[:, half:],
+        in_shard,
+        mlp_out_shard,
     )
 
 
@@ -159,8 +443,12 @@
     frame_index = lax.axis_index("frames")
     patch_index = lax.axis_index("patches")
     shards = (time_proj, self_qkv, self_out, cross_q, cross_kv, cross_out, mlp_in, mlp_out)
-    weights = gather_forward(shards)
-    full_time, full_qkv, full_out, full_q, full_kv, full_cross_out, full_in, full_mlp_out = weights
+    fast = lax.axis_size("frames") == 2 and lax.axis_size("patches") == 16
+    if fast:
+        weights = fast_gather(*shards[1:])
+    else:
+        weights = gather_forward(shards)[1:]
+    full_qkv, full_out, full_q, full_kv, full_cross_out, full_in, full_mlp_out = weights
     bias_f = biases.astype(f32)
     bias_hidden = hidden_bias.astype(f32)
     patch_ids = patch_index * patches + jnp.arange(patches, dtype=jnp.int32)
@@ -169,8 +457,15 @@
     onehot = (clip_ids[:, None] == jnp.arange(clips, dtype=jnp.int32)[None, :]).astype(f32)
     slot_ids = jnp.arange(frames, dtype=jnp.int32)
     valid = (slot_ids < count)[:, None] & (patch_mask[None, :] == 1)
-    features = time_features(timesteps, full_time.shape[0]).astype(bf16)
-    modulation = table.astype(f32) + forward_dot(features, full_time).reshape(clips, 6, width)
+    time_rows, time_cols = time_proj.shape
+    features = time_features(timesteps, time_rows * lax.axis_size("patches")).astype(bf16)
+    own_features = lax.dynamic_slice_in_dim(features, patch_index * time_rows, time_rows, 1)
+    time_part = jnp.zeros((clips, 6 * width), f32)
+    time_part = lax.dynamic_update_slice(
+        time_part, forward_dot(own_features, time_proj), (0, frame_index * time_cols)
+    )
+    time_sum = lax.psum(time_part, ("frames", "patches"))
+    modulation = table.astype(f32) + time_sum.reshape(clips, 6, width)
     per_patch = jnp.einsum("pc,ckd->pkd", onehot, modulation, precision=HIGH)
     shift_a = per_patch[:, 0]
     scale_a = per_patch[:, 1]
@@ -252,8 +547,6 @@
     mlp_res = (forward_dot(activ_r, full_mlp_out) + bias_f[6]).reshape(frames, patches, width)
     final = resid_c + gate_m * mlp_res
     block_out = jnp.where(valid[:, :, None], final, 0.0).astype(bf16)
-    weights = gather_backward(shards)
-    full_time, full_qkv, full_out, full_q, full_kv, full_cross_out, full_in, full_mlp_out = weights
     grad_final = jnp.where(valid[:, :, None], cotangent.astype(f32), 0.0)
     grad_gate_m = jnp.sum(grad_final * mlp_res, axis=0)
     grad_mlp_r = (gate_m * grad_final).astype(bf16).reshape(row_count, width)
@@ -361,46 +654,49 @@
         cross_kv.shape,
     )
     grads = (self_qkv_grad, self_out_grad, cross_q_grad, cross_out_grad, mlp_in_grad, mlp_out_grad)
-    row_sums = (
-        lax.psum_scatter(
-            grads[0].astype(jnp.bfloat16), "patches", scatter_dimension=0, tiled=True
-        ).astype(jnp.float32),
-        lax.psum_scatter(
-            grads[1].astype(jnp.bfloat16), "patches", scatter_dimension=0, tiled=True
-        ).astype(jnp.float32),
-        lax.psum_scatter(
-            grads[2].astype(jnp.bfloat16), "patches", scatter_dimension=0, tiled=True
-        ).astype(jnp.float32),
-        lax.psum_scatter(
-            grads[3].astype(jnp.bfloat16), "patches", scatter_dimension=0, tiled=True
-        ).astype(jnp.float32),
-        lax.psum_scatter(
-            grads[4].astype(jnp.bfloat16), "patches", scatter_dimension=0, tiled=True
-        ).astype(jnp.float32),
-        lax.psum_scatter(
-            grads[5].astype(jnp.bfloat16), "patches", scatter_dimension=0, tiled=True
-        ).astype(jnp.float32),
-    )
-    col_sums = (
-        lax.psum_scatter(
-            row_sums[0].astype(jnp.bfloat16), "frames", scatter_dimension=1, tiled=True
-        ).astype(jnp.float32),
-        lax.psum_scatter(
-            row_sums[1].astype(jnp.bfloat16), "frames", scatter_dimension=1, tiled=True
-        ).astype(jnp.float32),
-        lax.psum_scatter(
-            row_sums[2].astype(jnp.bfloat16), "frames", scatter_dimension=1, tiled=True
-        ).astype(jnp.float32),
-        lax.psum_scatter(
-            row_sums[3].astype(jnp.bfloat16), "frames", scatter_dimension=1, tiled=True
-        ).astype(jnp.float32),
-        lax.psum_scatter(
-            row_sums[4].astype(jnp.bfloat16), "frames", scatter_dimension=1, tiled=True
-        ).astype(jnp.float32),
-        lax.psum_scatter(
-            row_sums[5].astype(jnp.bfloat16), "frames", scatter_dimension=1, tiled=True
-        ).astype(jnp.float32),
-    )
+    if fast:
+        col_sums = fast_scatter(*grads)
+    else:
+        row_sums = (
+            lax.psum_scatter(
+                grads[0].astype(jnp.bfloat16), "patches", scatter_dimension=0, tiled=True
+            ).astype(jnp.float32),
+            lax.psum_scatter(
+                grads[1].astype(jnp.bfloat16), "patches", scatter_dimension=0, tiled=True
+            ).astype(jnp.float32),
+            lax.psum_scatter(
+                grads[2].astype(jnp.bfloat16), "patches", scatter_dimension=0, tiled=True
+            ).astype(jnp.float32),
+            lax.psum_scatter(
+                grads[3].astype(jnp.bfloat16), "patches", scatter_dimension=0, tiled=True
+            ).astype(jnp.float32),
+            lax.psum_scatter(
+                grads[4].astype(jnp.bfloat16), "patches", scatter_dimension=0, tiled=True
+            ).astype(jnp.float32),
+            lax.psum_scatter(
+                grads[5].astype(jnp.bfloat16), "patches", scatter_dimension=0, tiled=True
+            ).astype(jnp.float32),
+        )
+        col_sums = (
+            lax.psum_scatter(
+                row_sums[0].astype(jnp.bfloat16), "frames", scatter_dimension=1, tiled=True
+            ).astype(jnp.float32),
+            lax.psum_scatter(
+                row_sums[1].astype(jnp.bfloat16), "frames", scatter_dimension=1, tiled=True
+            ).astype(jnp.float32),
+            lax.psum_scatter(
+                row_sums[2].astype(jnp.bfloat16), "frames", scatter_dimension=1, tiled=True
+            ).astype(jnp.float32),
+            lax.psum_scatter(
+                row_sums[3].astype(jnp.bfloat16), "frames", scatter_dimension=1, tiled=True
+            ).astype(jnp.float32),
+            lax.psum_scatter(
+                row_sums[4].astype(jnp.bfloat16), "frames", scatter_dimension=1, tiled=True
+            ).astype(jnp.float32),
+            lax.psum_scatter(
+                row_sums[5].astype(jnp.bfloat16), "frames", scatter_dimension=1, tiled=True
+            ).astype(jnp.float32),
+        )
     qkv_shard, out_shard, q_shard, cross_out_shard, in_shard, mlp_out_shard = col_sums
     return (
         block_out,

time: 2010 us -> 1510 us (0.75)
  waiting for transfers between devices: 1080 us -> 6.56 us
  Pallas kernels: 0 us -> 479 us
  local copies, waits for them, and re-layouts: 228 us -> 348 us
  blocking collectives: 143 us -> 106 us
    all_gather x16 -> x0, waiting for transfers between devices: 716 us -> none  [the longest x1 115 us: gather_forward(): lax.all_gather(row_parts[7], 'frames', axis=1, tiled=True)]
    pallas_call x0 -> x3, Pallas kernels: none -> 479 us  [the longest x2 250 us: scatter_call(): pl.pallas_call(partial(scatter_kernel, units, count), out_shape=[jax.Shap...]
    reduce_scatter x3 -> x0, waiting for transfers between devices: 136 us -> none  [the longest x1 110 us: body(): lax.psum_scatter(grads[4].astype(jnp.bfloat16), 'patches', scatter_dimens...]
    psum x1, waiting for transfers between devices: 122 us -> 0.01 us  [body(): lax.psum((cross_kv_part, bias_part, bias_hidden_grad, mod_part), ('frames...]
    reshape x1 -> x12, local copies, waits for them, and re-layouts: 0.05 us -> 118 us  [blocks_of(): grad.reshape(16, rows // 16, 2, cols // 2).transpose(2, 0, 1, 3)]
    unnamed x38 -> x2, waiting for transfers between devices: 101 us -> 0.03 us
    psum x1, blocking collectives: 143 us -> 106 us  [body(): lax.psum((cross_kv_part, bias_part, bias_hidden_grad, mod_part), ('frames...]
    slice x0 -> x6, local copies, waits for them, and re-layouts: none -> 24.6 us  [the longest x3 19.2 us: whole(): array[0, :, low:high]]
  transfers between devices with their start and end apart: 33 -> 6, of which waited for: 23 -> 2; matrix products, arithmetic and copies ran while one was open for 33% -> 9% of each run, Pallas kernels for 0% -> 22%
where the time goes in v1:
time: 1510 us; the launch traced here: 1500 us
  Pallas kernels  479 us (32%)
  matrix products  427 us (28%)
  local copies, waits for them, and re-layouts  348 us (23%)
  other arithmetic  108 us (7%)
  blocking collectives  106 us (7%)
  between operations  16.7 us (1%)
    pallas_call x2, Pallas kernels, scatter_call(): pl.pallas_call(partial(scatter_kernel, units, count), out_shape=[jax.Shap...  250 us
    pallas_call x1, Pallas kernels, gather_call(): pl.pallas_call(partial(gather_kernel, units, count), out_shape=[jax.Shape...  229 us
    reshape x12, local copies, waits for them, and re-layouts, blocks_of(): grad.reshape(16, rows // 16, 2, cols // 2).transpose(2, 0, 1, 3)  118 us
    psum x1, blocking collectives, body(): lax.psum((cross_kv_part, bias_part, bias_hidden_grad, mod_part), ('frames...  106 us
    dot_general x7, matrix products, times_transposed(): jnp.einsum('re,de->rd', grad, weight, preferred_element_type=jnp.float32)  82.7 us
    dot_general x8, matrix products, forward_dot(): return jnp.dot(left, right, preferred_element_type=jnp.float32)  68.7 us
    dot_general x7, matrix products, outer_sum(): jnp.einsum('rd,re->de', left, right, preferred_element_type=jnp.float32)  68.6 us
    dot_general x3, matrix products, self_attend(): mixed = jnp.einsum('phst,tphd->sphd', probs, value_heads, precision=HIGH)  58.2 us
  transfers between devices with their start and end apart: 6, of which 2 were waited for; matrix products, arithmetic and copies ran while one was open for 9% of the time, Pallas kernels for 22%

profile of v1, /device:TPU:0, one launch (start us, length us, event | category | flops | bytes accessed | tf_op | source)
XLA Modules:
  0.0 1501.4 jit_solution(4222400384888364489)
XLA Ops:
  19.5 228.7 %gather.1 = (bf16[2,4,2,2,72,2304]{5,4,3,2,1,0:T(8,128)(2,1)}, bf16[2,4,2,2,72,1152]{5,4,3,2,1,0:T(8,128)(2,1)}, bf16[2,4,2,2,72,2304]{5,4,3,2,1,0:T(8,128)(2,1)...) custom-call(bf16[72,2304]{1,0:T(8,128)(2,1)} %pad_maximum_fusion.35.refs_0_, ...), custom_call_target="tpu_custom_call" | custom-call | tf_op jit(solution)/shard_map/gather/pallas_call | solution.py:248
  265.6 8.7 fusion.114
  274.3 10.1 fusion.113
  298.8 8.8 add_convert_fusion
  342.5 10.8 copy.126
  365.0 11.0 copy.128
  376.0 11.0 copy.127
  387.1 9.6 fusion.16
  396.7 9.4 fusion.108
  407.2 17.9 %convert_bitcast_fusion.1 = bf16[9,96,16,72]{3,0,2,1:T(8,128)(2,1)} fusion(bf16[11,96,16,72]{3,0,2,1:T(8,128)(2,1)S(1)} %copy-done.25, f32[96,16,9]{2,1,0:T(8,128)S(1)} %fusion.108, f32[96,16,9,11]{3,2,1,0:T(8,128)S(1)} %copy-done.6, f32[96,16,9]{2,1,0:T(8,128)S(1)} %get-tuple-element.99, pred[9,11]{1,0:T(8,128)(4,1)S(1)} %fusion.74), kind=kOutput, calls=%fused_computation.66 | convolution fusion | flops 132986880 | bytes 5142627 | tf_op jit(solution)/shard_map/jvp(phst,tphd->sphd)/dot_general | solution.py:407
  425.1 8.5 copy.149
  464.2 16.1 %fusion.120 = (f32[864,16]{0,1:T(8,128)S(1)}, f32[864,16,480]{0,2,1:T(8,128)}) fusion(pred[864,480]{0,1:T(8,128)(4,1)} %broadcast_compare_fusion, bf16[480,16,72]{0,2,1:T(8,128)(2,1)S(1)} %bitcast.255, bf16[864,16,72]{0,2,1:T(8,128)(2,1)} %bitcast.250), kind=kOutput, calls=%fused_computation.255 | convolution fusion | flops 982057408 | bytes 30108672 | tf_op jit(solution)/shard_map/sub | solution.py:533
  480.4 13.0 fusion.62
  501.8 18.8 %fusion.36 = f32[864,4608]{1,0:T(8,128)} fusion(bf16[864,1152]{1,0:T(8,128)(2,1)S(1)} %bitcast.292, bf16[1152,2304]{1,0:T(8,128)(2,1)} %bitcast.270, bf16[1152,2304]{1,0:T(8,128)(2,1)} %bitcast.268), kind=kOutput, calls=%fused_computation.63 | convolution fusion | flops 9194176512 | bytes 28532736 | tf_op jit(solution)/shard_map/dot_general | solution.py:54
  520.6 21.1 %convolution_convert_fusion = bf16[4608,1152]{1,0:T(8,128)(2,1)} fusion(bf16[864,1152]{1,0:T(8,128)(2,1)} %bitcast.288, f32[864,4608]{1,0:T(8,128)} %fusion.36, f32[4608]{0:T(1024)S(1)} %copy-done.96), kind=kOutput, calls=%fused_computation.11 | convolution fusion | flops 9218064384 | bytes 28551168 | tf_op jit(solution)/shard_map/rd,re->de/dot_general | solution.py:58
  541.8 25.7 %convert_reduce_fusion = (f32[4608]{0:T(1024)}, bf16[864,4608]{1,0:T(8,128)(2,1)}) fusion(f32[864,4608]{1,0:T(8,128)} %fusion.36, f32[4608]{0:T(1024)S(1)} %copy-done.96, bf16[864,1152]{1,0:T(8,128)(2,1)} %bitcast.289, bf16[4608,576]{1,0:T(8,128)(2,1)S(1)} %bitcast.267, bf16[4608,576]{1,0:T(8,128)(2,1)S(1)} %bitcast.263), kind=kOutput, calls=%fused_computation.21 | convolution fusion | flops 9285742592 | bytes 36532224 | tf_op jit(solution)/shard_map/re,de->rd/dot_general | solution.py:62
  567.4 22.9 %fusion.50 = f32[864,1152]{1,0:T(8,128)} fusion(bf16[4608,576]{1,0:T(8,128)(2,1)} %bitcast.264, bf16[4608,576]{1,0:T(8,128)(2,1)} %bitcast.260, f32[1152]{0:T(1024)S(1)} %copy-done.108, f32[864,4608]{1,0:T(8,128)} %fusion.36, f32[4608]{0:T(1024)S(1)} %copy-done.96), kind=kOutput, calls=%fused_computation.91 | convolution fusion | flops 9234984960 | bytes 30546432 | tf_op jit(solution)/shard_map/dot_general | solution.py:54
  590.4 17.5 %fusion.35 = f32[864,1152]{1,0:T(8,128)} fusion(bf16[864,4608]{1,0:T(8,128)(2,1)} %get-tuple-element.115, bf16[1152,2304]{1,0:T(8,128)(2,1)} %bitcast.271, bf16[1152,2304]{1,0:T(8,128)(2,1)} %bitcast.269), kind=kOutput, calls=%fused_computation.62 | convolution fusion | flops 9194176512 | bytes 22560768 | tf_op jit(solution)/shard_map/re,de->rd/dot_general | solution.py:62
  631.3 13.8 convolution_convert_fusion.1
  649.1 13.4 fusion.31
  662.5 20.0 %fusion.1 = (f32[864,16]{0,1:T(8,128)S(1)}, f32[16,480,864]{2,1,0:T(8,128)}) fusion(f32[864,16,480]{0,2,1:T(8,128)} %get-tuple-element.102, f32[864,16]{0,1:T(8,128)S(1)} %copy-done.90, bf16[480,16,72]{0,2,1:T(8,128)(2,1)} %bitcast.295, bf16[864,16,72]{0,2,1:T(8,128)(2,1)} %bitcast.284), kind=kOutput, calls=%fused_computation.3 | convolution fusion | flops 975407616 | bytes 56291328 | tf_op jit(solution)/shard_map/rhd,khd->rhk/dot_general | solution.py:570
  682.4 23.9 %fusion.3 = bf16[864,16,480]{0,2,1:T(8,128)(2,1)} fusion(f32[16,480,864]{2,1,0:T(8,128)} %get-tuple-element.104, f32[864,16]{0,1:T(8,128)S(1)} %get-tuple-element.103, f32[864,16,480]{0,2,1:T(8,128)} %get-tuple-element.102, f32[864,16]{0,1:T(8,128)S(1)} %copy-done.90), kind=kLoop, calls=%fused_computation.5 | loop fusion | flops 26542080 | bytes 66465792 | tf_op jit(solution)/shard_map/convert_element_type | solution.py:574
  706.4 10.6 convolution_multiply_fusion
  717.0 9.6 convert_reduce_fusion.3
  739.5 9.6 convert_reduce_fusion.6
  755.0 8.5 reshape_reshape.3
  763.5 18.6 %multiply_reduce_fusion = (f32[96,16,9]{2,1,0:T(8,128)S(1)}, f32[96,16,9,11]{3,2,1,0:T(8,128)}) fusion(f32[96,16,9]{2,1,0:T(8,128)} %multiply_divide_fusion, f32[96,16,9]{2,1,0:T(8,128)S(1)} %copy-done.37, f32[96,16,9,11]{3,2,1,0:T(8,128)} %get-tuple-element.100, pred[9,11]{1,0:T(8,128)(4,1)S(1)} %copy-done.101, bf16[11,96,16,72]{3,0,2,1:T(8,128)(2,1)} %copy.128, ...), kind=kOutput, calls=%fused_computation.30 | convolution fusion | flops 22795776 | bytes 5806179 | tf_op jit(solution)/shard_map/transpose(jvp(phst,tphd->sphd))/dot_general | solution.py:407
  782.3 22.7 %convert_reduce_fusion.1 = (f32[16,72]{1,0:T(8,128)S(1)}, bf16[9,96,16,72]{3,0,2,1:T(8,128)(2,1)}) fusion(bf16[11,96,16,72]{3,0,2,1:T(8,128)(2,1)S(1)} %bitcast.234, f32[96,16,9,11]{3,2,1,0:T(8,128)} %get-tuple-element.107, f32[96,16,9]{2,1,0:T(8,128)S(1)} %neg.13, f32[96,16,9]{2,1,0:T(8,128)S(1)} %copy-done.39, pred[9,11]{1,0:T(8,128)(4,1)S(1)} %copy-done.101, ...), kind=kOutput, calls=%fused_computation.28 | convolution fusion | flops 135584640 | bytes 5810787 | tf_op jit(solution)/shard_map/transpose(jvp(sphd,tphd->phst))/dot_general | solution.py:402
  805.0 25.9 %convolution_bitcast_fusion.2 = f32[11,96,16,72]{3,0,2,1:T(8,128)} fusion(bf16[9,96,16,72]{3,0,2,1:T(8,128)(2,1)S(1)} %bitcast.232, f32[96,16,9,11]{3,2,1,0:T(8,128)} %get-tuple-element.107, f32[96,16,9]{2,1,0:T(8,128)S(1)} %neg.13, f32[96,16,9]{2,1,0:T(8,128)S(1)} %copy-done.39, pred[9,11]{1,0:T(8,128)(4,1)S(1)} %copy-done.101, ...), kind=kOutput, calls=%fused_computation.90 | convolution fusion | flops 132599808 | bytes 8239203 | tf_op jit(solution)/shard_map/transpose(jvp(sphd,tphd->phst))/dot_general | solution.py:402
  830.9 21.7 %fusion.47 = f32[11,96,16,72]{3,0,2,1:T(8,128)} fusion(f32[96,16,9]{2,1,0:T(8,128)S(1)} %copy-done.39, bf16[96,16,72,9]{2,1,0,3:T(8,128)(2,1)S(1)} %bitcast.275, f32[96,16,9,11]{3,2,1,0:T(8,128)S(1)} %bitcast.218, f32[96,16,9]{2,1,0:T(8,128)S(1)} %copy-done.37, pred[9,11]{1,0:T(8,128)(4,1)S(1)} %copy-done.101), kind=kOutput, calls=%fused_computation.89 | convolution fusion | flops 131991552 | bytes 7575651 | tf_op jit(solution)/shard_map/transpose(jvp(phst,tphd->sphd))/dot_general | solution.py:407
  852.6 25.2 %reshape.600 = bf16[16,288,2,576]{3,2,1,0:T(2,128)(2,1)} reshape(bf16[4608,1152]{1,0:T(8,128)(2,1)} %convolution_convert_fusion) | data formatting | bytes 21233664 | tf_op jit(solution)/shard_map/reshape | solution.py:356
  877.8 11.5 copy.155
  895.6 14.5 reshape.598
  910.2 10.4 copy.154
  920.6 148.2 %scatter.3 = (f32[72,2304]{1,0:T(8,128)}, f32[288,576]{1,0:T(8,128)}) custom-call(bf16[2,4,2,2,72,2304]{5,4,3,2,1,0:T(8,128)(2,1)} %bitcast.224, bf16[2,4,2,2,288,576]{5,4,3,2,1,0:T(8,128)(2,1)} %bitcast.219), custom_call_target="tpu_custom_call" | custom-call | tf_op jit(solution)/shard_map/scatter/pallas_call | solution.py:302
  1078.9 7.4 reshape.594
  1094.7 7.8 reshape.591
  1106.3 11.4 copy.145
  1117.7 11.3 copy.141
  1142.0 8.6 copy.138
  1180.7 106.0 %all-reduce.11 = (bf16[480,2304]{0,1:T(8,128)(2,1)}, f32[7,1152]{1,0:T(8,128)S(1)}, f32[4608]{0:T(1024)}) all-reduce(f32[480,2304]{0,1:T(8,128)} %pad_maximum_fusion.14, f32[7,1152]{1,0:T(8,128)S(1)} %stack.58, f32[4608]{0:T(1024)S(1)} %copy-done.95), channel_id=1, replica_groups=mesh['frames'=2,'patches'=16] {'frames','patches'}, use_global_device_ids=true, to_apply=%region_17.18 | all-reduce | flops 1118592 | bytes 6736896 | tf_op jit(solution)/shard_map/psum | solution.py:632
  1286.7 7.4 fusion.57
  1294.3 13.6 fusion.55
  1307.9 14.0 fusion.12
  1339.4 19.2 %reshape.589 = bf16[16,72,2,1728]{3,2,1,0:T(2,128)(2,1)} reshape(bf16[1152,3456]{1,0:T(8,128)(2,1)} %fusion.12) | data formatting | bytes 15925248 | tf_op jit(solution)/shard_map/reshape | solution.py:356
  1358.7 7.9 copy.148
  1366.5 10.7 pad_maximum_fusion.2.refs_0_
  1377.2 102.1 %scatter.2 = (f32[72,2304]{1,0:T(8,128)}, f32[72,1152]{1,0:T(8,128)}) custom-call(bf16[2,4,2,2,72,2304]{5,4,3,2,1,0:T(8,128)(2,1)} %pad_maximum_fusion.2.refs_0_, bf16[2,4,2,2,72,1152]{5,4,3,2,1,0:T(8,128)(2,1)} %pad_maximum_fusion.11.refs_1_), custom_call_target="tpu_custom_call" | custom-call | tf_op jit(solution)/shard_map/scatter/pallas_call | solution.py:302
  (437 shorter events, 279.7 us)
Async XLA Ops:
  7.2 282.9 %all-reduce.8.cloned.1.call-start = ((), (), s32[]{:S(2)}) async-start(), calls=%async_computation | async-start | bytes 221184 | tf_op jit(solution)/shard_map/psum | solution.py:467
  8.3 246.7 %copy-start.103 = (bf16[4,128]{1,0:T(4,128)(2,1)}, bf16[4,128]{1,0:T(4,128)(2,1)S(1)}, u32[]{:S(2)}) copy-start(bf16[4,128]{1,0:T(4,128)(2,1)S(1)} %get-tuple-element.97) | copy-start | bytes 3076
  8.3 246.7 %copy-start.105 = (bf16[4,128]{1,0:T(4,128)(2,1)}, bf16[4,128]{1,0:T(4,128)(2,1)S(1)}, u32[]{:S(2)}) copy-start(bf16[4,128]{1,0:T(4,128)(2,1)S(1)} %get-tuple-element.98) | copy-start | bytes 3076
  9.2 1477.9 %all-reduce.10.cloned.1.call-start = ((), (), s32[]{:S(2)}) async-start(), calls=%async_computation.1 | async-start | bytes 221184 | tf_op jit(solution)/shard_map/psum | solution.py:632
  10.6 244.8 %copy-start.116 = (pred[4]{0:T(512)(128)(4,1)}, pred[4]{0:T(512)(128)(4,1)S(1)}, u32[]{:S(2)}) copy-start(pred[4]{0:T(512)(128)(4,1)S(1)} %broadcast_compare_fusion.1) | copy-start | bytes 16
  12.1 273.5 %copy-start.112 = (pred[9]{0:T(512)(128)(4,1)}, pred[9]{0:T(512)(128)(4,1)S(1)}, u32[]{:S(2)}) copy-start(pred[9]{0:T(512)(128)(4,1)S(1)} %get-tuple-element.119) | copy-start | bytes 31
  12.2 273.5 %copy-start.114 = (pred[9]{0:T(512)(128)(4,1)}, pred[9]{0:T(512)(128)(4,1)S(1)}, u32[]{:S(2)}) copy-start(pred[9]{0:T(512)(128)(4,1)S(1)} %get-tuple-element.120) | copy-start | bytes 31
  12.4 277.8 %copy-start.110 = (s32[96]{0:T(128)}, s32[96]{0:T(128)S(1)}, u32[]{:S(2)}) copy-start(s32[96]{0:T(128)S(1)} %convert_reduce_fusion.9) | copy-start | bytes 1156
  14.3 279.3 %copy-start.74 = (f32[9,96]{1,0:T(8,128)}, f32[9,96]{1,0:T(8,128)S(1)}, u32[]{:S(2)}) copy-start(f32[9,96]{1,0:T(8,128)S(1)} %broadcast_multiply_fusion.1) | copy-start | bytes 10372
  17.2 276.4 %copy-start.78 = (f32[9,96]{1,0:T(8,128)}, f32[9,96]{1,0:T(8,128)S(1)}, u32[]{:S(2)}) copy-start(f32[9,96]{1,0:T(8,128)S(1)} %fusion.75) | copy-start | bytes 10372
  285.7 121.5 %copy-start.100 = (pred[9,11]{1,0:T(8,128)(4,1)}, pred[9,11]{1,0:T(8,128)(4,1)S(1)}, u32[]{:S(2)}) copy-start(pred[9,11]{1,0:T(8,128)(4,1)S(1)} %fusion.74) | copy-start | bytes 301
  288.5 175.7 %copy-start.24 = (bf16[480,1152]{0,1:T(8,128)(2,1)}, bf16[480,1152]{0,1:T(8,128)(2,1)S(1)}, u32[]{:S(2)}) copy-start(bf16[480,1152]{0,1:T(8,128)(2,1)S(1)} %copy.131) | copy-start | bytes 3317764
  311.5 41.8 %collective-permute-start.1 = (bf16[1,96,2304]{2,1,0:T(8,128)(2,1)}, bf16[1,96,2304]{2,1,0:T(8,128)(2,1)}, u32[]{:S(2)}, u32[]{:S(2)}) collective-permute-start(bf16[1,96,2304]{2,1,0:T(8,128)(2,1)} %slice.201), channel_id=1, source_target_pairs={{16,0},{17,1},{18,2},{19,3},{20,4},{21,5},{22,6},{23,7},{24,8},{25... | collective-permute-start | bytes 1327112 | tf_op jit(solution)/shard_map/ppermute | solution.py:26
  323.4 32.0 %collective-permute-start = (bf16[1,96,2304]{2,1,0:T(8,128)(2,1)}, bf16[1,96,2304]{2,1,0:T(8,128)(2,1)}, u32[]{:S(2)}, u32[]{:S(2)}) collective-permute-start(bf16[1,96,2304]{2,1,0:T(8,128)(2,1)} %copy.122), channel_id=1, source_target_pairs={{0,16},{1,17},{2,18},{3,19},{4,20},{5,21},{6,22},{7,23},{8,24},{9,... | collective-permute-start | bytes 1327112 | tf_op jit(solution)/shard_map/ppermute | solution.py:25
  387.1 20.1 %copy-start.25 = (bf16[11,96,16,72]{3,0,2,1:T(8,128)(2,1)S(1)}, bf16[11,96,16,72]{3,0,2,1:T(8,128)(2,1)}, u32[]{:S(2)}) copy-start(bf16[11,96,16,72]{3,0,2,1:T(8,128)(2,1)} %copy.128) | copy-start | bytes 7299076
  480.3 13.1 copy-start.89
  499.8 20.8 %copy-start.87 = (f32[9,96]{1,0:T(8,128)}, f32[9,96]{1,0:T(8,128)S(1)}, u32[]{:S(2)}) copy-start(f32[9,96]{1,0:T(8,128)S(1)} %multiply_reduce_fusion.5) | copy-start | bytes 10372
  499.8 20.7 %copy-start.80 = (f32[9,96]{1,0:T(8,128)}, f32[9,96]{1,0:T(8,128)S(1)}, u32[]{:S(2)}) copy-start(f32[9,96]{1,0:T(8,128)S(1)} %fusion.76) | copy-start | bytes 10372
  501.8 18.8 %copy-start.49 = (bf16[9,96,1152]{2,1,0:T(8,128)(2,1)}, bf16[9,96,1152]{2,1,0:T(8,128)(2,1)S(1)}, u32[]{:S(2)}) copy-start(bf16[9,96,1152]{2,1,0:T(8,128)(2,1)S(1)} %add_convert_fusion.1) | copy-start | bytes 5971972
  501.8 18.8 %copy-start.96 = (f32[4608]{0:T(1024)S(1)}, f32[4608]{0:T(1024)}, u32[]{:S(2)}) copy-start(f32[4608]{0:T(1024)} %convert_element_type.174) | copy-start | bytes 55300
  501.8 39.9 %slice-start.13 = ((s8[5898240]{0:T(1024)(128)(4,1)}), s8[1703936]{0:T(1024)(128)(4,1)S(1)}, s32[]{:S(2)}) async-start(s8[5898240]{0:T(1024)(128)(4,1)} %bitcast.261), calls=%async_computation.15 | async-start | bytes 3407872
  501.8 39.9 %slice-start.15 = ((s8[5898240]{0:T(1024)(128)(4,1)}), s8[4194304]{0:T(1024)(128)(4,1)S(1)}, s32[]{:S(2)}) async-start(s8[5898240]{0:T(1024)(128)(4,1)} %bitcast.265), calls=%async_computation.17 | async-start | bytes 8388608
  520.6 21.1 %slice-start.14 = ((s8[5898240]{0:T(1024)(128)(4,1)}), s8[4194304]{0:T(1024)(128)(4,1)S(1)}, s32[]{:S(2)}) async-start(s8[5898240]{0:T(1024)(128)(4,1)} %bitcast.261), calls=%async_computation.16 | async-start | bytes 8388608
  520.6 21.1 %slice-start.16 = ((s8[5898240]{0:T(1024)(128)(4,1)}), s8[1703936]{0:T(1024)(128)(4,1)S(1)}, s32[]{:S(2)}) async-start(s8[5898240]{0:T(1024)(128)(4,1)} %bitcast.265), calls=%async_computation.18 | async-start | bytes 3407872
  541.7 25.7 %copy-start.108 = (f32[1152]{0:T(1024)S(1)}, f32[1152]{0:T(1024)}, u32[]{:S(2)}) copy-start(f32[1152]{0:T(1024)} %get-tuple-element.39) | copy-start | bytes 13828
  590.4 17.5 %copy-start.3 = (f32[9,96,1152]{2,1,0:T(8,128)S(1)}, f32[9,96,1152]{2,1,0:T(8,128)}, u32[]{:S(2)}) copy-start(f32[9,96,1152]{2,1,0:T(8,128)} %copy-done.2) | copy-start | bytes 11943940
  590.4 17.5 %copy-start.22 = (f32[96,1152]{1,0:T(8,128)S(1)}, f32[96,1152]{1,0:T(8,128)}, u32[]{:S(2)}) copy-start(f32[96,1152]{1,0:T(8,128)} %get-tuple-element.85) | copy-start | bytes 1327108
  590.4 17.5 %copy-start.77 = (f32[9,96]{1,0:T(8,128)S(1)}, f32[9,96]{1,0:T(8,128)}, u32[]{:S(2)}) copy-start(f32[9,96]{1,0:T(8,128)} %copy-done.76) | copy-start | bytes 10372
  590.4 17.5 %copy-start.81 = (f32[9,96]{1,0:T(8,128)S(1)}, f32[9,96]{1,0:T(8,128)}, u32[]{:S(2)}) copy-start(f32[9,96]{1,0:T(8,128)} %copy-done.80) | copy-start | bytes 10372
  682.4 23.9 %copy-start.18 = (bf16[864,1152]{0,1:T(8,128)(2,1)S(1)}, bf16[864,1152]{0,1:T(8,128)(2,1)}, u32[]{:S(2)}) copy-start(bf16[864,1152]{0,1:T(8,128)(2,1)} %copy.132) | copy-start | bytes 5971972
  755.0 27.3 %slice-start.9 = ((s8[6291456]{0:T(1024)(128)(4,1)}), s8[2097152]{0:T(1024)(128)(4,1)S(1)}, s32[]{:S(2)}) async-start(s8[6291456]{0:T(1024)(128)(4,1)} %bitcast.233), calls=%async_computation.11 | async-start | bytes 4194304
  763.5 18.7 %slice-start.10 = ((s8[6291456]{0:T(1024)(128)(4,1)}), s8[4194304]{0:T(1024)(128)(4,1)S(1)}, s32[]{:S(2)}) async-start(s8[6291456]{0:T(1024)(128)(4,1)} %bitcast.233), calls=%async_computation.12 | async-start | bytes 8388608
  763.5 18.8 %copy-start.39 = (f32[96,16,9]{2,1,0:T(8,128)S(1)}, f32[96,16,9]{2,1,0:T(8,128)}, u32[]{:S(2)}) copy-start(f32[96,16,9]{2,1,0:T(8,128)} %copy-done.38) | copy-start | bytes 165892
  763.5 41.5 %slice-start = ((s8[12582912]{0:T(1024)(128)(4,1)}), s8[4194304]{0:T(1024)(128)(4,1)S(1)}, s32[]{:S(2)}) async-start(s8[12582912]{0:T(1024)(128)(4,1)} %bitcast.217), calls=%async_computation.2 | async-start | bytes 8388608
  763.5 41.5 %slice-start.1 = ((s8[12582912]{0:T(1024)(128)(4,1)}), s8[4194304]{0:T(1024)(128)(4,1)S(1)}, s32[]{:S(2)}) async-start(s8[12582912]{0:T(1024)(128)(4,1)} %bitcast.217), calls=%async_computation.3 | async-start | bytes 8388608
  763.5 41.5 %slice-start.7 = ((s8[6291456]{0:T(1024)(128)(4,1)}), s8[2097152]{0:T(1024)(128)(4,1)S(1)}, s32[]{:S(2)}) async-start(s8[6291456]{0:T(1024)(128)(4,1)} %bitcast.231), calls=%async_computation.9 | async-start | bytes 4194304
  782.3 22.7 %slice-start.2 = ((s8[12582912]{0:T(1024)(128)(4,1)}), s8[4194304]{0:T(1024)(128)(4,1)S(1)}, s32[]{:S(2)}) async-start(s8[12582912]{0:T(1024)(128)(4,1)} %bitcast.217), calls=%async_computation.4 | async-start | bytes 8388608
  782.3 22.7 %slice-start.8 = ((s8[6291456]{0:T(1024)(128)(4,1)}), s8[4194304]{0:T(1024)(128)(4,1)S(1)}, s32[]{:S(2)}) async-start(s8[6291456]{0:T(1024)(128)(4,1)} %bitcast.231), calls=%async_computation.10 | async-start | bytes 8388608
  805.0 25.9 %copy-start.35 = (bf16[9,96,16,72]{3,2,1,0:T(8,128)(2,1)S(1)}, bf16[9,96,16,72]{3,2,1,0:T(8,128)(2,1)}, u32[]{:S(2)}) copy-start(bf16[9,96,16,72]{3,2,1,0:T(8,128)(2,1)} %reshape_reshape.3) | copy-start | bytes 5971972
  920.6 148.2 %copy-start.91 = (f32[16,72]{1,0:T(8,128)S(1)}, f32[16,72]{1,0:T(8,128)}, u32[]{:S(2)}) copy-start(f32[16,72]{1,0:T(8,128)} %get-tuple-element.112) | copy-start | bytes 13828
  1162.7 9.6 collective-permute-start.2
  1164.0 12.4 collective-permute-start.3
  1178.2 108.5 %copy-start.41 = (bf16[1,4,2,2,72,1152]{5,4,3,2,1,0:T(8,128)(2,1)S(1)}, bf16[1,4,2,2,72,1152]{5,4,3,2,1,0:T(8,128)(2,1)}, u32[]{:S(2)}) copy-start(bf16[1,4,2,2,72,1152]{5,4,3,2,1,0:T(8,128)(2,1)} %copy-done.40) | copy-start | bytes 7962628
  1307.9 14.0 copy-start.65
  1307.9 14.0 copy-start.69
  1377.2 102.1 %copy-start.118 = (pred[7]{0:T(512)(128)(4,1)S(1)}, pred[7]{0:T(512)(128)(4,1)}, u32[]{:S(2)}) copy-start(pred[7]{0:T(512)(128)(4,1)} %iota_compare_fusion.1) | copy-start | bytes 25
  1377.2 109.9 %copy-start.104 = (bf16[4,128]{1,0:T(4,128)(2,1)S(1)}, bf16[4,128]{1,0:T(4,128)(2,1)}, u32[]{:S(2)}) copy-start(bf16[4,128]{1,0:T(4,128)(2,1)} %copy-done.103) | copy-start | bytes 3076
  1377.2 109.9 %copy-start.106 = (bf16[4,128]{1,0:T(4,128)(2,1)S(1)}, bf16[4,128]{1,0:T(4,128)(2,1)}, u32[]{:S(2)}) copy-start(bf16[4,128]{1,0:T(4,128)(2,1)} %copy-done.105) | copy-start | bytes 3076
  (99 other events, 596.7 us)
Sparse Core Ops, SparseCore 0:
  14.2 151.9 all-reduce.7
  1339.5 128.3 all-reduce.9

commit v2 on v0

--- a/solution.py
+++ b/solution.py
@@ -4,9 +4,12 @@
 import jax
 import jax.numpy as jnp
 from jax import lax
+from jax.experimental import pallas as pl
+from jax.experimental.pallas import tpu as pltpu
 from jax.sharding import PartitionSpec as P
 
 HEADS = 16
+MESH = pl.DeviceIdType.MESH
 
 
 HIGH = lax.Precision.HIGHEST
@@ -86,29 +89,6 @@
     )
 
 
-def gather_backward(shards):
-    row_parts = (
-        lax.all_gather(shards[0], "patches", axis=0, tiled=True),
-        lax.all_gather(shards[1], "patches", axis=0, tiled=True),
-        lax.all_gather(shards[2], "patches", axis=0, tiled=True),
-        lax.all_gather(shards[3], "patches", axis=0, tiled=True),
-        lax.all_gather(shards[4], "patches", axis=0, tiled=True),
-        lax.all_gather(shards[5], "patches", axis=0, tiled=True),
-        lax.all_gather(shards[6], "patches", axis=0, tiled=True),
-        lax.all_gather(shards[7], "patches", axis=0, tiled=True),
-    )
-    return (
-        lax.all_gather(row_parts[0], "frames", axis=1, tiled=True),
-        lax.all_gather(row_parts[1], "frames", axis=1, tiled=True),
-        lax.all_gather(row_parts[2], "frames", axis=1, tiled=True),
-        lax.all_gather(row_parts[3], "frames", axis=1, tiled=True),
-        lax.all_gather(row_parts[4], "frames", axis=1, tiled=True),
-        lax.all_gather(row_parts[5], "frames", axis=1, tiled=True),
-        lax.all_gather(row_parts[6], "frames", axis=1, tiled=True),
-        lax.all_gather(row_parts[7], "frames", axis=1, tiled=True),
-    )
-
-
 def self_attend(queries, keys_vals, key_mask, heads):
     frames, patches, width = queries.shape
     head_dim = width // heads
@@ -124,7 +104,7 @@
     return mixed.reshape(frames, patches, width)
 
 
-def body(
+def plain_body(
     tokens,
     cotangent,
     caption,
@@ -252,8 +232,6 @@
     mlp_res = (forward_dot(activ_r, full_mlp_out) + bias_f[6]).reshape(frames, patches, width)
     final = resid_c + gate_m * mlp_res
     block_out = jnp.where(valid[:, :, None], final, 0.0).astype(bf16)
-    weights = gather_backward(shards)
-    full_time, full_qkv, full_out, full_q, full_kv, full_cross_out, full_in, full_mlp_out = weights
     grad_final = jnp.where(valid[:, :, None], cotangent.astype(f32), 0.0)
     grad_gate_m = jnp.sum(grad_final * mlp_res, axis=0)
     grad_mlp_r = (gate_m * grad_final).astype(bf16).reshape(row_count, width)
@@ -419,6 +397,1088 @@
         biases_grad,
         hidden_total,
     )
+
+
+BF = jnp.bfloat16
+F32 = jnp.float32
+VMEM_LIMIT = 60 * 2**20
+NEG = -1e30
+IN_VMEM = pl.BlockSpec(memory_space=pltpu.VMEM)
+IN_ANY = pl.BlockSpec(memory_space=pl.ANY)
+IN_SMEM = pl.BlockSpec(memory_space=pltpu.SMEM)
+GELU_C = math.sqrt(2.0 / math.pi)
+
+
+def dot(a, b):
+    return jnp.dot(a, b, preferred_element_type=F32)
+
+
+def dot_nt(a, b):
+    return lax.dot_general(a, b, (((1,), (1,)), ((), ())), preferred_element_type=F32)
+
+
+def dot_tn(a, b):
+    return lax.dot_general(a, b, (((0,), (0,)), ((), ())), preferred_element_type=F32)
+
+
+def gelu_parts(v):
+    square = v * v
+    inner = GELU_C * (v + 0.044715 * (v * square))
+    t = jnp.tanh(inner)
+    half = 0.5 * (1.0 + t)
+    act = v * half
+    slope = half + (0.5 * GELU_C) * v * (1.0 - t * t) * (1.0 + (3 * 0.044715) * square)
+    return act, slope
+
+
+def normalise(v):
+    mean = jnp.mean(v, axis=-1, keepdims=True)
+    cen = v - mean
+    var = jnp.mean(cen * cen, axis=-1, keepdims=True)
+    rstd = lax.rsqrt(var + 1e-06)
+    return cen * rstd, rstd
+
+
+def normalise_back(xhat, rstd, g, scale):
+    h = g * (1.0 + scale)
+    a = jnp.mean(h, axis=-1, keepdims=True)
+    b = jnp.mean(h * xhat, axis=-1, keepdims=True)
+    return rstd * (h - a - xhat * b)
+
+
+def rows_at(start, size):
+    return pl.ds(pl.multiple_of(start, 16), size)
+
+
+def each(count, fn):
+    def step(i, carry):
+        fn(i)
+        return carry
+
+    lax.fori_loop(0, count, step, 0)
+
+
+def norm_body(x_ref, mods_ref, out_ref, patches):
+    def frame(s):
+        r = rows_at(s * patches, patches)
+        xhat, _ = normalise(x_ref[r, :].astype(F32))
+        out_ref[r, :] = (xhat * (1.0 + mods_ref[1]) + mods_ref[0]).astype(BF)
+
+    each(x_ref.shape[0] // patches, frame)
+
+
+def key_ok(t, per, patches, j, count, y):
+    rows = per * patches
+    row = lax.broadcasted_iota(jnp.int32, (rows, 128), 0)
+    slot = jnp.zeros((rows, 128), jnp.int32)
+    for i in range(1, per):
+        slot = slot + (row >= i * patches).astype(jnp.int32)
+    key = slot + (t * per + j - 1)
+    low = (key >= 0) | (y > 0)
+    high = (key < count) | ((key == count) & (y < 1))
+    return low & high
+
+
+def spread(p, et_ref):
+    hi = p.astype(BF)
+    lo = (p - hi.astype(F32)).astype(BF)
+    return dot(jnp.concatenate([hi, lo], axis=1), et_ref[...])
+
+
+def attend_tile(t, per, patches, count, y, scale, q_ref, kvx_ref, e_ref, et_ref, probs_ref, attn_ref):
+    rows = per * patches
+    width = q_ref.shape[1]
+    r = rows_at(t * rows, rows)
+    q = q_ref[r, :].astype(F32)
+    scores = []
+    for j in range(3):
+        kr = rows_at(t * rows + j * patches, rows)
+        s = dot((q * kvx_ref[kr, :width].astype(F32)).astype(BF), e_ref[...]) * scale
+        scores.append(jnp.where(key_ok(t, per, patches, j, count, y), s, NEG))
+    top = jnp.maximum(jnp.maximum(scores[0], scores[1]), scores[2])
+    ex = [jnp.exp(s - top) for s in scores]
+    inv = 1.0 / (ex[0] + ex[1] + ex[2])
+    total = None
+    for j in range(3):
+        p = ex[j] * inv
+        probs_ref[j, r, :] = p
+        kr = rows_at(t * rows + j * patches, rows)
+        term = spread(p, et_ref) * kvx_ref[kr, width:].astype(F32)
+        total = term if total is None else total + term
+    attn_ref[r, :] = total.astype(BF)
+
+
+def attend_tile_back(t, per, patches, scale, q_ref, kvx_ref, e_ref, et_ref, probs_ref, go_ref, gq_ref, gkv_ref):
+    rows = per * patches
+    width = q_ref.shape[1]
+    r = rows_at(t * rows, rows)
+    q = q_ref[r, :].astype(F32)
+    go = go_ref[r, :].astype(F32)
+    dps, ps = [], []
+    for j in range(3):
+        kr = rows_at(t * rows + j * patches, rows)
+        dps.append(dot((go * kvx_ref[kr, width:].astype(F32)).astype(BF), e_ref[...]))
+        ps.append(probs_ref[j, r, :])
+    mean = dps[0] * ps[0] + dps[1] * ps[1] + dps[2] * ps[2]
+    gq = None
+    for j in range(3):
+        kr = rows_at(t * rows + j * patches, rows)
+        ds = spread(ps[j] * (dps[j] - mean) * scale, et_ref)
+        term = ds * kvx_ref[kr, :width].astype(F32)
+        gq = term if gq is None else gq + term
+        gkv_ref[kr, :width] += ds * q
+        gkv_ref[kr, width:] += spread(ps[j], et_ref) * go
+    gq_ref[r, :] = gq.astype(BF)
+
+
+def head_window(h, head_dim, width):
+    return min(h * head_dim // 128 * 128, width - 256)
+
+
+def head_lanes(h, head_dim, width):
+    lane = lax.broadcasted_iota(jnp.int32, (1, 256), 1) + head_window(h, head_dim, width)
+    return (lane >= h * head_dim) & (lane < (h + 1) * head_dim)
+
+
+def cross_head(h, heads, tiles, q_ref, keys_ref, vals_ref, cmask_ref, lse_ref, mix_ref):
+    width = q_ref.shape[1]
+    head_dim = width // heads
+    scale = head_dim ** (-0.5)
+    w = head_window(h, head_dim, width)
+    keep = head_lanes(h, head_dim, width)
+    kw = jnp.where(keep, keys_ref[:, w : w + 256], 0)
+    vw = jnp.where(keep, vals_ref[:, w : w + 256], 0)
+    rows = q_ref.shape[0] // tiles
+    for i in range(tiles):
+        r = slice(i * rows, (i + 1) * rows)
+        s = dot_nt(q_ref[r, w : w + 256], kw) * scale + cmask_ref[...]
+        top = jnp.max(s, axis=-1, keepdims=True)
+        ex = jnp.exp(s - top)
+        total = jnp.sum(ex, axis=-1, keepdims=True)
+        p = (ex * (1.0 / total)).astype(BF)
+        lse_ref[r, h : h + 1] = top + jnp.log(total)
+        mix_ref[r, w : w + 256] += dot(p, vw)
+
+
+def cross_head_back(h, heads, tiles, q_ref, keys_ref, vals_ref, cmask_ref, lse_ref, gmix_ref, gq_ref, gkv_ref, p_buf, ds_buf):
+    width = q_ref.shape[1]
+    head_dim = width // heads
+    scale = head_dim ** (-0.5)
+    w = head_window(h, head_dim, width)
+    keep = head_lanes(h, head_dim, width)
+    kw = jnp.where(keep, keys_ref[:, w : w + 256], 0)
+    vw = jnp.where(keep, vals_ref[:, w : w + 256], 0)
+    rows = q_ref.shape[0] // tiles
+    for i in range(tiles):
+        r = slice(i * rows, (i + 1) * rows)
+        s = dot_nt(q_ref[r, w : w + 256], kw) * scale + cmask_ref[...]
+        p = jnp.exp(s - lse_ref[r, h : h + 1])
+        dp = dot_nt(gmix_ref[r, w : w + 256], vw)
+        ds = (p * (dp - jnp.sum(dp * p, axis=-1, keepdims=True))).astype(BF)
+        p_buf[r, :] = p.astype(BF)
+        ds_buf[r, :] = ds
+        gq_ref[r, w : w + 256] += dot(ds, kw)
+    gk = dot_tn(ds_buf[...], q_ref[:, w : w + 256]) * scale
+    gv = dot_tn(p_buf[...], gmix_ref[:, w : w + 256])
+    gkv_ref[0, :, w : w + 256] += jnp.where(keep, gk, 0.0)
+    gkv_ref[1, :, w : w + 256] += jnp.where(keep, gv, 0.0)
+
+
+class Place:
+    def __init__(self):
+        self.y=lax.axis_index("frames"); p=lax.axis_index("patches")
+        self.z=p//4; self.x=lax.rem(p//2,2); self.c=lax.rem(p,2)
+    def dev(self,y=None,z=None,x=None,c=None):
+        y=self.y if y is None else y; z=self.z if z is None else z
+        x=self.x if x is None else x; c=self.c if c is None else c
+        return (y,(z*2+x)*2+c)
+    def zoff(self,d): return lax.rem(self.z+d,4)
+
+def barrier(pos):
+    bar=pltpu.get_barrier_semaphore()
+    peers=[pos.dev(z=pos.zoff(d)) for d in (1,2,3)]+[pos.dev(x=1-pos.x),pos.dev(y=1-pos.y),pos.dev(c=1-pos.c)]
+    for t in peers: pl.semaphore_signal(bar,inc=1,device_id=t,device_id_type=MESH)
+    pl.semaphore_wait(bar,6)
+
+N_AG=9
+class Gather:
+    def __init__(self,pos,shard,full,send,recv,first):
+        self.pos=pos; self.shard=shard; self.full=full; self.send=send; self.recv=recv; self.first=first
+    def _rc(self,i,src,dst,dev):
+        return pltpu.make_async_remote_copy(src_ref=src,dst_ref=dst,send_sem=self.send.at[i],recv_sem=self.recv.at[i],device_id=dev,device_id_type=MESH)
+    def _copies(self):
+        p=self.pos; F=self.full; y,z,x,c=p.y,p.z,p.x,p.c
+        cs=[]
+        mine=F.at[y,z,x,c]
+        for d in (1,2,3):
+            cs.append(self._rc(d-1,self.shard,mine,p.dev(z=p.zoff(d))))
+        line=F.at[y,:,x,c]
+        if self.first=="x":
+            cs.append(self._rc(3,line,line,p.dev(x=1-x)))
+            plane=F.at[y,:,:,c]
+            cs.append(self._rc(4,plane,plane,p.dev(y=1-y)))
+            got1=F.at[y,:,1-x,c]; got2=F.at[1-y,:,:,c]
+        else:
+            cs.append(self._rc(3,line,line,p.dev(y=1-y)))
+            plane=F.at[:,:,x,c]
+            cs.append(self._rc(4,plane,plane,p.dev(x=1-x)))
+            got1=F.at[1-y,:,x,c]; got2=F.at[:,:,1-x,c]
+        o=p.dev(c=1-c)
+        cs.append(self._rc(5,line,line,o)); cs.append(self._rc(6,got1,got1,o)); cs.append(self._rc(7,got2,got2,o))
+        return cs
+    def start(self):
+        self.cs=self._copies()
+        p=self.pos
+        for i in (0,1,2): self.cs[i].start()
+        self.loc=pltpu.make_async_copy(self.shard,self.full.at[p.y,p.z,p.x,p.c],self.send.at[8])
+        self.loc.start()
+    def step1(self):
+        self.loc.wait()
+        for i in (0,1,2): self.cs[i].wait_recv()
+        self.cs[3].start(); self.cs[5].start()
+    def step2(self):
+        self.cs[3].wait_recv(); self.cs[4].start(); self.cs[6].start()
+    def step3(self):
+        self.cs[4].wait_recv(); self.cs[7].start()
+    def finish(self):
+        for i in (5,6,7): self.cs[i].wait_recv()
+        for i in range(8): self.cs[i].wait_send()
+
+N_RS=6
+class Scatter:
+    def __init__(self,pos,part,out,bufs,send,recv,first):
+        self.pos=pos; self.part=part; self.out=out; self.send=send; self.recv=recv; self.first=first
+        self.own,self.r1,self.r2,self.r3,self.r4=bufs
+    def _rc(self,i,src,dst,dev):
+        return pltpu.make_async_remote_copy(src_ref=src,dst_ref=dst,send_sem=self.send.at[i],recv_sem=self.recv.at[i],device_id=dev,device_id_type=MESH)
+    def start(self):
+        p=self.pos
+        self.loc=pltpu.make_async_copy(self.part.at[:,:,:,p.c],self.own,self.send.at[6])
+        self.cc=self._rc(0,self.part.at[:,:,:,1-p.c],self.r1,p.dev(c=1-p.c))
+        self.loc.start(); self.cc.start()
+    def step1(self):
+        p=self.pos; own=self.own
+        self.loc.wait(); self.cc.wait_recv()
+        def body(i,_):
+            f,r=i//8,lax.rem(i,8); z,x=r//2,lax.rem(r,2)
+            own[f,z,x]=(own[f,z,x].astype(jnp.float32)+self.r1[f,z,x].astype(jnp.float32)).astype(jnp.bfloat16)
+            return 0
+        lax.fori_loop(0,16,body,0)
+        if self.first=="y": self.c1=self._rc(1,own.at[1-p.y],self.r2,p.dev(y=1-p.y))
+        else: self.c1=self._rc(1,own.at[:,:,1-p.x],self.r2,p.dev(x=1-p.x))
+        self.c1.start()
+    def step2(self):
+        p=self.pos; own=self.own
+        self.c1.wait_recv()
+        def body(i,_):
+            if self.first=="y": f,z,x=p.y,i//2,lax.rem(i,2); a,b=z,x
+            else: f,z,x=i//4,lax.rem(i,4),p.x; a,b=f,z
+            own[f,z,x]=(own[f,z,x].astype(jnp.float32)+self.r2[a,b].astype(jnp.float32)).astype(jnp.bfloat16)
+            return 0
+        lax.fori_loop(0,8,body,0)
+        if self.first=="y": self.c2=self._rc(2,own.at[p.y,:,1-p.x],self.r3,p.dev(x=1-p.x))
+        else: self.c2=self._rc(2,own.at[1-p.y,:,p.x],self.r3,p.dev(y=1-p.y))
+        self.c2.start()
+    def step3(self):
+        p=self.pos; own=self.own
+        self.c2.wait_recv()
+        def body(z,_):
+            own[p.y,z,p.x]=(own[p.y,z,p.x].astype(jnp.float32)+self.r3[z].astype(jnp.float32)).astype(jnp.bfloat16)
+            return 0
+        lax.fori_loop(0,4,body,0)
+        self.cz=[self._rc(2+d,own.at[p.y,p.zoff(d),p.x],self.r4.at[d-1],p.dev(z=p.zoff(d))) for d in (1,2,3)]
+        for c in self.cz: c.start()
+    def step4(self):
+        p=self.pos
+        for c in self.cz: c.wait_recv()
+        f32=jnp.float32
+        self.out[...]=((self.own[p.y,p.z,p.x].astype(f32)+self.r4[0].astype(f32))+(self.r4[1].astype(f32)+self.r4[2].astype(f32)))
+    def finish(self):
+        for c in [self.cc,self.c1,self.c2]+self.cz: c.wait_send()
+def scatter_bufs(R,C,first):
+    bf=jnp.bfloat16
+    return [pltpu.VMEM((2,4,2,R,C),bf),pltpu.VMEM((2,4,2,R,C),bf),
+      pltpu.VMEM((4,2,R,C) if first=="y" else (2,4,R,C),bf),pltpu.VMEM((4,R,C),bf),pltpu.VMEM((3,R,C),bf)]
+
+
+def part_of(ref, rows, cols, lead):
+    index = [slice(None)] * lead
+    index.append(pl.ds(*rows) if rows else slice(None))
+    index.append(pl.ds(*cols) if cols else slice(None))
+    return ref.at[tuple(index)]
+
+
+def gather_kernel(units, count, *refs):
+    shards, fulls = refs[:count], refs[count : 2 * count]
+    send, recv = refs[2 * count :]
+    pos = Place()
+    barrier(pos)
+    work = [
+        Gather(
+            pos,
+            part_of(shards[a], r, c, 0),
+            part_of(fulls[a], r, c, 4),
+            send.at[k],
+            recv.at[k],
+            first,
+        )
+        for k, (a, r, c, first) in enumerate(units)
+    ]
+    for unit in work:
+        unit.start()
+    total = len(work)
+    for t in range(total + 2):
+        if t < total:
+            work[t].step1()
+        if 0 <= t - 1 < total:
+            work[t - 1].step2()
+        if 0 <= t - 2 < total:
+            work[t - 2].step3()
+    for unit in work:
+        unit.finish()
+
+
+def gather_call(shards, units, ident):
+    count = len(shards)
+    return pl.pallas_call(
+        partial(gather_kernel, units, count),
+        out_shape=[jax.ShapeDtypeStruct((2, 4, 2, 2) + s.shape, s.dtype) for s in shards],
+        in_specs=[pl.BlockSpec(memory_space=pl.ANY)] * count,
+        out_specs=[pl.BlockSpec(memory_space=pl.ANY)] * count,
+        scratch_shapes=[
+            pltpu.SemaphoreType.DMA((len(units), N_AG)),
+            pltpu.SemaphoreType.DMA((len(units), 8)),
+        ],
+        compiler_params=pltpu.CompilerParams(collective_id=ident, has_side_effects=True),
+        name="gather",
+    )(*shards)
+
+
+def scatter_kernel(units, count, *refs):
+    parts, outs = refs[:count], refs[count : 2 * count]
+    rest = refs[2 * count :]
+    send, recv = rest[-2:]
+    pos = Place()
+    barrier(pos)
+    work = [
+        Scatter(
+            pos,
+            part_of(parts[a], r, c, 4),
+            part_of(outs[a], r, c, 0),
+            rest[5 * k : 5 * k + 5],
+            send.at[k],
+            recv.at[k],
+            first,
+        )
+        for k, (a, r, c, first) in enumerate(units)
+    ]
+    total = len(work)
+    for unit in work:
+        unit.start()
+    for t in range(total + 3):
+        if t < total:
+            work[t].step1()
+        if 0 <= t - 1 < total:
+            work[t - 1].step2()
+        if 0 <= t - 2 < total:
+            work[t - 2].step3()
+        if 0 <= t - 3 < total:
+            work[t - 3].step4()
+    for unit in work:
+        unit.finish()
+
+
+def scatter_call(parts, units, ident):
+    count = len(parts)
+    scratch = []
+    for a, r, c, first in units:
+        rows, cols = parts[a].shape[-2:]
+        scratch += scatter_bufs(r[1] if r else rows, c[1] if c else cols, first)
+    return pl.pallas_call(
+        partial(scatter_kernel, units, count),
+        out_shape=[jax.ShapeDtypeStruct(p.shape[-2:], jnp.float32) for p in parts],
+        in_specs=[pl.BlockSpec(memory_space=pl.ANY)] * count,
+        out_specs=[pl.BlockSpec(memory_space=pltpu.VMEM)] * count,
+        scratch_shapes=scratch
+        + [
+            pltpu.SemaphoreType.DMA((len(units), 7)),
+            pltpu.SemaphoreType.DMA((len(units), N_RS)),
+        ],
+        compiler_params=pltpu.CompilerParams(
+            collective_id=ident, has_side_effects=True, vmem_limit_bytes=60 * 2**20
+        ),
+        name="scatter",
+    )(*parts)
+
+
+def attend_kernel(
+    patches, heads, nm_ref, x_ref, mods_ref, w1_ref, w2_ref, qb_ref, ob_ref, e_ref, et_ref, info_ref,
+    wqkv_ref, wo_ref, q_ref, kvx_ref, probs_ref, attn_ref, ao_ref, resid_ref, residb_ref,
+    w1_buf, w2_buf, wqkv_buf, wo_buf, halo_out, halo_in, sems, send, recv,
+):
+    pos = Place()
+    rows, width = x_ref.shape
+    frames = rows // patches
+    count, y = info_ref[0], info_ref[1]
+    loads = (
+        pltpu.make_async_copy(w1_ref, w1_buf, sems.at[0]),
+        pltpu.make_async_copy(w2_ref, w2_buf, sems.at[1]),
+    )
+    for c in loads:
+        c.start()
+    pair_barrier(pos)
+    cut = 3 * width // 2
+    half = width // 2
+    loads[0].wait()
+    for f in range(2):
+        wqkv_buf[:, f * cut : (f + 1) * cut] = w1_buf[f, :, :cut]
+    loads[1].wait()
+    for f in range(2):
+        wo_buf[:, f * half : (f + 1) * half] = w2_buf[f, :, :half]
+    keep = (
+        pltpu.make_async_copy(wqkv_buf, wqkv_ref, sems.at[2]),
+        pltpu.make_async_copy(wo_buf, wo_ref, sems.at[3]),
+    )
+    for c in keep:
+        c.start()
+    zero = jnp.zeros((patches, 2 * width), BF)
+    kvx_ref[0:patches, :] = zero
+    kvx_ref[(frames + 1) * patches :, :] = zero
+    own = slice(patches, (frames + 1) * patches)
+    for third in (1, 2, 0):
+        cols = slice(third * width, (third + 1) * width)
+        got = (dot(nm_ref[...], wqkv_buf[:, cols]) + qb_ref[:, cols]).astype(BF)
+        if third == 0:
+            q_ref[...] = got
+        else:
+            kvx_ref[own, (third - 1) * width : third * width] = got
+        if third == 2:
+            copy = halo_send(pos, frames, patches, count, y, kvx_ref, halo_out, halo_in, send, recv)
+    copy.wait()
+    place = jnp.where(y == 0, count, -1) + 1
+
+    def settle(s):
+        r = rows_at(s * patches, patches)
+        hit = jnp.full((patches, 2 * width), (s == place).astype(F32), F32)
+        kvx_ref[r, :] = jnp.where(hit > 0.5, halo_in[...].astype(F32), kvx_ref[r, :].astype(F32)).astype(BF)
+
+    each(frames + 2, settle)
+    scale = (width // heads) ** (-0.5)
+    each(
+        frames // 3,
+        lambda t: attend_tile(t, 3, patches, count, y, scale, q_ref, kvx_ref, e_ref, et_ref, probs_ref, attn_ref),
+    )
+    resid_ref[...] = dot(attn_ref[...], wo_buf[...]) + ob_ref[...]
+
+    def frame(s):
+        r = rows_at(s * patches, patches)
+        ao = resid_ref[r, :]
+        ao_ref[r, :] = ao.astype(BF)
+        resid = x_ref[r, :].astype(F32) + mods_ref[2] * ao
+        resid_ref[r, :] = resid
+        residb_ref[r, :] = resid.astype(BF)
+
+    each(frames, frame)
+    for c in keep:
+        c.wait()
+
+
+def pair_barrier(pos):
+    bar = pltpu.get_barrier_semaphore()
+    pl.semaphore_signal(bar, inc=1, device_id=pos.dev(y=1 - pos.y), device_id_type=MESH)
+    pl.semaphore_wait(bar, 1)
+
+
+def pick_slot(frames, patches, slot, src_ref, dst_ref):
+    dst_ref[...] = jnp.zeros(dst_ref.shape, dst_ref.dtype)
+
+    def step(s):
+        r = rows_at(s * patches, patches)
+        hit = jnp.full(dst_ref.shape, (s == slot).astype(F32), F32)
+        dst_ref[...] = jnp.where(hit > 0.5, src_ref[r, :].astype(F32), dst_ref[...].astype(F32)).astype(dst_ref.dtype)
+
+    each(frames, step)
+
+
+def halo_send(pos, frames, patches, count, y, kvx_ref, halo_out, halo_in, send, recv):
+    pick_slot(frames + 2, patches, jnp.where(y == 0, count - 1, 0) + 1, kvx_ref, halo_out)
+    copy = pltpu.make_async_remote_copy(
+        src_ref=halo_out, dst_ref=halo_in, send_sem=send, recv_sem=recv,
+        device_id=pos.dev(y=1 - pos.y), device_id_type=MESH,
+    )
+    copy.start()
+    return copy
+
+
+def attend_call(patches, heads, nm, x, mods, w1, w2, qb, ob, e, et, info, ident):
+    rows, width = x.shape
+    frames = rows // patches
+    ext = (frames + 2) * patches
+    S = jax.ShapeDtypeStruct
+    return pl.pallas_call(
+        partial(attend_kernel, patches, heads),
+        out_shape=[
+            S((width, 3 * width), BF), S((width, width), BF), S((rows, width), BF), S((ext, 2 * width), BF),
+            S((3, rows, 128), F32), S((rows, width), BF), S((rows, width), BF), S((rows, width), F32), S((rows, width), BF),
+        ],
+        in_specs=[IN_VMEM] * 3 + [IN_ANY] * 2 + [IN_VMEM] * 4 + [IN_SMEM],
+        out_specs=[IN_ANY] * 2 + [IN_VMEM] * 7,
+        scratch_shapes=[
+            pltpu.VMEM(w1.shape, BF), pltpu.VMEM(w2.shape, BF), pltpu.VMEM((width, 3 * width), BF), pltpu.VMEM((width, width), BF),
+            pltpu.VMEM((patches, 2 * width), BF), pltpu.VMEM((patches, 2 * width), BF),
+            pltpu.SemaphoreType.DMA((4,)), pltpu.SemaphoreType.DMA, pltpu.SemaphoreType.DMA,
+        ],
+        compiler_params=pltpu.CompilerParams(collective_id=ident, has_side_effects=True, vmem_limit_bytes=VMEM_LIMIT),
+        name="attend",
+    )(nm, x, mods, w1, w2, qb, ob, e, et, info)
+
+
+def norm_call(patches, x, mods):
+    return pl.pallas_call(
+        lambda x_ref, m_ref, o_ref: norm_body(x_ref, m_ref, o_ref, patches),
+        out_shape=jax.ShapeDtypeStruct(x.shape, BF), in_specs=[IN_VMEM] * 2, out_specs=IN_VMEM, name="norm",
+    )(x, mods)
+
+
+def cross_kernel(
+    patches, heads, resid_ref, residb_ref, mods_ref, used_ref, cm_ref, w2_ref, w3_ref, kv_ref, b3_ref, b4_ref, b5_ref,
+    wq_ref, wco_ref, q_ref, keys_ref, vals_ref, lse_ref, mixb_ref, rc_ref, nm_ref,
+    w2_buf, w3_buf, kv_buf, wq_buf, wco_buf, mix_buf, cmask, sems,
+):
+    rows, width = resid_ref.shape
+    frames = rows // patches
+    half = width // 2
+    loads = (
+        pltpu.make_async_copy(kv_ref, kv_buf, sems.at[0]),
+        pltpu.make_async_copy(w2_ref, w2_buf, sems.at[1]),
+        pltpu.make_async_copy(w3_ref, w3_buf, sems.at[4]),
+    )
+    for c in loads:
+        c.start()
+    for i in range(3):
+        cmask[i * patches : (i + 1) * patches, :] = cm_ref[...]
+    mix_buf[...] = jnp.zeros(mix_buf.shape, F32)
+    loads[0].wait()
+    keys_ref[...] = dot(used_ref[...], kv_buf[0]).astype(BF)
+    vals_ref[...] = (dot(used_ref[...], kv_buf[1]) + b4_ref[...]).astype(BF)
+    loads[1].wait()
+    loads[2].wait()
+    for f in range(2):
+        wq_buf[:, f * half : (f + 1) * half] = w2_buf[f]
+        wco_buf[:, f * half : (f + 1) * half] = w3_buf[f]
+    keep = (
+        pltpu.make_async_copy(wq_buf, wq_ref, sems.at[2]),
+        pltpu.make_async_copy(wco_buf, wco_ref, sems.at[3]),
+    )
+    for c in keep:
+        c.start()
+    q_ref[...] = (dot(residb_ref[...], wq_buf[...]) + b3_ref[...]).astype(BF)
+    for h in range(heads):
+        cross_head(h, heads, rows // cmask.shape[0], q_ref, keys_ref, vals_ref, cmask, lse_ref, mix_buf)
+    mixb_ref[...] = mix_buf[...].astype(BF)
+    rc_ref[...] = dot(mixb_ref[...], wco_buf[...]) + b5_ref[...]
+
+    def frame(s):
+        r = rows_at(s * patches, patches)
+        rc = rc_ref[r, :] + resid_ref[r, :]
+        rc_ref[r, :] = rc
+        xhat, _ = normalise(rc)
+        nm_ref[r, :] = (xhat * (1.0 + mods_ref[4]) + mods_ref[3]).astype(BF)
+
+    each(frames, frame)
+    for c in keep:
+        c.wait()
+
+
+def cross_call(patches, heads, resid, residb, mods, used, cm, w2, w3, kv, b3, b4, b5):
+    rows, width = resid.shape
+    caps = used.shape[0]
+    S = jax.ShapeDtypeStruct
+    return pl.pallas_call(
+        partial(cross_kernel, patches, heads),
+        out_shape=[
+            S((width, width), BF), S((width, width), BF), S((rows, width), BF), S((caps, width), BF), S((caps, width), BF),
+            S((rows, 128), F32), S((rows, width), BF), S((rows, width), F32), S((rows, width), BF),
+        ],
+        in_specs=[IN_VMEM] * 5 + [IN_ANY] * 3 + [IN_VMEM] * 3,
+        out_specs=[IN_ANY] * 2 + [IN_VMEM] * 7,
+        scratch_shapes=[
+            pltpu.VMEM(w2.shape, BF), pltpu.VMEM(w3.shape, BF), pltpu.VMEM(kv.shape, BF), pltpu.VMEM((width, width), BF), pltpu.VMEM((width, width), BF),
+            pltpu.VMEM((rows, width), F32), pltpu.VMEM((3 * patches, caps), F32), pltpu.SemaphoreType.DMA((5,)),
+        ],
+        compiler_params=pltpu.CompilerParams(vmem_limit_bytes=VMEM_LIMIT),
+        name="cross",
+    )(resid, residb, mods, used, cm, w2, w3, kv, b3, b4, b5)
+
+
+def mlp_kernel(
+    chunk, patches, nm_ref, cot_ref, valid_ref, rc_ref, mods_ref, hb_ref, b6_ref, win_ref, wout_ref,
+    out_ref, grc_ref, hsum_ref, bsum_ref, gp_ref, dwin_ref, dwout_ref,
+    gm_ref, res_ref, win_b, wout_h, wout_b, act_b, gpre_b, din_s, dout_s, in_sem, out_sem,
+):
+    rows, width = nm_ref.shape
+    frames = rows // patches
+    half = wout_ref.shape[2]
+    per = win_ref.shape[2] // chunk
+    total = 2 * per
+
+    def loads(j, slot):
+        f, u = j // per, lax.rem(j, per)
+        cols = pl.ds(pl.multiple_of(u * chunk, 128), chunk)
+        rws = pl.ds(pl.multiple_of(j * chunk, 128), chunk)
+        return (
+            pltpu.make_async_copy(win_ref.at[f, :, cols], win_b.at[slot], in_sem.at[slot, 0]),
+            pltpu.make_async_copy(wout_ref.at[:, rws], wout_h.at[slot], in_sem.at[slot, 1]),
+        )
+
+    def stores(j, slot):
+        f, u = j // per, lax.rem(j, per)
+        cols = pl.ds(pl.multiple_of(u * chunk, 128), chunk)
+        rws = pl.ds(pl.multiple_of(j * chunk, 128), chunk)
+        return (
+            pltpu.make_async_copy(din_s.at[slot], dwin_ref.at[f, :, cols], out_sem.at[slot, 0]),
+            pltpu.make_async_copy(dout_s.at[slot], dwout_ref.at[:, rws], out_sem.at[slot, 1]),
+        )
+
+    for c in loads(0, 0):
+        c.start()
+    bsum_ref[...] = jnp.zeros(bsum_ref.shape, F32)
+    gp_ref[...] = jnp.zeros(gp_ref.shape, F32)
+
+    def prepare(s):
+        r = rows_at(s * patches, patches)
+        gf = jnp.where(valid_ref[r, :] > 0.5, cot_ref[r, :].astype(F32), 0.0)
+        gm = (mods_ref[5] * gf).astype(BF)
+        gm_ref[r, :] = gm
+        bsum_ref[0:1, :] += jnp.sum(gm.astype(F32), axis=0, keepdims=True)
+
+    each(frames, prepare)
+
+    def step(j, carry):
+        slot = lax.rem(j, 2)
+        for c in loads(j, slot):
+            c.wait()
+
+        @pl.when(j + 1 < total)
+        def _():
+            for c in loads(j + 1, 1 - slot):
+                c.start()
+
+        @pl.when(j >= 2)
+        def _():
+            for c in stores(j - 2, slot):
+                c.wait()
+
+        wout_b[...] = jnp.concatenate([wout_h[slot, 0], wout_h[slot, 1]], axis=1)
+        pre = dot(nm_ref[...], win_b[slot]) + hb_ref[pl.ds(j, 1), :]
+        act, slope = gelu_parts(pre)
+        act_b[...] = act.astype(BF)
+        gpre = (dot_nt(gm_ref[...], wout_b[...]) * slope).astype(BF)
+        gpre_b[...] = gpre
+        hsum_ref[pl.ds(j, 1), :] = jnp.sum(gpre.astype(F32), axis=0, keepdims=True)
+        part = dot(act_b[...], wout_b[...])
+        back = dot_nt(gpre_b[...], win_b[slot])
+
+        @pl.when(j == 0)
+        def _():
+            res_ref[...] = part
+            grc_ref[...] = back
+
+        @pl.when(j > 0)
+        def _():
+            res_ref[...] += part
+            grc_ref[...] += back
+
+        din_s[slot] = dot_tn(nm_ref[...], gpre_b[...]).astype(BF)
+        d = dot_tn(act_b[...], gm_ref[...]).astype(BF)
+        dout_s[slot, 0] = d[:, :half]
+        dout_s[slot, 1] = d[:, half:]
+        for c in stores(j, slot):
+            c.start()
+        return carry
+
+    lax.fori_loop(0, total, step, 0)
+
+    def finish(s):
+        r = rows_at(s * patches, patches)
+        ok = valid_ref[r, :] > 0.5
+        rc = rc_ref[r, :]
+        res = res_ref[r, :] + b6_ref[...]
+        gf = jnp.where(ok, cot_ref[r, :].astype(F32), 0.0)
+        out_ref[r, :] = jnp.where(ok, rc + mods_ref[5] * res, 0.0).astype(BF)
+        xhat, rstd = normalise(rc)
+        g = grc_ref[r, :]
+        gp_ref[0] += g
+        gp_ref[1] += g * xhat
+        gp_ref[2] += gf * res
+        grc_ref[r, :] = gf + normalise_back(xhat, rstd, g, mods_ref[4])
+
+    each(frames, finish)
+    for back in (2, 1):
+        for c in stores(total - back, (total - back) % 2):
+            c.wait()
+
+
+def mlp_call(patches, nm, cot, valid, rc, mods, hb, b6, win, wout):
+    rows, width = nm.shape
+    chunk = 768
+    total = 2 * win.shape[2] // chunk
+    half = wout.shape[2]
+    S = jax.ShapeDtypeStruct
+    return pl.pallas_call(
+        partial(mlp_kernel, chunk, patches),
+        out_shape=[
+            S((rows, width), BF), S((rows, width), F32), S((total, chunk), F32), S((8, width), F32), S((3, patches, width), F32),
+            S(win.shape, BF), S(wout.shape, BF),
+        ],
+        in_specs=[IN_VMEM] * 7 + [IN_ANY] * 2,
+        out_specs=[IN_VMEM] * 5 + [IN_ANY] * 2,
+        scratch_shapes=[
+            pltpu.VMEM((rows, width), BF), pltpu.VMEM((rows, width), F32),
+            pltpu.VMEM((2, width, chunk), BF), pltpu.VMEM((2, 2, chunk, half), BF), pltpu.VMEM((chunk, width), BF),
+            pltpu.VMEM((rows, chunk), BF), pltpu.VMEM((rows, chunk), BF),
+            pltpu.VMEM((2, width, chunk), BF), pltpu.VMEM((2, 2, chunk, half), BF),
+            pltpu.SemaphoreType.DMA((2, 2)), pltpu.SemaphoreType.DMA((2, 2)),
+        ],
+        compiler_params=pltpu.CompilerParams(vmem_limit_bytes=VMEM_LIMIT),
+        name="mlp",
+    )(nm, cot, valid, rc, mods, hb.reshape(total, chunk), b6, win, wout)
+
+
+def cross_back_kernel(
+    patches, heads, grc_ref, mixb_ref, q_ref, keys_ref, vals_ref, lse_ref, cm_ref, residb_ref, attn_ref, ao_ref, gate_ref,
+    wco_ref, wq_ref, wo_ref,
+    gra_ref, gai_ref, gkvb_ref, bsum_ref, gp_ref, dwo_ref, dwq_ref, dwco_ref,
+    w_buf, gcb, gmix, gq, gkv, p_buf, ds_buf, cmask, dw_s, sems, out_sem,
+):
+    rows, width = grc_ref.shape
+    frames = rows // patches
+    half = width // 2
+    scale = (width // heads) ** (-0.5)
+    loads = [pltpu.make_async_copy(src, w_buf, sems.at[i]) for i, src in enumerate((wco_ref, wq_ref, wo_ref))]
+    outs = [pltpu.make_async_copy(dw_s.at[i % 2], dst, out_sem.at[i]) for i, dst in enumerate((dwco_ref, dwq_ref, dwo_ref))]
+    loads[0].start()
+    for i in range(3):
+        cmask[i * patches : (i + 1) * patches, :] = cm_ref[...]
+    bsum_ref[...] = jnp.zeros(bsum_ref.shape, F32)
+    gp_ref[...] = jnp.zeros(gp_ref.shape, F32)
+    gkv[...] = jnp.zeros(gkv.shape, F32)
+    gq[...] = jnp.zeros(gq.shape, F32)
+
+    def first(s):
+        r = rows_at(s * patches, patches)
+        g = grc_ref[r, :].astype(BF)
+        gcb[r, :] = g
+        bsum_ref[0:1, :] += jnp.sum(g.astype(F32), axis=0, keepdims=True)
+
+    each(frames, first)
+    loads[0].wait()
+    gmix[...] = dot_nt(gcb[...], w_buf[...]).astype(BF)
+    loads[1].start()
+
+    def weight_grad(k, left, right):
+        d = dot_tn(left, right).astype(BF)
+        for f in range(2):
+            dw_s[k % 2, f] = d[:, f * half : (f + 1) * half]
+        outs[k].start()
+
+    weight_grad(0, mixb_ref[...], gcb[...])
+    for h in range(heads):
+        cross_head_back(
+            h, heads, rows // cmask.shape[0], q_ref, keys_ref, vals_ref, cmask, lse_ref, gmix, gq, gkv, p_buf, ds_buf
+        )
+    gkvb_ref[...] = gkv[...].astype(BF)
+
+    def second(s):
+        r = rows_at(s * patches, patches)
+        g = (gq[r, :] * scale).astype(BF)
+        gcb[r, :] = g
+        bsum_ref[1:2, :] += jnp.sum(g.astype(F32), axis=0, keepdims=True)
+
+    each(frames, second)
+    weight_grad(1, residb_ref[...], gcb[...])
+    loads[1].wait()
+    gra_ref[...] = dot_nt(gcb[...], w_buf[...])
+    loads[2].start()
+
+    def third(s):
+        r = rows_at(s * patches, patches)
+        gra = gra_ref[r, :] + grc_ref[r, :]
+        gra_ref[r, :] = gra
+        gp_ref[...] += gra * ao_ref[r, :].astype(F32)
+        g = (gate_ref[...] * gra).astype(BF)
+        gmix[r, :] = g
+        bsum_ref[2:3, :] += jnp.sum(g.astype(F32), axis=0, keepdims=True)
+
+    each(frames, third)
+    loads[2].wait()
+    gai_ref[...] = dot_nt(gmix[...], w_buf[...]).astype(BF)
+    outs[0].wait()
+    weight_grad(2, attn_ref[...], gmix[...])
+    outs[1].wait()
+    outs[2].wait()
+
+
+def cross_back_call(patches, heads, grc, mixb, q, keys, vals, lse, cm, residb, attn, ao, gate, wco, wq, wo):
+    rows, width = grc.shape
+    caps = keys.shape[0]
+    S = jax.ShapeDtypeStruct
+    return pl.pallas_call(
+        partial(cross_back_kernel, patches, heads),
+        out_shape=[
+            S((rows, width), F32), S((rows, width), BF), S((2, caps, width), BF), S((8, width), F32), S((patches, width), F32),
+        ]
+        + [S((2, width, width // 2), BF)] * 3,
+        in_specs=[IN_VMEM] * 11 + [IN_ANY] * 3,
+        out_specs=[IN_VMEM] * 5 + [IN_ANY] * 3,
+        scratch_shapes=[
+            pltpu.VMEM((width, width), BF), pltpu.VMEM((rows, width), BF), pltpu.VMEM((rows, width), BF),
+            pltpu.VMEM((rows, width), F32), pltpu.VMEM((2, caps, width), F32),
+            pltpu.VMEM((rows, caps), BF), pltpu.VMEM((rows, caps), BF), pltpu.VMEM((3 * patches, caps), F32),
+            pltpu.VMEM((2, 2, width, width // 2), BF),
+            pltpu.SemaphoreType.DMA((3,)), pltpu.SemaphoreType.DMA((3,)),
+        ],
+        compiler_params=pltpu.CompilerParams(vmem_limit_bytes=VMEM_LIMIT),
+        name="cross_back",
+    )(grc, mixb, q, keys, vals, lse, cm, residb, attn, ao, gate, wco, wq, wo)
+
+
+def attend_back_kernel(
+    patches, heads, gai_ref, q_ref, kvx_ref, probs_ref, e_ref, et_ref, info_ref, nm_ref, x_ref, scale_ref, gra_ref, wqkv_ref,
+    ig_ref, bsum_ref, gp_ref, dw_ref,
+    w_buf, gqb, gkb, gvb, gkv, halo_out, halo_in, dw_s, sems, send, recv,
+):
+    pos = Place()
+    rows, width = x_ref.shape
+    frames = rows // patches
+    half = width // 2
+    count, y = info_ref[0], info_ref[1]
+    load = pltpu.make_async_copy(wqkv_ref, w_buf, sems.at[0])
+    load.start()
+    pair_barrier(pos)
+    gkv[...] = jnp.zeros(gkv.shape, F32)
+    scale = (width // heads) ** (-0.5)
+    each(
+        frames // 3,
+        lambda t: attend_tile_back(t, 3, patches, scale, q_ref, kvx_ref, e_ref, et_ref, probs_ref, gai_ref, gqb, gkv),
+    )
+    place = jnp.where(y == 0, count, -1) + 1
+    pick_slot(frames + 2, patches, place, gkv, halo_out)
+    copy = pltpu.make_async_remote_copy(
+        src_ref=halo_out, dst_ref=halo_in, send_sem=send, recv_sem=recv,
+        device_id=pos.dev(y=1 - pos.y), device_id_type=MESH,
+    )
+    copy.start()
+    bsum_ref[...] = jnp.zeros(bsum_ref.shape, F32)
+    gp_ref[...] = jnp.zeros(gp_ref.shape, F32)
+    dw_s[:, :width] = dot_tn(nm_ref[...], gqb[...]).astype(BF)
+    load.wait()
+    ig_ref[...] = dot_nt(gqb[...], w_buf[:, :width])
+    copy.wait()
+    mine = jnp.where(y == 0, count - 1, 0) + 1
+
+    def settle(s):
+        r = rows_at((s + 1) * patches, patches)
+        o = rows_at(s * patches, patches)
+        shape = (patches, 2 * width)
+        drop = jnp.full(shape, (s + 1 == place).astype(F32), F32)
+        add = jnp.full(shape, (s + 1 == mine).astype(F32), F32)
+        g = jnp.where(drop > 0.5, 0.0, gkv[r, :]) + jnp.where(add > 0.5, halo_in[...].astype(F32), 0.0)
+        g = g.astype(BF)
+        gkb[o, :] = g[:, :width]
+        gvb[o, :] = g[:, width:]
+        bsum_ref[0:1, :] += jnp.sum(gqb[o, :].astype(F32), axis=0, keepdims=True)
+        bsum_ref[1:2, :] += jnp.sum(g[:, width:].astype(F32), axis=0, keepdims=True)
+
+    each(frames, settle)
+    late = pltpu.make_async_copy(gra_ref, gkv.at[pl.ds(0, rows), pl.ds(0, width)], sems.at[2])
+    late.start()
+    dw_s[:, width:] = dot_tn(nm_ref[...], gkb[:, :half]).astype(BF)
+    out = [pltpu.make_async_copy(dw_s, dw_ref.at[f], sems.at[1]) for f in range(2)]
+    out[0].start()
+    ig_ref[...] += dot_nt(gkb[...], w_buf[:, width : 2 * width])
+    ig_ref[...] += dot_nt(gvb[...], w_buf[:, 2 * width :])
+    out[0].wait()
+    dw_s[:, :half] = dot_tn(nm_ref[...], gkb[:, half:]).astype(BF)
+    dw_s[:, half:] = dot_tn(nm_ref[...], gvb[...]).astype(BF)
+    out[1].start()
+    late.wait()
+
+    def finish(s):
+        r = rows_at(s * patches, patches)
+        xhat, rstd = normalise(x_ref[r, :].astype(F32))
+        g = ig_ref[r, :]
+        gp_ref[0] += g
+        gp_ref[1] += g * xhat
+        ig_ref[r, :] = gkv[r, :width] + normalise_back(xhat, rstd, g, scale_ref[...])
+
+    each(frames, finish)
+    out[1].wait()
+
+
+def attend_back_call(patches, heads, gai, q, kvx, probs, e, et, info, nm, x, scale, gra, wqkv, ident):
+    cols = 3 * x.shape[1] // 2
+    rows, width = x.shape
+    S = jax.ShapeDtypeStruct
+    return pl.pallas_call(
+        partial(attend_back_kernel, patches, heads),
+        out_shape=[S((rows, width), F32), S((8, width), F32), S((2, patches, width), F32), S((2, width, cols), BF)],
+        in_specs=[IN_VMEM] * 6 + [IN_SMEM] + [IN_VMEM] * 3 + [IN_ANY] * 2,
+        out_specs=[IN_VMEM] * 3 + [IN_ANY],
+        scratch_shapes=[
+            pltpu.VMEM(wqkv.shape, BF), pltpu.VMEM((rows, width), BF), pltpu.VMEM((rows, width), BF), pltpu.VMEM((rows, width), BF),
+            pltpu.VMEM(kvx.shape, F32), pltpu.VMEM((patches, 2 * width), BF), pltpu.VMEM((patches, 2 * width), BF),
+            pltpu.VMEM((width, cols), BF),
+            pltpu.SemaphoreType.DMA((3,)), pltpu.SemaphoreType.DMA, pltpu.SemaphoreType.DMA,
+        ],
+        compiler_params=pltpu.CompilerParams(collective_id=ident, has_side_effects=True, vmem_limit_bytes=VMEM_LIMIT),
+        name="attend_back",
+    )(gai, q, kvx, probs, e, et, info, nm, x, scale, gra, wqkv)
+
+
+UNITS_ALL = (
+    (0, None, (0, 896), "x"),
+    (0, None, (896, 832), "y"),
+    (1, None, None, "x"),
+    (2, None, None, "y"),
+    (3, None, None, "x"),
+    (4, None, None, "y"),
+    (5, None, (0, 1152), "x"),
+    (5, None, (1152, 1152), "y"),
+    (6, (0, 144), None, "x"),
+    (6, (144, 144), None, "y"),
+)
+
+
+def fast_body(
+    tokens, cotangent, caption, null_embed, timesteps, null_mask, bucket_sizes, patch_mask, frame_counts, table, time_proj,
+    self_qkv, self_out, cross_q, cross_kv, cross_out, mlp_in, mlp_out, biases, hidden_bias,
+):
+    frames, patches, width = tokens.shape
+    heads = HEADS
+    head_dim = width // heads
+    clips, cap_len, _ = caption.shape
+    cap_pad = -(-cap_len // 128) * 128
+    rows = frames * patches
+    count = frame_counts[0]
+    frame_index = lax.axis_index("frames")
+    patch_index = lax.axis_index("patches")
+    bias_f = biases.astype(F32)
+    patch_ids = patch_index * patches + jnp.arange(patches, dtype=jnp.int32)
+    bucket_ends = jnp.cumsum(bucket_sizes)
+    clip_ids = jnp.sum((patch_ids[:, None] >= bucket_ends[None, :]).astype(jnp.int32), axis=1)
+    onehot = (clip_ids[:, None] == jnp.arange(clips, dtype=jnp.int32)[None, :]).astype(F32)
+    valid = (jnp.arange(frames, dtype=jnp.int32) < count)[:, None] & (patch_mask[None, :] == 1)
+    valid = valid.reshape(rows, 1).astype(F32)
+    time_rows, time_cols = time_proj.shape
+    features = time_features(timesteps, time_rows * lax.axis_size("patches")).astype(BF)
+    own_features = lax.dynamic_slice_in_dim(features, patch_index * time_rows, time_rows, 1)
+    time_part = lax.dynamic_update_slice(
+        jnp.zeros((clips, 6 * width), F32), forward_dot(own_features, time_proj), (0, frame_index * time_cols)
+    )
+    time_sum = lax.psum(time_part, ("frames", "patches"))
+    modulation = table.astype(F32) + time_sum.reshape(clips, 6, width)
+    mods = jnp.einsum("pc,ckd->kpd", onehot, modulation, precision=HIGH)
+    used = jnp.where(null_mask[:, None, None] == 1, null_embed[None], caption)
+    used = jnp.pad(used, ((0, 0), (0, cap_pad - cap_len), (0, 0))).reshape(clips * cap_pad, width)
+    key_ids = jnp.arange(clips * cap_pad, dtype=jnp.int32)
+    open_key = (clip_ids[:, None] == (key_ids // cap_pad)[None, :]) & (key_ids % cap_pad < cap_len)[None, :]
+    cmask = jnp.where(open_key, 0.0, NEG)
+    lanes = jnp.arange(width, dtype=jnp.int32)[:, None] // head_dim
+    e = (lanes == jnp.arange(128, dtype=jnp.int32)[None, :]).astype(BF)
+    et = jnp.concatenate([e.T, e.T], axis=0)
+    info = jnp.stack([count, frame_index]).astype(jnp.int32)
+    qkv_bias = jnp.concatenate([bias_f[0], jnp.zeros((width,), F32), bias_f[1]])[None]
+
+    got = gather_call([self_qkv, self_out, cross_q, cross_out, cross_kv, mlp_in, mlp_out], UNITS_ALL, 0)
+    w_qkv, w_out, w_q, w_co, w_kv, w_in, w_mo = [g.reshape(2, -1, g.shape[-1]) for g in got]
+    x = tokens.reshape(rows, width)
+    cot = cotangent.reshape(rows, width)
+    nm_a = norm_call(patches, x, mods)
+    wqkv, wo, q, kvx, probs, attn, ao, resid, residb = attend_call(
+        patches, heads, nm_a, x, mods, w_qkv, w_out, qkv_bias, bias_f[2:3], e, et, info, 3
+    )
+    wq, wco, cq, keys, vals, lse, mixb, rc, nm_m = cross_call(
+        patches, heads, resid, residb, mods, used, cmask, w_q, w_co, w_kv, bias_f[3:4], bias_f[4:5], bias_f[5:6]
+    )
+    block_out, grc, hsum, bsum_m, gp_m, dw_in, dw_mo = mlp_call(
+        patches, nm_m, cot, valid, rc, mods, hidden_bias.astype(F32), bias_f[6:7], w_in, w_mo
+    )
+    gra, gai, gkv, bsum_c, gp_g, dwo, dwq, dwco = cross_back_call(
+        patches, heads, grc, mixb, cq, keys, vals, lse, cmask, residb, attn, ao, mods[2], wco, wq, wo
+    )
+    input_grad, bsum_a, gp_a, dwqkv = attend_back_call(
+        patches, heads, gai, q, kvx, probs, e, et, info, nm_a, x, mods[1], gra, wqkv, 4
+    )
+    per_patch = jnp.stack([gp_a[0], gp_a[1], gp_g, gp_m[0], gp_m[1], gp_m[2]], axis=1)
+    mod_part = jnp.einsum("pc,pkd->ckd", onehot, per_patch, precision=HIGH)
+    bias_part = jnp.stack(
+        [bsum_a[0], bsum_a[1], bsum_c[2], bsum_c[1], jnp.zeros((width,), F32), bsum_c[0], bsum_m[0]]
+    )
+    kv_total, bias_total, hidden_total, mod_total = lax.psum(
+        (gkv.astype(F32), bias_part, hsum.reshape(-1), mod_part), ("frames", "patches")
+    )
+    kv_low = kv_total.astype(BF)
+    bias_cv = jnp.sum(kv_low[1].astype(F32), axis=0)
+    biases_grad = bias_total.at[4].add(bias_cv)
+    own_used = lax.dynamic_slice_in_dim(used, patch_index * cross_kv.shape[0], cross_kv.shape[0], 1)
+    cross_kv_grad = outer_sum(own_used, kv_low[frame_index])
+    caption_rows = times_transposed(kv_low[0], w_kv[0]) + times_transposed(kv_low[1], w_kv[1])
+    caption_rows = caption_rows.reshape(clips, cap_pad, width)[:, :cap_len]
+    dropped = (null_mask == 1)[:, None, None]
+    caption_grad = jnp.where(dropped, 0.0, caption_rows)
+    null_grad = jnp.sum(jnp.where(dropped, caption_rows, 0.0), axis=0)
+    table_grad = jnp.sum(mod_total, axis=0)
+    own_mod = lax.dynamic_slice_in_dim(mod_total.reshape(clips, 6 * width), frame_index * time_cols, time_cols, 1)
+    time_proj_grad = jnp.dot(own_features.astype(F32).T, own_mod, precision=HIGH)
+
+    def blocks(part, shard):
+        return part.reshape((2, 4, 2, 2) + shard.shape)
+
+    in_shard, mo_shard = scatter_call(
+        [blocks(dw_in, mlp_in), blocks(dw_mo, mlp_out)],
+        (
+            (0, None, (0, 1152), "x"),
+            (0, None, (1152, 1152), "y"),
+            (1, (0, 144), None, "x"),
+            (1, (144, 144), None, "y"),
+        ),
+        1,
+    )
+    out_shard, q_shard, co_shard, qkv_shard = scatter_call(
+        [blocks(dwo, self_out), blocks(dwq, cross_q), blocks(dwco, cross_out), blocks(dwqkv, self_qkv)],
+        (
+            (0, None, None, "x"),
+            (1, None, None, "y"),
+            (2, None, None, "x"),
+            (3, None, (0, 896), "y"),
+            (3, None, (896, 832), "x"),
+        ),
+        2,
+    )
+    return (
+        block_out.reshape(tokens.shape),
+        input_grad.reshape(tokens.shape),
+        caption_grad,
+        null_grad,
+        table_grad,
+        time_proj_grad,
+        qkv_shard,
+        out_shard,
+        q_shard,
+        cross_kv_grad,
+        co_shard,
+        in_shard,
+        mo_shard,
+        biases_grad,
+        hidden_total,
+    )
+
+
+def body(*args):
+    if lax.axis_size("frames") == 2 and lax.axis_size("patches") == 16:
+        return fast_body(*args)
+    return plain_body(*args)
 
 
 def solution(mesh):

time: 2010 us -> 993 us (0.49)
  waiting for transfers between devices: 1080 us -> 0.02 us
  Pallas kernels: 0 us -> 772 us
  matrix products: 422 us -> 11.7 us
  local copies, waits for them, and re-layouts: 228 us -> 31.3 us
  other arithmetic: 99.3 us -> 12.8 us
    pallas_call x0 -> x9, Pallas kernels: none -> 772 us  [the longest x2 251 us: scatter_call(): pl.pallas_call(partial(scatter_kernel, units, count), out_shape=[jax.Shap...]
    all_gather x16 -> x0, waiting for transfers between devices: 716 us -> none  [the longest x1 115 us: gather_forward(): lax.all_gather(row_parts[7], 'frames', axis=1, tiled=True)]
    dot_general x14 -> x3, matrix products: 186 us -> 4.18 us  [the longest x1 2.14 us: fast_body(): mods = jnp.einsum('pc,ckd->kpd', onehot, modulation, precision=HIGH)]
    reduce_scatter x3 -> x0, waiting for transfers between devices: 136 us -> none  [the longest x1 110 us: body(): lax.psum_scatter(grads[4].astype(jnp.bfloat16), 'patches', scatter_dimens...]
    psum x1, waiting for transfers between devices: 122 us -> 0.01 us  [fast_body(): time_sum = lax.psum(time_part, ('frames', 'patches'))]
    unnamed x38 -> x1, waiting for transfers between devices: 101 us -> 0.02 us
    dot_general x8 -> x1, matrix products: 76.4 us -> 0.22 us  [forward_dot(): return jnp.dot(left, right, preferred_element_type=jnp.float32)]
    dot_general x7 -> x2, matrix products: 75.2 us -> 5.16 us  [times_transposed(): jnp.einsum('re,de->rd', grad, weight, preferred_element_type=jnp.float32)]
  transfers between devices with their start and end apart: 33 -> 1, of which waited for: 23 -> 0; matrix products, arithmetic and copies ran while one was open for 33% -> 2% of each run, Pallas kernels for 0% -> 23%
where the time goes in v2:
time: 993 us; the launch traced here: 989 us
  Pallas kernels  772 us (78%)
  blocking collectives  145 us (15%)
  local copies, waits for them, and re-layouts  31.3 us (3%)
  between operations  15.3 us (2%)
  other arithmetic  12.8 us (1%)
  matrix products  11.7 us (1%)
    pallas_call x2, Pallas kernels, scatter_call(): pl.pallas_call(partial(scatter_kernel, units, count), out_shape=[jax.Shap...  251 us
    pallas_call x1, Pallas kernels, gather_call(): pl.pallas_call(partial(gather_kernel, units, count), out_shape=[jax.Shape...  227 us
    psum x2, blocking collectives, fast_body(): lax.psum((gkv.astype(F32), bias_part, hsum.reshape(-1), mod_part), ('fram...  145 us
    pallas_call x1, Pallas kernels, mlp_call(): pl.pallas_call(partial(mlp_kernel, chunk, patches), out_shape=[S((rows, w...  86.8 us
    pallas_call x1, Pallas kernels, cross_back_call(): pl.pallas_call(partial(cross_back_kernel, patches, heads), out_shape=[S((...  66.3 us
    pallas_call x1, Pallas kernels, attend_back_call(): pl.pallas_call(partial(attend_back_kernel, patches, heads), out_shape=[S(...  50.1 us
    pallas_call x1, Pallas kernels, attend_call(): pl.pallas_call(partial(attend_kernel, patches, heads), out_shape=[S((widt...  48.4 us
    pallas_call x1, Pallas kernels, cross_call(): pl.pallas_call(partial(cross_kernel, patches, heads), out_shape=[S((width...  36.4 us
  transfers between devices with their start and end apart: 1, of which 0 were waited for; matrix products, arithmetic and copies ran while one was open for 2% of the time, Pallas kernels for 23%

profile of v2, /device:TPU:0, one launch (start us, length us, event | category | flops | bytes accessed | tf_op | source)
XLA Modules:
  0.0 988.6 jit_solution(2204978108869541946)
XLA Ops:
  9.1 0.9 fusion.4.e_ref
  10.0 1.5 fusion.36
  11.5 0.7 convert_element_type.40
  12.3 0.8 reduce-window.8
  13.8 0.9 add_convert_fusion.et_ref
  16.0 227.1 %gather.1 = (bf16[2,4,2,2,72,1728]{5,4,3,2,1,0:T(8,128)(2,1)}, bf16[2,4,2,2,72,576]{5,4,3,2,1,0:T(8,128)(2,1)}, bf16[2,4,2,2,72,576]{5,4,3,2,1,0:T(8,128)(2,1)},...) custom-call(bf16[72,1728]{1,0:T(8,128)(2,1)} %refs_0_.1, ...), custom_call_target="tpu_custom_call" | custom-call | tf_op jit(solution)/shard_map/gather/pallas_call | solution.py:743
  243.1 5.4 fusion.34
  248.7 0.8 and_select_fusion.cm_ref
  250.9 1.1 reshape.283.valid_ref
  252.7 1.1 pad.6
  253.8 2.1 convolution_bitcast_fusion.m_ref.mods_ref
  256.0 1.1 slice_bitcast_fusion.4
  257.0 0.8 copy-done.2
  257.8 6.2 norm.1.nm_ref
  264.0 48.4 %attend.1 = (bf16[1152,3456]{1,0:T(8,128)(2,1)}, bf16[1152,1152]{1,0:T(8,128)(2,1)}, bf16[864,1152]{1,0:T(8,128)(2,1)}, bf16[1056,2304]{1,0:T(8,128)(2,1)}, f32[...) custom-call(bf16[864,1152]{1,0:T(8,128)(2,1)} %norm.1.nm_ref, ...), custom_call_target="tpu_custom_call" | custom-call | tf_op jit(solution)/shard_map/attend/pallas_call | solution.py:918
  312.4 36.4 %cross.1 = (bf16[1152,1152]{1,0:T(8,128)(2,1)}, bf16[1152,1152]{1,0:T(8,128)(2,1)}, bf16[864,1152]{1,0:T(8,128)(2,1)}, bf16[512,1152]{1,0:T(8,128)(2,1)}, bf16[5...) custom-call(f32[864,1152]{1,0:T(8,128)} %get-tuple-element.79.resid_, ...), custom_call_target="tpu_custom_call" | custom-call | tf_op jit(solution)/shard_map/cross/pallas_call | solution.py:997
  348.9 86.8 %mlp.1 = (bf16[864,1152]{1,0:T(8,128)(2,1)}, f32[864,1152]{1,0:T(8,128)}, f32[6,768]{1,0:T(8,128)}, f32[8,1152]{1,0:T(8,128)}, f32[3,96,1152]{2,1,0:T(8,128)}, /...) custom-call(bf16[864,1152]{1,0:T(8,128)(2,1)} %get-tuple-element.84.nm_ref, bf16[864,1152]{1,0:T(8,128)(2,1)} %bitcast.87, ...), custom_call_target="tpu_custom_call" | custom-call | tf_op jit(solution)/shard_map/mlp/pallas_call | solution.py:1128
  435.7 66.3 %cross_back.1 = (f32[864,1152]{1,0:T(8,128)}, bf16[864,1152]{1,0:T(8,128)(2,1)}, bf16[2,512,1152]{2,1,0:T(8,128)(2,1)}, f32[8,1152]{1,0:T(8,128)}, f32[96,1152]{...) custom-call(f32[864,1152]{1,0:T(8,128)} %get-tuple-element.89.grc_ref, ...), custom_call_target="tpu_custom_call" | custom-call | tf_op jit(solution)/shard_map/cross_back/pallas_call | solution.py:1226
  502.0 50.1 %attend_back.1 = (f32[864,1152]{1,0:T(8,128)}, f32[8,1152]{1,0:T(8,128)}, f32[2,96,1152]{2,1,0:T(8,128)}, bf16[2,1152,1728]{2,1,0:T(8,128)(2,1)}) custom-call(bf16[864,1152]{1,0:T(8,128)(2,1)} %get-tuple-element.100.gai_ref, bf16[864,1152]{1,0:T(8,128)(2,1)} %get-tuple-element.101.q_ref, bf16[1056,2304]{1,0:T(8,128)(2,1)} %get-tuple-element.102.kvx_ref, ...), custom_call_target="tpu_custom_call" | custom-call | tf_op jit(solution)/shard_map/attend_back/pallas_call | solution.py:1323
  552.1 0.8 slice.113
  552.8 0.9 fusion.35
  553.7 0.8 slice.117
  554.5 1.0 bitcast_dynamic-update-slice_fusion.5
  555.6 1.0 bitcast_dynamic-update-slice_fusion.4
  556.7 1.2 bitcast_dynamic-update-slice_fusion.2
  557.9 1.0 bitcast_dynamic-update-slice_fusion.1
  558.9 1.0 bitcast_dynamic-update-slice_fusion
  560.0 1.0 fusion.26
  560.9 103.8 %all-reduce.7 = (bf16[2,512,1152]{2,1,0:T(8,128)(2,1)}, f32[4,6,1152]{2,0,1:T(4,128)S(1)}) all-reduce(bf16[2,512,1152]{2,1,0:T(8,128)(2,1)S(1)} %copy-done.5, f32[4,6,1152]{2,0,1:T(4,128)S(1)} %fusion.26), channel_id=1, replica_groups=mesh['frames'=2,'patches'=16] {'frames','patches'}, use_global_device_ids=true, to_apply=%region_3.4 | all-reduce | flops 1207296 | bytes 4939776 | tf_op jit(solution)/shard_map/psum | solution.py:1418
  664.7 1.5 convert_reduce_fusion
  666.2 137.7 %scatter.3 = (f32[72,2304]{1,0:T(8,128)}, f32[288,576]{1,0:T(8,128)}) custom-call(bf16[2,4,2,2,72,2304]{5,4,3,2,1,0:T(8,128)(2,1)} %bitcast.71, bf16[2,4,2,2,288,576]{5,4,3,2,1,0:T(8,128)(2,1)} %bitcast.69), custom_call_target="tpu_custom_call" | custom-call | tf_op jit(solution)/shard_map/scatter/pallas_call | solution.py:797
  803.9 113.1 %scatter.2 = (f32[72,576]{1,0:T(8,128)}, f32[72,576]{1,0:T(8,128)}, f32[72,576]{1,0:T(8,128)}, f32[72,1728]{1,0:T(8,128)}) custom-call(bf16[2,4,2,2,72,576]{5,4,3,2,1,0:T(8,128)(2,1)} %bitcast.80, bf16[2,4,2,2,72,576]{5,4,3,2,1,0:T(8,128)(2,1)} %bitcast.81, bf16[2,4,2,2,72,576]{5,4,3,2,1,0:T(8,128)(2,1)} %bitcast.82, bf16[2,4,2,2,72,1728]{5,4,3,2,1,0:T(8,128)(2,1)} %bitcast.74), custom_call_target="tpu_custom_call" | custom-call | tf_op jit(solution)/shard_map/scatter/pallas_call | solution.py:797
  917.1 3.3 fusion
  920.4 1.9 convolution_add_fusion
  922.3 2.5 select_reduce_fusion
  924.8 0.7 reduce_sum.38
  925.5 1.1 fusion.7
  926.6 41.7 %all-reduce.1 = (f32[7,1152]{1,0:T(8,128)}, f32[4608]{0:T(1024)}) all-reduce(f32[7,1152]{1,0:T(8,128)S(1)} %stack.20, f32[4608]{0:T(1024)S(1)} %reshape.278), channel_id=1, replica_groups=mesh['frames'=2,'patches'=16] {'frames','patches'}, use_global_device_ids=true, to_apply=%region_7.8 | all-reduce | flops 12672 | bytes 101376 | tf_op jit(solution)/shard_map/psum | solution.py:1418
  968.2 0.8 slice_add_fusion
  969.0 1.4 scatter-add.4
  970.4 2.1 fusion.1
  972.6 4.5 copy.55
  977.0 0.8 copy.56
  977.8 0.7 copy.57
  978.5 0.7 copy.58
  979.2 0.7 copy.59
  979.9 0.8 copy.60
  980.7 0.9 copy.61
  (71 shorter events, 5.7 us)
Async XLA Ops:
  7.2 0.9 copy-start
  7.2 246.6 %all-reduce.6.cloned.1.call-start = ((), (), s32[]{:S(2)}) async-start(), calls=%async_computation | async-start | bytes 221184 | tf_op jit(solution)/shard_map/psum | solution.py:1379
  8.3 0.6 copy-start.13
  243.1 6.3 copy-start.8
  243.1 6.3 copy-start.14
  248.5 1.8 copy-start.19
  248.5 3.5 copy-start.20
  256.0 1.8 copy-start.2
  501.9 52.6 %copy-start.18 = (f32[6,768]{1,0:T(8,128)S(1)}, f32[6,768]{1,0:T(8,128)}, u32[]{:S(2)}) copy-start(f32[6,768]{1,0:T(8,128)} %get-tuple-element.126) | copy-start | bytes 55300
  501.9 54.7 %copy-start.12 = (f32[96,1152]{1,0:T(8,128)S(1)}, f32[96,1152]{1,0:T(8,128)}, u32[]{:S(2)}) copy-start(f32[96,1152]{1,0:T(8,128)} %get-tuple-element.109) | copy-start | bytes 1327108
  556.6 4.3 copy-start.5
  803.9 113.2 %copy-start.4 = (bf16[1,4,2,2,72,1152]{5,4,3,2,1,0:T(8,128)(2,1)S(1)}, bf16[1,4,2,2,72,1152]{5,4,3,2,1,0:T(8,128)(2,1)}, u32[]{:S(2)}) copy-start(bf16[1,4,2,2,72,1152]{5,4,3,2,1,0:T(8,128)(2,1)} %get-tuple-element.134) | copy-start | bytes 7962628
  917.1 3.3 copy-start.3
  917.1 3.3 copy-start.6
  922.3 48.1 %copy-start.7 = (bf16[2,512,1152]{2,1,0:T(8,128)(2,1)S(1)}, bf16[2,512,1152]{2,1,0:T(8,128)(2,1)}, u32[]{:S(2)}) copy-start(bf16[2,512,1152]{2,1,0:T(8,128)(2,1)} %get-tuple-element.131) | copy-start | bytes 7077892
  972.6 4.5 copy-start.11
  972.6 5.3 copy-start.17
  972.6 6.0 copy-start.16
  972.6 6.6 copy-start.15
  972.6 7.3 copy-start.10
  972.6 9.0 copy-start.1
  977.0 3.7 copy-start.9
Sparse Core Ops, SparseCore 0:
  14.2 139.1 all-reduce.5

commit v3 on v2

--- a/solution.py
+++ b/solution.py
@@ -586,119 +586,36 @@
 
 class Place:
     def __init__(self):
-        self.y=lax.axis_index("frames"); p=lax.axis_index("patches")
-        self.z=p//4; self.x=lax.rem(p//2,2); self.c=lax.rem(p,2)
-    def dev(self,y=None,z=None,x=None,c=None):
-        y=self.y if y is None else y; z=self.z if z is None else z
-        x=self.x if x is None else x; c=self.c if c is None else c
-        return (y,(z*2+x)*2+c)
-    def zoff(self,d): return lax.rem(self.z+d,4)
+        self.y = lax.axis_index("frames")
+        p = lax.axis_index("patches")
+        self.z = p // 4
+        self.x = lax.rem(p // 2, 2)
+        self.c = lax.rem(p, 2)
+
+    def dev(self, y=None, z=None, x=None, c=None):
+        y = self.y if y is None else y
+        z = self.z if z is None else z
+        x = self.x if x is None else x
+        c = self.c if c is None else c
+        return (y, (z * 2 + x) * 2 + c)
+
+    def zoff(self, d):
+        return lax.rem(self.z + d, 4)
+
 
 def barrier(pos):
-    bar=pltpu.get_barrier_semaphore()
-    peers=[pos.dev(z=pos.zoff(d)) for d in (1,2,3)]+[pos.dev(x=1-pos.x),pos.dev(y=1-pos.y),pos.dev(c=1-pos.c)]
-    for t in peers: pl.semaphore_signal(bar,inc=1,device_id=t,device_id_type=MESH)
-    pl.semaphore_wait(bar,6)
-
-N_AG=9
-class Gather:
-    def __init__(self,pos,shard,full,send,recv,first):
-        self.pos=pos; self.shard=shard; self.full=full; self.send=send; self.recv=recv; self.first=first
-    def _rc(self,i,src,dst,dev):
-        return pltpu.make_async_remote_copy(src_ref=src,dst_ref=dst,send_sem=self.send.at[i],recv_sem=self.recv.at[i],device_id=dev,device_id_type=MESH)
-    def _copies(self):
-        p=self.pos; F=self.full; y,z,x,c=p.y,p.z,p.x,p.c
-        cs=[]
-        mine=F.at[y,z,x,c]
-        for d in (1,2,3):
-            cs.append(self._rc(d-1,self.shard,mine,p.dev(z=p.zoff(d))))
-        line=F.at[y,:,x,c]
-        if self.first=="x":
-            cs.append(self._rc(3,line,line,p.dev(x=1-x)))
-            plane=F.at[y,:,:,c]
-            cs.append(self._rc(4,plane,plane,p.dev(y=1-y)))
-            got1=F.at[y,:,1-x,c]; got2=F.at[1-y,:,:,c]
-        else:
-            cs.append(self._rc(3,line,line,p.dev(y=1-y)))
-            plane=F.at[:,:,x,c]
-            cs.append(self._rc(4,plane,plane,p.dev(x=1-x)))
-            got1=F.at[1-y,:,x,c]; got2=F.at[:,:,1-x,c]
-        o=p.dev(c=1-c)
-        cs.append(self._rc(5,line,line,o)); cs.append(self._rc(6,got1,got1,o)); cs.append(self._rc(7,got2,got2,o))
-        return cs
-    def start(self):
-        self.cs=self._copies()
-        p=self.pos
-        for i in (0,1,2): self.cs[i].start()
-        self.loc=pltpu.make_async_copy(self.shard,self.full.at[p.y,p.z,p.x,p.c],self.send.at[8])
-        self.loc.start()
-    def step1(self):
-        self.loc.wait()
-        for i in (0,1,2): self.cs[i].wait_recv()
-        self.cs[3].start(); self.cs[5].start()
-    def step2(self):
-        self.cs[3].wait_recv(); self.cs[4].start(); self.cs[6].start()
-    def step3(self):
-        self.cs[4].wait_recv(); self.cs[7].start()
-    def finish(self):
-        for i in (5,6,7): self.cs[i].wait_recv()
-        for i in range(8): self.cs[i].wait_send()
-
-N_RS=6
-class Scatter:
-    def __init__(self,pos,part,out,bufs,send,recv,first):
-        self.pos=pos; self.part=part; self.out=out; self.send=send; self.recv=recv; self.first=first
-        self.own,self.r1,self.r2,self.r3,self.r4=bufs
-    def _rc(self,i,src,dst,dev):
-        return pltpu.make_async_remote_copy(src_ref=src,dst_ref=dst,send_sem=self.send.at[i],recv_sem=self.recv.at[i],device_id=dev,device_id_type=MESH)
-    def start(self):
-        p=self.pos
-        self.loc=pltpu.make_async_copy(self.part.at[:,:,:,p.c],self.own,self.send.at[6])
-        self.cc=self._rc(0,self.part.at[:,:,:,1-p.c],self.r1,p.dev(c=1-p.c))
-        self.loc.start(); self.cc.start()
-    def step1(self):
-        p=self.pos; own=self.own
-        self.loc.wait(); self.cc.wait_recv()
-        def body(i,_):
-            f,r=i//8,lax.rem(i,8); z,x=r//2,lax.rem(r,2)
-            own[f,z,x]=(own[f,z,x].astype(jnp.float32)+self.r1[f,z,x].astype(jnp.float32)).astype(jnp.bfloat16)
-            return 0
-        lax.fori_loop(0,16,body,0)
-        if self.first=="y": self.c1=self._rc(1,own.at[1-p.y],self.r2,p.dev(y=1-p.y))
-        else: self.c1=self._rc(1,own.at[:,:,1-p.x],self.r2,p.dev(x=1-p.x))
-        self.c1.start()
-    def step2(self):
-        p=self.pos; own=self.own
-        self.c1.wait_recv()
-        def body(i,_):
-            if self.first=="y": f,z,x=p.y,i//2,lax.rem(i,2); a,b=z,x
-            else: f,z,x=i//4,lax.rem(i,4),p.x; a,b=f,z
-            own[f,z,x]=(own[f,z,x].astype(jnp.float32)+self.r2[a,b].astype(jnp.float32)).astype(jnp.bfloat16)
-            return 0
-        lax.fori_loop(0,8,body,0)
-        if self.first=="y": self.c2=self._rc(2,own.at[p.y,:,1-p.x],self.r3,p.dev(x=1-p.x))
-        else: self.c2=self._rc(2,own.at[1-p.y,:,p.x],self.r3,p.dev(y=1-p.y))
-        self.c2.start()
-    def step3(self):
-        p=self.pos; own=self.own
-        self.c2.wait_recv()
-        def body(z,_):
-            own[p.y,z,p.x]=(own[p.y,z,p.x].astype(jnp.float32)+self.r3[z].astype(jnp.float32)).astype(jnp.bfloat16)
-            return 0
-        lax.fori_loop(0,4,body,0)
-        self.cz=[self._rc(2+d,own.at[p.y,p.zoff(d),p.x],self.r4.at[d-1],p.dev(z=p.zoff(d))) for d in (1,2,3)]
-        for c in self.cz: c.start()
-    def step4(self):
-        p=self.pos
-        for c in self.cz: c.wait_recv()
-        f32=jnp.float32
-        self.out[...]=((self.own[p.y,p.z,p.x].astype(f32)+self.r4[0].astype(f32))+(self.r4[1].astype(f32)+self.r4[2].astype(f32)))
-    def finish(self):
-        for c in [self.cc,self.c1,self.c2]+self.cz: c.wait_send()
-def scatter_bufs(R,C,first):
-    bf=jnp.bfloat16
-    return [pltpu.VMEM((2,4,2,R,C),bf),pltpu.VMEM((2,4,2,R,C),bf),
-      pltpu.VMEM((4,2,R,C) if first=="y" else (2,4,R,C),bf),pltpu.VMEM((4,R,C),bf),pltpu.VMEM((3,R,C),bf)]
+    bar = pltpu.get_barrier_semaphore()
+    peers = [pos.dev(z=pos.zoff(d)) for d in (1, 2, 3)]
+    peers += [pos.dev(x=1 - pos.x), pos.dev(y=1 - pos.y), pos.dev(c=1 - pos.c)]
+    for t in peers:
+        pl.semaphore_signal(bar, inc=1, device_id=t, device_id_type=MESH)
+    pl.semaphore_wait(bar, 6)
+
+
+def remote(src, dst, send, recv, i, dev):
+    return pltpu.make_async_remote_copy(
+        src_ref=src, dst_ref=dst, send_sem=send.at[i], recv_sem=recv.at[i], device_id=dev, device_id_type=MESH
+    )
 
 
 def part_of(ref, rows, cols, lead):
@@ -708,114 +625,464 @@
     return ref.at[tuple(index)]
 
 
-def gather_kernel(units, count, *refs):
-    shards, fulls = refs[:count], refs[count : 2 * count]
-    send, recv = refs[2 * count :]
-    pos = Place()
-    barrier(pos)
-    work = [
-        Gather(
-            pos,
-            part_of(shards[a], r, c, 0),
-            part_of(fulls[a], r, c, 4),
-            send.at[k],
-            recv.at[k],
-            first,
-        )
-        for k, (a, r, c, first) in enumerate(units)
-    ]
-    for unit in work:
-        unit.start()
-    total = len(work)
+class Ticker:
+    def __init__(self, process):
+        self.process = process
+
+    def __call__(self, steps=1):
+        for _ in range(steps):
+            next(self.process, None)
+
+    def drain(self):
+        for _ in self.process:
+            pass
+
+
+N_AG = 11
+
+
+class Gather:
+    def __init__(self, pos, shard, full, send, recv, order):
+        y, z, x, c = pos.y, pos.z, pos.x, pos.c
+        self.order = order
+        mine = full.at[y, z, x, c]
+        self.local = pltpu.make_async_copy(shard, mine, send.at[8])
+        rc = lambda i, ref, dev, src=None: remote(ref if src is None else src, ref, send, recv, i, dev)
+        xd, yd, cd = pos.dev(x=1 - x), pos.dev(y=1 - y), pos.dev(c=1 - c)
+        zd = [pos.dev(z=pos.zoff(d)) for d in (1, 2, 3)]
+        if order == "zxy":
+            line, plane, got1, got2 = full.at[y, :, x, c], full.at[y, :, :, c], full.at[y, :, 1 - x, c], full.at[1 - y, :, :, c]
+            self.stages = [[rc(d, mine, zd[d], shard) for d in range(3)], [rc(3, line, xd)], [rc(4, plane, yd)]]
+        elif order == "zyx":
+            line, plane, got1, got2 = full.at[y, :, x, c], full.at[:, :, x, c], full.at[1 - y, :, x, c], full.at[:, :, 1 - x, c]
+            self.stages = [[rc(d, mine, zd[d], shard) for d in range(3)], [rc(3, line, yd)], [rc(4, plane, xd)]]
+        else:
+            line, plane = full.at[y, z, :, c], full.at[:, z, :, c]
+            self.stages = [[rc(3, mine, xd, shard)], [rc(4, line, yd)], [rc(d, plane, zd[d]) for d in range(3)]]
+            got1, got2 = full.at[1 - y, z, :, c], None
+        self.core = [[rc(5, line, cd)], [rc(6, got1, cd)]]
+        if got2 is not None:
+            self.core.append([rc(7, got2, cd)])
+        else:
+            self.core.append([rc((7, 9, 10)[d], full.at[:, pos.zoff(d + 1), :, c], cd) for d in range(3)])
+
+    def start(self):
+        for k in self.stages[0]:
+            k.start()
+        self.local.start()
+
+    def step1(self):
+        self.local.wait()
+        for k in self.stages[0]:
+            k.wait_recv()
+        for k in self.stages[1]:
+            k.start()
+        for k in self.core[0]:
+            k.start()
+
+    def step2(self):
+        for k in self.stages[1]:
+            k.wait_recv()
+        for k in self.stages[2]:
+            k.start()
+        for k in self.core[1]:
+            k.start()
+
+    def step3(self):
+        for k in self.stages[2]:
+            k.wait_recv()
+        for k in self.core[2]:
+            k.start()
+
+    def finish(self):
+        for stage in self.core:
+            for k in stage:
+                k.wait()
+        for stage in self.stages:
+            for k in stage:
+                k.wait_send()
+
+
+    def head1(self):
+        self.start()
+
+    def head2(self):
+        if self.order == "xyz":
+            self.step1()
+
+    def head_finish(self):
+        if self.order == "xyz":
+            for k in self.stages[1]:
+                k.wait_recv()
+            for k in self.core[0]:
+                k.wait()
+            for k in self.stages[0] + self.stages[1]:
+                k.wait_send()
+        else:
+            self.local.wait()
+            for k in self.stages[0]:
+                k.wait()
+
+    def tail1(self):
+        if self.order == "xyz":
+            for k in self.stages[2]:
+                k.start()
+            for k in self.core[1]:
+                k.start()
+        else:
+            for k in self.stages[1]:
+                k.start()
+            for k in self.core[0]:
+                k.start()
+
+    def tail2(self):
+        if self.order != "xyz":
+            self.step2()
+
+    def tail3(self):
+        self.step3()
+
+    def tail_finish(self):
+        if self.order == "xyz":
+            for stage in self.core[1:]:
+                for k in stage:
+                    k.wait()
+            for k in self.stages[2]:
+                k.wait_send()
+        else:
+            for stage in self.core:
+                for k in stage:
+                    k.wait()
+            for k in self.stages[1] + self.stages[2]:
+                k.wait_send()
+
+
+def gather_process(units, heads=()):
+    for u in units:
+        u.start()
+    yield
+    total = len(units)
     for t in range(total + 2):
         if t < total:
-            work[t].step1()
+            units[t].step1()
+            if t == total - 2 or total == 1:
+                for u in heads:
+                    u.head1()
+            yield
+        elif t == total:
+            for u in heads:
+                u.head2()
         if 0 <= t - 1 < total:
-            work[t - 1].step2()
+            units[t - 1].step2()
+            yield
         if 0 <= t - 2 < total:
-            work[t - 2].step3()
-    for unit in work:
-        unit.finish()
-
-
-def gather_call(shards, units, ident):
-    count = len(shards)
-    return pl.pallas_call(
-        partial(gather_kernel, units, count),
-        out_shape=[jax.ShapeDtypeStruct((2, 4, 2, 2) + s.shape, s.dtype) for s in shards],
-        in_specs=[pl.BlockSpec(memory_space=pl.ANY)] * count,
-        out_specs=[pl.BlockSpec(memory_space=pl.ANY)] * count,
-        scratch_shapes=[
-            pltpu.SemaphoreType.DMA((len(units), N_AG)),
-            pltpu.SemaphoreType.DMA((len(units), 8)),
-        ],
-        compiler_params=pltpu.CompilerParams(collective_id=ident, has_side_effects=True),
-        name="gather",
-    )(*shards)
-
-
-def scatter_kernel(units, count, *refs):
-    parts, outs = refs[:count], refs[count : 2 * count]
-    rest = refs[2 * count :]
-    send, recv = rest[-2:]
-    pos = Place()
-    barrier(pos)
-    work = [
-        Scatter(
-            pos,
-            part_of(parts[a], r, c, 4),
-            part_of(outs[a], r, c, 0),
-            rest[5 * k : 5 * k + 5],
-            send.at[k],
-            recv.at[k],
-            first,
+            units[t - 2].step3()
+            yield
+    for u in units:
+        u.finish()
+    for u in heads:
+        u.head_finish()
+
+
+def head_tail_process(heads, tails, lags):
+    for u in heads:
+        u.head1()
+    total = len(tails)
+    for t in range(total + lags[1]):
+        if t == 0:
+            for u in tails:
+                if u.order == "zxy":
+                    u.tail1()
+        elif t < total and tails[t].order != "zxy":
+            tails[t].tail1()
+        if t == 1:
+            for u in heads:
+                u.head2()
+        if 0 <= t - lags[0] < total:
+            tails[t - lags[0]].tail2()
+        if 0 <= t - lags[1] < total:
+            tails[t - lags[1]].tail3()
+        yield
+    for u in tails:
+        u.tail_finish()
+    for u in heads:
+        u.head_finish()
+
+
+def tail_process(units, lags=(2, 4)):
+    total = len(units)
+    for t in range(total + lags[1]):
+        if t < total:
+            units[t].tail1()
+        if 0 <= t - lags[0] < total:
+            units[t - lags[0]].tail2()
+        if 0 <= t - lags[1] < total:
+            units[t - lags[1]].tail3()
+        yield
+    for u in units:
+        u.tail_finish()
+
+
+def both_processes(*processes):
+    live = list(processes)
+    while live:
+        left = []
+        for p in live:
+            try:
+                next(p)
+                left.append(p)
+            except StopIteration:
+                pass
+        live = left
+        if live:
+            yield
+
+
+def after(first, second):
+    yield from first
+    yield from second
+
+
+def gather_units(pos, units, shards, fulls, send, recv):
+    return [
+        Gather(pos, part_of(shards[a], r, c, 0), part_of(fulls[a], r, c, 4), send.at[k], recv.at[k], order)
+        for k, (a, r, c, order) in enumerate(units)
+    ]
+
+
+def gather_shapes(shards):
+    return [jax.ShapeDtypeStruct((2, 4, 2, 2) + s.shape, s.dtype) for s in shards]
+
+
+def gather_sems(units):
+    return [pltpu.SemaphoreType.DMA((len(units), N_AG)), pltpu.SemaphoreType.DMA((len(units), N_AG))]
+
+
+N_RS = 8
+
+
+def add_into(dst, src, count, index_dst, index_src):
+    def step(i, carry):
+        d, s = index_dst(i), index_src(i)
+        dst[d] = dst[d] + src[s]
+        return carry
+
+    lax.fori_loop(0, count, step, 0)
+
+
+def half_shape(size, order):
+    return ((4, 2) if order == "yxz" else (2, 4)) + size
+
+
+class ScatterHead:
+    def __init__(self, pos, part, r1, r2, keep, own, other, send, recv, order):
+        self.own, self.other = own, other
+        y, x, c = pos.y, pos.x, pos.c
+        self.cc = remote(part.at[:, :, :, 1 - c], r1, send, recv, 0, pos.dev(c=1 - c))
+        self.loads = (
+            pltpu.make_async_copy(part.at[:, :, :, c], own, send.at[2]),
+            pltpu.make_async_copy(r1, other, send.at[3]),
         )
-        for k, (a, r, c, first) in enumerate(units)
-    ]
-    total = len(work)
-    for unit in work:
-        unit.start()
-    for t in range(total + 3):
-        if t < total:
-            work[t].step1()
-        if 0 <= t - 1 < total:
-            work[t - 1].step2()
-        if 0 <= t - 2 < total:
-            work[t - 2].step3()
-        if 0 <= t - 3 < total:
-            work[t - 3].step4()
-    for unit in work:
-        unit.finish()
-
-
-def scatter_call(parts, units, ident):
-    count = len(parts)
-    scratch = []
-    for a, r, c, first in units:
-        rows, cols = parts[a].shape[-2:]
-        scratch += scatter_bufs(r[1] if r else rows, c[1] if c else cols, first)
-    return pl.pallas_call(
-        partial(scatter_kernel, units, count),
-        out_shape=[jax.ShapeDtypeStruct(p.shape[-2:], jnp.float32) for p in parts],
-        in_specs=[pl.BlockSpec(memory_space=pl.ANY)] * count,
-        out_specs=[pl.BlockSpec(memory_space=pltpu.VMEM)] * count,
-        scratch_shapes=scratch
-        + [
-            pltpu.SemaphoreType.DMA((len(units), 7)),
-            pltpu.SemaphoreType.DMA((len(units), N_RS)),
-        ],
-        compiler_params=pltpu.CompilerParams(
-            collective_id=ident, has_side_effects=True, vmem_limit_bytes=60 * 2**20
-        ),
-        name="scatter",
-    )(*parts)
+        if order == "yxz":
+            self.c1 = remote(own.at[1 - y], r2, send, recv, 1, pos.dev(y=1 - y))
+            self.store = pltpu.make_async_copy(own.at[y], keep, send.at[4])
+        else:
+            self.c1 = remote(own.at[:, :, 1 - x], r2, send, recv, 1, pos.dev(x=1 - x))
+            self.store = pltpu.make_async_copy(own.at[:, :, x], keep, send.at[4])
+
+    def send(self):
+        self.cc.start()
+
+    def load(self):
+        self.cc.wait_recv()
+        for k in self.loads:
+            k.start()
+
+    def step1(self):
+        for k in self.loads:
+            k.wait()
+        at = lambda i: (i // 8, lax.rem(i // 2, 4), lax.rem(i, 2))
+        add_into(self.own, self.other, 16, at, at)
+        self.c1.start()
+        self.store.start()
+
+    def step2(self):
+        self.c1.wait()
+        self.store.wait()
+
+    def finish(self):
+        self.cc.wait_send()
+
+
+class ScatterTail:
+    def __init__(self, pos, keep, r2, out, h, g, r3, r4, send, recv, order):
+        self.pos, self.out, self.order = pos, out, order
+        self.h, self.g, self.r3, self.r4 = h, g, r3, r4
+        y, x = pos.y, pos.x
+        self.loads = (pltpu.make_async_copy(keep, h, send.at[4]), pltpu.make_async_copy(r2, g, send.at[5]))
+        if order == "yxz":
+            self.c2 = remote(h.at[:, 1 - x], r3, send, recv, 0, pos.dev(x=1 - x))
+        else:
+            self.c2 = remote(h.at[1 - y], r3, send, recv, 0, pos.dev(y=1 - y))
+        self.cz = [remote(r3.at[pos.zoff(d)], r4.at[d - 1], send, recv, d, pos.dev(z=pos.zoff(d))) for d in (1, 2, 3)]
+
+    def load(self):
+        for k in self.loads:
+            k.start()
+
+    def step1(self):
+        for k in self.loads:
+            k.wait()
+        if self.order == "yxz":
+            at = lambda i: (i // 2, lax.rem(i, 2))
+        else:
+            at = lambda i: (i // 4, lax.rem(i, 4))
+        add_into(self.h, self.g, 8, at, at)
+        self.c2.start()
+
+    def step2(self):
+        y, x = self.pos.y, self.pos.x
+        self.c2.wait()
+        add_into(self.r3, self.h, 4, lambda i: (i,), (lambda i: (i, x)) if self.order == "yxz" else (lambda i: (y, i)))
+        for k in self.cz:
+            k.start()
+
+    def step3(self):
+        for k in self.cz:
+            k.wait()
+        f = lambda v: v.astype(F32)
+        total = (f(self.r3[self.pos.z]) + f(self.r4[0])) + (f(self.r4[1]) + f(self.r4[2]))
+        self.out[...] = total.astype(self.out.dtype)
+
+
+def scatter_head_process(units, deep=3, ahead=3):
+    lags = (1, deep)
+    total = len(units)
+    for u in units[:ahead]:
+        u.send()
+    yield
+    for t in range(total + lags[1]):
+        if t + ahead < total:
+            units[t + ahead].send()
+        for lag, step in ((lags[1], "step2"), (lags[0], "step1"), (0, "load")):
+            if 0 <= t - lag < total:
+                getattr(units[t - lag], step)()
+        yield
+    for u in units:
+        u.finish()
+
+
+def scatter_tail_process(units, deep=3, more=3):
+    lags = (1, deep, deep + more)
+    total = len(units)
+    for t in range(total + lags[2]):
+        for lag, step in ((lags[2], "step3"), (lags[1], "step2"), (lags[0], "step1"), (0, "load")):
+            if 0 <= t - lag < total:
+                getattr(units[t - lag], step)()
+        yield
+
+
+class Slots:
+    def __init__(self):
+        self.scratch, self.at, self.turn = [], {}, {}
+
+    def take(self, kind, shape, most, want):
+        key = (kind, shape)
+        if key not in self.at:
+            n = min(most, want)
+            self.at[key] = (len(self.scratch), n)
+            self.turn[key] = 0
+            self.scratch += [pltpu.VMEM(shape, BF)] * n
+        base, n = self.at[key]
+        k = self.turn[key]
+        self.turn[key] = k + 1
+        return base + k % n
+
+
+class ScatterPlan:
+    def __init__(self, shapes, units, deep=3, others=1):
+        self.units, self.deep, self.others = units, deep, others
+        self.sizes = [(r[1] if r else shapes[a][0], c[1] if c else shapes[a][1]) for a, r, c, *_ in units]
+        self.halves = [jax.ShapeDtypeStruct(half_shape(s, u[3]), BF) for s, u in zip(self.sizes, units)]
+        self.r1_shapes = [jax.ShapeDtypeStruct((2, 4, 2) + s, BF) for s in self.sizes]
+        self.n = len(units)
+
+    def head_scratch(self):
+        slots = Slots()
+        kinds = [(2, 4, 2) + s for s in self.sizes]
+        self.own_at = [slots.take("own", k, self.deep, kinds.count(k)) for k in kinds]
+        self.other_at = [slots.take("other", k, self.others, kinds.count(k)) for k in kinds]
+        return slots.scratch + [pltpu.SemaphoreType.DMA((self.n, 5)), pltpu.SemaphoreType.DMA((self.n, 2))]
+
+    def head_bind(self, pos, parts, r1s, r2s, keeps, refs):
+        send, recv = refs[-2:]
+        return [
+            ScatterHead(
+                pos, part_of(parts[u[0]], u[1], u[2], 4), r1s[k], r2s[k], keeps[k], refs[self.own_at[k]], refs[self.other_at[k]],
+                send.at[k], recv.at[k], u[3],
+            )
+            for k, u in enumerate(self.units)
+        ]
+
+    def tail_scratch(self):
+        slots = Slots()
+        kinds = [h.shape for h in self.halves]
+        self.h_at = [slots.take("h", k, self.deep, kinds.count(k)) for k in kinds]
+        self.g_at = [slots.take("g", k, self.others, kinds.count(k)) for k in kinds]
+        self.landing = len(slots.scratch)
+        scratch = slots.scratch
+        for s in self.sizes:
+            scratch += [pltpu.VMEM((4,) + s, BF), pltpu.VMEM((3,) + s, BF)]
+        return scratch + [pltpu.SemaphoreType.DMA((self.n, 6)), pltpu.SemaphoreType.DMA((self.n, 4))]
+
+    def tail_bind(self, pos, keeps, r2s, outs, refs):
+        send, recv = refs[-2:]
+        made = []
+        for k, (a, r, c, order, base) in enumerate(self.units):
+            o = (r[0] - base, r[1]) if r else None
+            at = self.landing + 2 * k
+            made.append(
+                ScatterTail(
+                    pos, keeps[k], r2s[k], part_of(outs[a], o, c, 0), refs[self.h_at[k]], refs[self.g_at[k]], refs[at], refs[at + 1],
+                    send.at[k], recv.at[k], order,
+                )
+            )
+        return made
+
+
+def take(refs, *counts):
+    out, at = [], 0
+    for n in counts:
+        out.append(refs[at : at + n])
+        at += n
+    return out + [refs[at:]]
+
+
+def sum_process(pos, acc, land, zland, send, recv):
+    copies = [remote(acc, zland.at[pos.z], send, recv, 2 + d, pos.dev(z=pos.zoff(d))) for d in (1, 2, 3)]
+    zland[pos.z] = acc[...]
+    for copy in copies:
+        copy.start()
+    yield
+    for copy in copies:
+        copy.wait()
+    acc[...] = (zland[0] + zland[1]) + (zland[2] + zland[3])
+    for i, dev in enumerate((pos.dev(c=1 - pos.c), pos.dev(x=1 - pos.x), pos.dev(y=1 - pos.y))):
+        if land[i] is None:
+            continue
+        copy = remote(acc, land[i], send, recv, i, dev)
+        copy.start()
+        yield
+        copy.wait()
+        acc[...] += land[i][...]
 
 
 def attend_kernel(
-    patches, heads, nm_ref, x_ref, mods_ref, w1_ref, w2_ref, qb_ref, ob_ref, e_ref, et_ref, info_ref,
-    wqkv_ref, wo_ref, q_ref, kvx_ref, probs_ref, attn_ref, ao_ref, resid_ref, residb_ref,
-    w1_buf, w2_buf, wqkv_buf, wo_buf, halo_out, halo_in, sems, send, recv,
+    patches, heads, units, n, hunits, hn, nm_ref, x_ref, gate_ref, w1_ref, w2_ref, qb_ref, ob_ref, e_ref, et_ref, info_ref, *refs
 ):
+    shards, _, hshards, outs, fulls, hfulls, refs = take(refs, n, n, hn, 9, n, hn)
+    wqkv_ref, wo_ref, q_ref, kvx_ref, probs_ref, attn_ref, ao_ref, resid_ref, residb_ref = outs
+    w1_buf, w2_buf, wqkv_buf, wo_buf, halo_out, halo_in, sems, send, recv, g_send, g_recv, h_send, h_recv = refs
     pos = Place()
     rows, width = x_ref.shape
     frames = rows // patches
@@ -826,7 +1093,13 @@
     )
     for c in loads:
         c.start()
-    pair_barrier(pos)
+    barrier(pos)
+    tick = Ticker(
+        head_tail_process(
+            gather_units(pos, hunits, hshards, hfulls, h_send, h_recv), gather_units(pos, units, shards, fulls, g_send, g_recv), (2, 4)
+        )
+    )
+    tick()
     cut = 3 * width // 2
     half = width // 2
     loads[0].wait()
@@ -854,6 +1127,7 @@
             kvx_ref[own, (third - 1) * width : third * width] = got
         if third == 2:
             copy = halo_send(pos, frames, patches, count, y, kvx_ref, halo_out, halo_in, send, recv)
+    tick()
     copy.wait()
     place = jnp.where(y == 0, count, -1) + 1
 
@@ -863,30 +1137,26 @@
         kvx_ref[r, :] = jnp.where(hit > 0.5, halo_in[...].astype(F32), kvx_ref[r, :].astype(F32)).astype(BF)
 
     each(frames + 2, settle)
+    tick()
     scale = (width // heads) ** (-0.5)
-    each(
-        frames // 3,
-        lambda t: attend_tile(t, 3, patches, count, y, scale, q_ref, kvx_ref, e_ref, et_ref, probs_ref, attn_ref),
-    )
+    for t in range(frames // 3):
+        attend_tile(t, 3, patches, count, y, scale, q_ref, kvx_ref, e_ref, et_ref, probs_ref, attn_ref)
+        tick()
     resid_ref[...] = dot(attn_ref[...], wo_buf[...]) + ob_ref[...]
+    tick()
 
     def frame(s):
         r = rows_at(s * patches, patches)
         ao = resid_ref[r, :]
         ao_ref[r, :] = ao.astype(BF)
-        resid = x_ref[r, :].astype(F32) + mods_ref[2] * ao
+        resid = x_ref[r, :].astype(F32) + gate_ref[...] * ao
         resid_ref[r, :] = resid
         residb_ref[r, :] = resid.astype(BF)
 
     each(frames, frame)
     for c in keep:
         c.wait()
-
-
-def pair_barrier(pos):
-    bar = pltpu.get_barrier_semaphore()
-    pl.semaphore_signal(bar, inc=1, device_id=pos.dev(y=1 - pos.y), device_id_type=MESH)
-    pl.semaphore_wait(bar, 1)
+    tick.drain()
 
 
 def pick_slot(frames, patches, slot, src_ref, dst_ref):
@@ -910,41 +1180,112 @@
     return copy
 
 
-def attend_call(patches, heads, nm, x, mods, w1, w2, qb, ob, e, et, info, ident):
+def attend_call(patches, heads, nm, x, gate, w1, w2, qb, ob, e, et, info, shards, fulls, units, hshards, hunits, ident):
     rows, width = x.shape
     frames = rows // patches
     ext = (frames + 2) * patches
     S = jax.ShapeDtypeStruct
-    return pl.pallas_call(
-        partial(attend_kernel, patches, heads),
+    n, hn = len(shards), len(hshards)
+    out = pl.pallas_call(
+        partial(attend_kernel, patches, heads, units, n, hunits, hn),
         out_shape=[
             S((width, 3 * width), BF), S((width, width), BF), S((rows, width), BF), S((ext, 2 * width), BF),
             S((3, rows, 128), F32), S((rows, width), BF), S((rows, width), BF), S((rows, width), F32), S((rows, width), BF),
-        ],
-        in_specs=[IN_VMEM] * 3 + [IN_ANY] * 2 + [IN_VMEM] * 4 + [IN_SMEM],
-        out_specs=[IN_ANY] * 2 + [IN_VMEM] * 7,
+        ]
+        + gather_shapes(shards)
+        + gather_shapes(hshards),
+        in_specs=[IN_VMEM] * 3 + [IN_ANY] * 2 + [IN_VMEM] * 4 + [IN_SMEM] + [IN_ANY] * (2 * n + hn),
+        out_specs=[IN_ANY] * 2 + [IN_VMEM] * 7 + [IN_ANY] * (n + hn),
+        input_output_aliases={10 + n + i: 9 + i for i in range(n)},
         scratch_shapes=[
             pltpu.VMEM(w1.shape, BF), pltpu.VMEM(w2.shape, BF), pltpu.VMEM((width, 3 * width), BF), pltpu.VMEM((width, width), BF),
             pltpu.VMEM((patches, 2 * width), BF), pltpu.VMEM((patches, 2 * width), BF),
             pltpu.SemaphoreType.DMA((4,)), pltpu.SemaphoreType.DMA, pltpu.SemaphoreType.DMA,
-        ],
+        ]
+        + gather_sems(units)
+        + gather_sems(hunits),
         compiler_params=pltpu.CompilerParams(collective_id=ident, has_side_effects=True, vmem_limit_bytes=VMEM_LIMIT),
         name="attend",
-    )(nm, x, mods, w1, w2, qb, ob, e, et, info)
-
-
-def norm_call(patches, x, mods):
-    return pl.pallas_call(
-        lambda x_ref, m_ref, o_ref: norm_body(x_ref, m_ref, o_ref, patches),
-        out_shape=jax.ShapeDtypeStruct(x.shape, BF), in_specs=[IN_VMEM] * 2, out_specs=IN_VMEM, name="norm",
-    )(x, mods)
+    )(nm, x, gate, w1, w2, qb, ob, e, et, info, *shards, *fulls, *hshards)
+    return out[:9], [g.reshape(2, -1, g.shape[-1]) for g in out[9 : 9 + n]], out[9 + n :]
+
+
+def clip_rows(one_ref, rows):
+    total = None
+    for c, row in enumerate(rows):
+        term = one_ref[:, c : c + 1] * row
+        total = term if total is None else total + term
+    return total
+
+
+def open_kernel(patches, units, count, hunits, hcount, x_ref, part_ref, table_ref, one_ref, *refs):
+    shards, hshards, (nm_ref, scale_ref, gate_ref, mods_ref), fulls, hfulls, refs = take(refs, count, hcount, 4, count, hcount)
+    shift_ref, acc, land_c, land_x, zland, both, g_send, g_recv, h_send, h_recv, s_send, s_recv = refs
+    pos = Place()
+    width = x_ref.shape[1]
+    clips = one_ref.shape[1]
+    barrier(pos)
+    heads = gather_units(pos, hunits, hshards, hfulls, h_send, h_recv)
+    tick = Ticker(gather_process(gather_units(pos, units, shards, fulls, g_send, g_recv), heads))
+    acc[...] = part_ref[...]
+    small = Ticker(sum_process(pos, acc, (land_c, land_x, None), zland, s_send, s_recv))
+    small()
+    small()
+    tick()
+    small.drain()
+    both[pos.y] = acc[...]
+    swap = remote(acc, both.at[pos.y], s_send, s_recv, 2, pos.dev(y=1 - pos.y))
+    swap.start()
+    swap.wait()
+    for k in range(6):
+        f, u = k // 3, k % 3
+        rows = [
+            both[f, c : c + 1, u * width : (u + 1) * width] + table_ref[k : k + 1, :] for c in range(clips)
+        ]
+        (shift_ref, scale_ref, gate_ref, mods_ref.at[0], mods_ref.at[1], mods_ref.at[2])[k][...] = clip_rows(one_ref, rows)
+        if k % 2:
+            tick()
+
+    def frame(s):
+        r = rows_at(s * patches, patches)
+        xhat, _ = normalise(x_ref[r, :].astype(F32))
+        nm_ref[r, :] = (xhat * (1.0 + scale_ref[...]) + shift_ref[...]).astype(BF)
+
+    each(x_ref.shape[0] // patches, frame)
+    tick.drain()
+
+
+def open_call(patches, x, part, table, one, shards, units, hshards, hunits, ident):
+    rows, width = x.shape
+    count, hcount = len(shards), len(hshards)
+    S = jax.ShapeDtypeStruct
+    out = pl.pallas_call(
+        partial(open_kernel, patches, units, count, hunits, hcount),
+        out_shape=[S((rows, width), BF), S((patches, width), F32), S((patches, width), F32), S((3, patches, width), F32)]
+        + gather_shapes(shards)
+        + gather_shapes(hshards),
+        in_specs=[IN_VMEM] * 4 + [IN_ANY] * (count + hcount),
+        out_specs=[IN_VMEM] * 4 + [IN_ANY] * (count + hcount),
+        scratch_shapes=[
+            pltpu.VMEM((patches, width), F32),
+            pltpu.VMEM(part.shape, F32), pltpu.VMEM(part.shape, F32), pltpu.VMEM(part.shape, F32),
+            pltpu.VMEM((4,) + part.shape, F32), pltpu.VMEM((2,) + part.shape, F32),
+        ]
+        + gather_sems(units)
+        + gather_sems(hunits)
+        + [pltpu.SemaphoreType.DMA((6,)), pltpu.SemaphoreType.DMA((6,))],
+        compiler_params=pltpu.CompilerParams(collective_id=ident, has_side_effects=True, vmem_limit_bytes=VMEM_LIMIT),
+        name="open",
+    )(x, part, table, one, *shards, *hshards)
+    return out[:4], [g.reshape(2, -1, g.shape[-1]) for g in out[4 : 4 + count]], out[4 + count :]
 
 
 def cross_kernel(
-    patches, heads, resid_ref, residb_ref, mods_ref, used_ref, cm_ref, w2_ref, w3_ref, kv_ref, b3_ref, b4_ref, b5_ref,
-    wq_ref, wco_ref, q_ref, keys_ref, vals_ref, lse_ref, mixb_ref, rc_ref, nm_ref,
-    w2_buf, w3_buf, kv_buf, wq_buf, wco_buf, mix_buf, cmask, sems,
+    patches, heads, units, n, resid_ref, residb_ref, mods_ref, used_ref, cm_ref, w2_ref, w3_ref, kv_ref, b3_ref, b4_ref, b5_ref, *refs
 ):
+    shards, _, (wq_ref, wco_ref, q_ref, keys_ref, vals_ref, lse_ref, mixb_ref, rc_ref, nm_ref), fulls, refs = take(refs, n, n, 9, n)
+    w2_buf, w3_buf, kv_buf, wq_buf, wco_buf, mix_buf, cmask, sems, g_send, g_recv = refs
+    pos = Place()
     rows, width = resid_ref.shape
     frames = rows // patches
     half = width // 2
@@ -955,6 +1296,9 @@
     )
     for c in loads:
         c.start()
+    barrier(pos)
+    tick = Ticker(tail_process(gather_units(pos, units, shards, fulls, g_send, g_recv), (4, 8)))
+    tick()
     for i in range(3):
         cmask[i * patches : (i + 1) * patches, :] = cm_ref[...]
     mix_buf[...] = jnp.zeros(mix_buf.shape, F32)
@@ -973,8 +1317,11 @@
     for c in keep:
         c.start()
     q_ref[...] = (dot(residb_ref[...], wq_buf[...]) + b3_ref[...]).astype(BF)
+    tick()
     for h in range(heads):
         cross_head(h, heads, rows // cmask.shape[0], q_ref, keys_ref, vals_ref, cmask, lse_ref, mix_buf)
+        if h % 2:
+            tick()
     mixb_ref[...] = mix_buf[...].astype(BF)
     rc_ref[...] = dot(mixb_ref[...], wco_buf[...]) + b5_ref[...]
 
@@ -983,79 +1330,101 @@
         rc = rc_ref[r, :] + resid_ref[r, :]
         rc_ref[r, :] = rc
         xhat, _ = normalise(rc)
-        nm_ref[r, :] = (xhat * (1.0 + mods_ref[4]) + mods_ref[3]).astype(BF)
+        nm_ref[r, :] = (xhat * (1.0 + mods_ref[1]) + mods_ref[0]).astype(BF)
 
     each(frames, frame)
     for c in keep:
         c.wait()
-
-
-def cross_call(patches, heads, resid, residb, mods, used, cm, w2, w3, kv, b3, b4, b5):
+    tick.drain()
+
+
+def cross_call(patches, heads, resid, residb, mods, used, cm, w2, w3, kv, b3, b4, b5, shards, fulls, units, ident):
     rows, width = resid.shape
     caps = used.shape[0]
     S = jax.ShapeDtypeStruct
-    return pl.pallas_call(
-        partial(cross_kernel, patches, heads),
+    n = len(shards)
+    out = pl.pallas_call(
+        partial(cross_kernel, patches, heads, units, n),
         out_shape=[
             S((width, width), BF), S((width, width), BF), S((rows, width), BF), S((caps, width), BF), S((caps, width), BF),
             S((rows, 128), F32), S((rows, width), BF), S((rows, width), F32), S((rows, width), BF),
-        ],
-        in_specs=[IN_VMEM] * 5 + [IN_ANY] * 3 + [IN_VMEM] * 3,
-        out_specs=[IN_ANY] * 2 + [IN_VMEM] * 7,
+        ]
+        + gather_shapes(shards),
+        in_specs=[IN_VMEM] * 5 + [IN_ANY] * 3 + [IN_VMEM] * 3 + [IN_ANY] * 2 * n,
+        out_specs=[IN_ANY] * 2 + [IN_VMEM] * 7 + [IN_ANY] * n,
+        input_output_aliases={11 + n + i: 9 + i for i in range(n)},
         scratch_shapes=[
             pltpu.VMEM(w2.shape, BF), pltpu.VMEM(w3.shape, BF), pltpu.VMEM(kv.shape, BF), pltpu.VMEM((width, width), BF), pltpu.VMEM((width, width), BF),
             pltpu.VMEM((rows, width), F32), pltpu.VMEM((3 * patches, caps), F32), pltpu.SemaphoreType.DMA((5,)),
-        ],
-        compiler_params=pltpu.CompilerParams(vmem_limit_bytes=VMEM_LIMIT),
+        ]
+        + gather_sems(units),
+        compiler_params=pltpu.CompilerParams(collective_id=ident, has_side_effects=True, vmem_limit_bytes=VMEM_LIMIT),
         name="cross",
-    )(resid, residb, mods, used, cm, w2, w3, kv, b3, b4, b5)
+    )(resid, residb, mods, used, cm, w2, w3, kv, b3, b4, b5, *shards, *fulls)
+    return out[:9], [g.reshape(2, -1, g.shape[-1]) for g in out[9:]]
 
 
 def mlp_kernel(
-    chunk, patches, nm_ref, cot_ref, valid_ref, rc_ref, mods_ref, hb_ref, b6_ref, win_ref, wout_ref,
-    out_ref, grc_ref, hsum_ref, bsum_ref, gp_ref, dwin_ref, dwout_ref,
-    gm_ref, res_ref, win_b, wout_h, wout_b, act_b, gpre_b, din_s, dout_s, in_sem, out_sem,
+    chunk, patches, plan, nm_ref, cot_ref, valid_ref, rc_ref, mods_ref, hb_ref, b6_ref, win_ref, wout_ref, *refs
 ):
+    m = plan.n
+    outs, r1s, r2s, keeps, refs = take(refs, 7, m, m, m)
+    out_ref, grc_ref, hsum_ref, bsum_ref, gp_ref, dwin_ref, dwout_ref = outs
+    (gm_ref, res_ref, win_b, wout_h, wout_b, act_b, gpre_b, din_s, dout_s, in_sem, out_sem), refs = refs[:11], refs[11:]
+    pos = Place()
     rows, width = nm_ref.shape
     frames = rows // patches
     half = wout_ref.shape[2]
     per = win_ref.shape[2] // chunk
     total = 2 * per
 
+    def places(j):
+        f, u = lax.rem(j, 2), j // 2
+        return f, f * per + u, pl.ds(pl.multiple_of(u * chunk, 128), chunk)
+
     def loads(j, slot):
-        f, u = j // per, lax.rem(j, per)
-        cols = pl.ds(pl.multiple_of(u * chunk, 128), chunk)
-        rws = pl.ds(pl.multiple_of(j * chunk, 128), chunk)
+        f, at, cols = places(j)
+        rws = pl.ds(pl.multiple_of(at * chunk, 128), chunk)
         return (
             pltpu.make_async_copy(win_ref.at[f, :, cols], win_b.at[slot], in_sem.at[slot, 0]),
             pltpu.make_async_copy(wout_ref.at[:, rws], wout_h.at[slot], in_sem.at[slot, 1]),
         )
 
-    def stores(j, slot):
-        f, u = j // per, lax.rem(j, per)
-        cols = pl.ds(pl.multiple_of(u * chunk, 128), chunk)
-        rws = pl.ds(pl.multiple_of(j * chunk, 128), chunk)
+    def stores(j):
+        f, at, cols = places(j)
+        rws = pl.ds(pl.multiple_of(at * chunk, 128), chunk)
         return (
-            pltpu.make_async_copy(din_s.at[slot], dwin_ref.at[f, :, cols], out_sem.at[slot, 0]),
-            pltpu.make_async_copy(dout_s.at[slot], dwout_ref.at[:, rws], out_sem.at[slot, 1]),
+            pltpu.make_async_copy(din_s, dwin_ref.at[f, :, :, :, :, cols], out_sem.at[0]),
+            pltpu.make_async_copy(dout_s, dwout_ref.at[:, rws], out_sem.at[1]),
         )
 
     for c in loads(0, 0):
         c.start()
+    barrier(pos)
+    units = plan.head_bind(pos, [dwin_ref], r1s, r2s, keeps, refs)
     bsum_ref[...] = jnp.zeros(bsum_ref.shape, F32)
     gp_ref[...] = jnp.zeros(gp_ref.shape, F32)
 
     def prepare(s):
         r = rows_at(s * patches, patches)
         gf = jnp.where(valid_ref[r, :] > 0.5, cot_ref[r, :].astype(F32), 0.0)
-        gm = (mods_ref[5] * gf).astype(BF)
+        gm = (mods_ref[2] * gf).astype(BF)
         gm_ref[r, :] = gm
         bsum_ref[0:1, :] += jnp.sum(gm.astype(F32), axis=0, keepdims=True)
 
     each(frames, prepare)
 
+    def reduce(j, late, step):
+        for u in range(per - 1):
+
+            @pl.when(j == 2 * u + 2 + late)
+            def _():
+                for unit in units[2 * u : 2 * u + 2]:
+                    getattr(unit, step)()
+
     def step(j, carry):
         slot = lax.rem(j, 2)
+        _, at, _ = places(j)
         for c in loads(j, slot):
             c.wait()
 
@@ -1064,37 +1433,49 @@
             for c in loads(j + 1, 1 - slot):
                 c.start()
 
-        @pl.when(j >= 2)
-        def _():
-            for c in stores(j - 2, slot):
-                c.wait()
-
         wout_b[...] = jnp.concatenate([wout_h[slot, 0], wout_h[slot, 1]], axis=1)
-        pre = dot(nm_ref[...], win_b[slot]) + hb_ref[pl.ds(j, 1), :]
+        pre = dot(nm_ref[...], win_b[slot]) + hb_ref[pl.ds(at, 1), :]
         act, slope = gelu_parts(pre)
         act_b[...] = act.astype(BF)
         gpre = (dot_nt(gm_ref[...], wout_b[...]) * slope).astype(BF)
         gpre_b[...] = gpre
-        hsum_ref[pl.ds(j, 1), :] = jnp.sum(gpre.astype(F32), axis=0, keepdims=True)
+        hsum_ref[pl.ds(at, 1), :] = jnp.sum(gpre.astype(F32), axis=0, keepdims=True)
+
+        @pl.when(j >= 1)
+        def _():
+            for c in stores(j - 1):
+                c.wait()
+
+        reduce(j, 0, "send")
         part = dot(act_b[...], wout_b[...])
-        back = dot_nt(gpre_b[...], win_b[slot])
 
         @pl.when(j == 0)
         def _():
             res_ref[...] = part
-            grc_ref[...] = back
 
         @pl.when(j > 0)
         def _():
             res_ref[...] += part
+
+        reduce(j, 0, "load")
+        back = dot_nt(gpre_b[...], win_b[slot])
+
+        @pl.when(j == 0)
+        def _():
+            grc_ref[...] = back
+
+        @pl.when(j > 0)
+        def _():
             grc_ref[...] += back
 
-        din_s[slot] = dot_tn(nm_ref[...], gpre_b[...]).astype(BF)
+        reduce(j, 0, "step1")
+        din_s[...] = dot_tn(nm_ref[...], gpre_b[...]).reshape(din_s.shape).astype(BF)
         d = dot_tn(act_b[...], gm_ref[...]).astype(BF)
-        dout_s[slot, 0] = d[:, :half]
-        dout_s[slot, 1] = d[:, half:]
-        for c in stores(j, slot):
+        dout_s[0] = d[:, :half]
+        dout_s[1] = d[:, half:]
+        for c in stores(j):
             c.start()
+        reduce(j, 1, "step2")
         return carry
 
     lax.fori_loop(0, total, step, 0)
@@ -1105,59 +1486,81 @@
         rc = rc_ref[r, :]
         res = res_ref[r, :] + b6_ref[...]
         gf = jnp.where(ok, cot_ref[r, :].astype(F32), 0.0)
-        out_ref[r, :] = jnp.where(ok, rc + mods_ref[5] * res, 0.0).astype(BF)
+        out_ref[r, :] = jnp.where(ok, rc + mods_ref[2] * res, 0.0).astype(BF)
         xhat, rstd = normalise(rc)
         g = grc_ref[r, :]
         gp_ref[0] += g
         gp_ref[1] += g * xhat
         gp_ref[2] += gf * res
-        grc_ref[r, :] = gf + normalise_back(xhat, rstd, g, mods_ref[4])
+        grc_ref[r, :] = gf + normalise_back(xhat, rstd, g, mods_ref[1])
 
     each(frames, finish)
-    for back in (2, 1):
-        for c in stores(total - back, (total - back) % 2):
-            c.wait()
-
-
-def mlp_call(patches, nm, cot, valid, rc, mods, hb, b6, win, wout):
+    for c in stores(total - 1):
+        c.wait()
+    for unit in units:
+        unit.finish()
+
+
+def mlp_call(patches, nm, cot, valid, rc, mods, hb, b6, win, wout, shard, plan, ident):
     rows, width = nm.shape
     chunk = 768
     total = 2 * win.shape[2] // chunk
     half = wout.shape[2]
+    m = plan.n
+    comm_scratch = plan.head_scratch()
     S = jax.ShapeDtypeStruct
-    return pl.pallas_call(
-        partial(mlp_kernel, chunk, patches),
+    out = pl.pallas_call(
+        partial(mlp_kernel, chunk, patches, plan),
         out_shape=[
             S((rows, width), BF), S((rows, width), F32), S((total, chunk), F32), S((8, width), F32), S((3, patches, width), F32),
-            S(win.shape, BF), S(wout.shape, BF),
-        ],
+            S((2, 4, 2, 2) + shard, BF), S(wout.shape, BF),
+        ]
+        + plan.r1_shapes
+        + plan.halves
+        + plan.halves,
         in_specs=[IN_VMEM] * 7 + [IN_ANY] * 2,
-        out_specs=[IN_VMEM] * 5 + [IN_ANY] * 2,
+        out_specs=[IN_VMEM] * 5 + [IN_ANY] * (2 + 3 * m),
         scratch_shapes=[
             pltpu.VMEM((rows, width), BF), pltpu.VMEM((rows, width), F32),
             pltpu.VMEM((2, width, chunk), BF), pltpu.VMEM((2, 2, chunk, half), BF), pltpu.VMEM((chunk, width), BF),
             pltpu.VMEM((rows, chunk), BF), pltpu.VMEM((rows, chunk), BF),
-            pltpu.VMEM((2, width, chunk), BF), pltpu.VMEM((2, 2, chunk, half), BF),
-            pltpu.SemaphoreType.DMA((2, 2)), pltpu.SemaphoreType.DMA((2, 2)),
-        ],
-        compiler_params=pltpu.CompilerParams(vmem_limit_bytes=VMEM_LIMIT),
+            pltpu.VMEM((4, 2, 2, width // 16, chunk), BF), pltpu.VMEM((2, chunk, half), BF),
+            pltpu.SemaphoreType.DMA((2, 2)), pltpu.SemaphoreType.DMA((2,)),
+        ]
+        + comm_scratch,
+        compiler_params=pltpu.CompilerParams(collective_id=ident, has_side_effects=True, vmem_limit_bytes=VMEM_LIMIT),
         name="mlp",
     )(nm, cot, valid, rc, mods, hb.reshape(total, chunk), b6, win, wout)
+    return out[:7], out[7 + m : 7 + 2 * m], out[7 + 2 * m :]
 
 
 def cross_back_kernel(
-    patches, heads, grc_ref, mixb_ref, q_ref, keys_ref, vals_ref, lse_ref, cm_ref, residb_ref, attn_ref, ao_ref, gate_ref,
-    wco_ref, wq_ref, wo_ref,
-    gra_ref, gai_ref, gkvb_ref, bsum_ref, gp_ref, dwo_ref, dwq_ref, dwco_ref,
-    w_buf, gcb, gmix, gq, gkv, p_buf, ds_buf, cmask, dw_s, sems, out_sem,
+    patches, heads, tail, plan, extra, n, cuts, grc_ref, q_ref, keys_ref, vals_ref, lse_ref, cm_ref, gate_ref,
+    mixb_ref, residb_ref, attn_ref, ao_ref, wco_ref, wq_ref, wo_ref, *refs
 ):
+    m, mt = plan.n, tail.n
+    parts, keeps_in, r2s_in, outs8, shards, r1s, r2s, keeps, tmp, refs = take(refs, n, mt, mt, 8, 1, m, m, m, 3)
+    gra_ref, gai_ref, gkvb_ref, bsum_ref, gp_ref, dwo_ref, dwq_ref, dwco_ref = outs8
+    (w_buf, a_buf, gcb, gmix, gkv, p_buf, ds_buf, cmask, dw_s, sems, out_sem), h_refs, t_refs, x_refs, _ = take(refs, 11, *cuts)
+    pos = Place()
     rows, width = grc_ref.shape
     frames = rows // patches
     half = width // 2
     scale = (width // heads) ** (-0.5)
+    gq = gra_ref
     loads = [pltpu.make_async_copy(src, w_buf, sems.at[i]) for i, src in enumerate((wco_ref, wq_ref, wo_ref))]
-    outs = [pltpu.make_async_copy(dw_s.at[i % 2], dst, out_sem.at[i]) for i, dst in enumerate((dwco_ref, dwq_ref, dwo_ref))]
+    acts = [
+        pltpu.make_async_copy(src, a_buf.at[i % 2], sems.at[3 + i])
+        for i, src in enumerate((mixb_ref, residb_ref, ao_ref, attn_ref))
+    ]
+    outs = [pltpu.make_async_copy(dw_s, dst, out_sem.at[i]) for i, dst in enumerate((dwco_ref, dwq_ref, dwo_ref))]
     loads[0].start()
+    acts[0].start()
+    acts[1].start()
+    barrier(pos)
+    tails = scatter_tail_process(tail.tail_bind(pos, keeps_in, r2s_in, shards, t_refs), tail.deep, 4)
+    tick = Ticker(both_processes(scatter_head_process(plan.head_bind(pos, parts, r1s, r2s, keeps, h_refs), plan.deep), tails))
+    tick()
     for i in range(3):
         cmask[i * patches : (i + 1) * patches, :] = cm_ref[...]
     bsum_ref[...] = jnp.zeros(bsum_ref.shape, F32)
@@ -1179,15 +1582,22 @@
     def weight_grad(k, left, right):
         d = dot_tn(left, right).astype(BF)
         for f in range(2):
-            dw_s[k % 2, f] = d[:, f * half : (f + 1) * half]
+            dw_s[f] = d[:, f * half : (f + 1) * half]
         outs[k].start()
 
-    weight_grad(0, mixb_ref[...], gcb[...])
+    acts[0].wait()
+    weight_grad(0, a_buf[0], gcb[...])
+    acts[2].start()
+    tick()
     for h in range(heads):
         cross_head_back(
             h, heads, rows // cmask.shape[0], q_ref, keys_ref, vals_ref, cmask, lse_ref, gmix, gq, gkv, p_buf, ds_buf
         )
-    gkvb_ref[...] = gkv[...].astype(BF)
+        if h % 2:
+            tick()
+    gkvb_ref[...] = gkv[...].reshape(gkvb_ref.shape).astype(BF)
+    captions = Ticker(scatter_head_process(extra.head_bind(pos, [gkvb_ref], tmp[:1], tmp[1:2], tmp[2:3], x_refs)))
+    captions()
 
     def second(s):
         r = rows_at(s * patches, patches)
@@ -1196,84 +1606,120 @@
         bsum_ref[1:2, :] += jnp.sum(g.astype(F32), axis=0, keepdims=True)
 
     each(frames, second)
-    weight_grad(1, residb_ref[...], gcb[...])
+    captions()
+    acts[1].wait()
+    outs[0].wait()
+    weight_grad(1, a_buf[1], gcb[...])
+    acts[3].start()
+    tick()
+    captions()
     loads[1].wait()
     gra_ref[...] = dot_nt(gcb[...], w_buf[...])
     loads[2].start()
+    acts[2].wait()
+    tick()
+    captions()
 
     def third(s):
         r = rows_at(s * patches, patches)
         gra = gra_ref[r, :] + grc_ref[r, :]
         gra_ref[r, :] = gra
-        gp_ref[...] += gra * ao_ref[r, :].astype(F32)
+        gp_ref[...] += gra * a_buf[0, r, :].astype(F32)
         g = (gate_ref[...] * gra).astype(BF)
         gmix[r, :] = g
         bsum_ref[2:3, :] += jnp.sum(g.astype(F32), axis=0, keepdims=True)
 
     each(frames, third)
     loads[2].wait()
+    tick()
     gai_ref[...] = dot_nt(gmix[...], w_buf[...]).astype(BF)
-    outs[0].wait()
-    weight_grad(2, attn_ref[...], gmix[...])
+    tick()
+    acts[3].wait()
     outs[1].wait()
+    weight_grad(2, a_buf[1], gmix[...])
+    tick.drain()
+    captions.drain()
     outs[2].wait()
 
 
-def cross_back_call(patches, heads, grc, mixb, q, keys, vals, lse, cm, residb, attn, ao, gate, wco, wq, wo):
+def cross_back_call(
+    patches, heads, grc, mixb, q, keys, vals, lse, cm, residb, attn, ao, gate, wco, wq, wo, keeps, r2s, tail, tail_outs, parts, plan, ident
+):
     rows, width = grc.shape
     caps = keys.shape[0]
+    n = len(parts)
+    m, mt = plan.n, tail.n
+    kv_blocks = (caps // 16, width)
+    extra = ScatterPlan([kv_blocks], SCATTER_KV)
+    scratches = [plan.head_scratch(), tail.tail_scratch(), extra.head_scratch()]
     S = jax.ShapeDtypeStruct
-    return pl.pallas_call(
-        partial(cross_back_kernel, patches, heads),
+    out = pl.pallas_call(
+        partial(cross_back_kernel, patches, heads, tail, plan, extra, n, [len(s) for s in scratches]),
         out_shape=[
-            S((rows, width), F32), S((rows, width), BF), S((2, caps, width), BF), S((8, width), F32), S((patches, width), F32),
+            S((rows, width), F32), S((rows, width), BF), S((2, 4, 2, 2) + kv_blocks, BF), S((8, width), F32), S((patches, width), F32),
         ]
-        + [S((2, width, width // 2), BF)] * 3,
-        in_specs=[IN_VMEM] * 11 + [IN_ANY] * 3,
-        out_specs=[IN_VMEM] * 5 + [IN_ANY] * 3,
+        + [S((2, width, width // 2), BF)] * 3
+        + [S(tail_outs, F32)]
+        + plan.r1_shapes
+        + plan.halves
+        + plan.halves
+        + extra.r1_shapes
+        + extra.halves
+        + extra.halves,
+        in_specs=[IN_VMEM] * 7 + [IN_ANY] * (7 + n + 2 * mt),
+        out_specs=[IN_VMEM] * 5 + [IN_ANY] * 3 + [IN_VMEM] + [IN_ANY] * (3 * m + 3),
         scratch_shapes=[
-            pltpu.VMEM((width, width), BF), pltpu.VMEM((rows, width), BF), pltpu.VMEM((rows, width), BF),
-            pltpu.VMEM((rows, width), F32), pltpu.VMEM((2, caps, width), F32),
+            pltpu.VMEM((width, width), BF), pltpu.VMEM((2, rows, width), BF), pltpu.VMEM((rows, width), BF), pltpu.VMEM((rows, width), BF),
+            pltpu.VMEM((2, caps, width), F32),
             pltpu.VMEM((rows, caps), BF), pltpu.VMEM((rows, caps), BF), pltpu.VMEM((3 * patches, caps), F32),
-            pltpu.VMEM((2, 2, width, width // 2), BF),
-            pltpu.SemaphoreType.DMA((3,)), pltpu.SemaphoreType.DMA((3,)),
-        ],
-        compiler_params=pltpu.CompilerParams(vmem_limit_bytes=VMEM_LIMIT),
+            pltpu.VMEM((2, width, width // 2), BF),
+            pltpu.SemaphoreType.DMA((7,)), pltpu.SemaphoreType.DMA((3,)),
+        ]
+        + sum(scratches, []),
+        compiler_params=pltpu.CompilerParams(collective_id=ident, has_side_effects=True, vmem_limit_bytes=VMEM_LIMIT),
         name="cross_back",
-    )(grc, mixb, q, keys, vals, lse, cm, residb, attn, ao, gate, wco, wq, wo)
+    )(grc, q, keys, vals, lse, cm, gate, mixb, residb, attn, ao, wco, wq, wo, *parts, *keeps, *r2s)
+    return out[:8], out[8], out[9 + m : 9 + 2 * m], out[9 + 2 * m : 9 + 3 * m], (out[11 + 3 * m], out[10 + 3 * m])
 
 
 def attend_back_kernel(
-    patches, heads, gai_ref, q_ref, kvx_ref, probs_ref, e_ref, et_ref, info_ref, nm_ref, x_ref, scale_ref, gra_ref, wqkv_ref,
-    ig_ref, bsum_ref, gp_ref, dw_ref,
-    w_buf, gqb, gkb, gvb, gkv, halo_out, halo_in, dw_s, sems, send, recv,
+    patches, heads, tail, head, extra, n, cuts, gai_ref, q_ref, kvx_ref, probs_ref, e_ref, et_ref, info_ref, nm_ref, *refs
 ):
+    mt, mh = tail.n, head.n
+    keeps_in, r2s_in, parts, kv_keep, kv_r2, outs5, shards, r1s, r2s, keeps, refs = take(refs, mt, mt, n, 1, 1, 5, 3, mh, mh, mh)
+    gq_ref, gk_ref, gv_ref, bsum_ref, dw_ref = outs5
+    (gkv, halo_out, halo_in, dw_s, a_buf, sems, send, recv), t_refs, h_refs, xt_refs, _ = take(refs, 8, *cuts)
+    loads = (pltpu.make_async_copy(gai_ref, a_buf, sems.at[2]), pltpu.make_async_copy(nm_ref, a_buf, sems.at[3]))
+    loads[0].start()
     pos = Place()
-    rows, width = x_ref.shape
+    rows, width = q_ref.shape
     frames = rows // patches
     half = width // 2
     count, y = info_ref[0], info_ref[1]
-    load = pltpu.make_async_copy(wqkv_ref, w_buf, sems.at[0])
-    load.start()
-    pair_barrier(pos)
+    barrier(pos)
+    tails = scatter_tail_process(tail.tail_bind(pos, keeps_in, r2s_in, shards[:2], t_refs), tail.deep, 4)
+    heads_ = scatter_head_process(head.head_bind(pos, parts, r1s, r2s, keeps, h_refs))
+    captions = scatter_tail_process(extra.tail_bind(pos, kv_keep, kv_r2, shards[2:], xt_refs))
+    tick = Ticker(both_processes(captions, tails, heads_))
+    tick()
     gkv[...] = jnp.zeros(gkv.shape, F32)
+    tick()
     scale = (width // heads) ** (-0.5)
-    each(
-        frames // 3,
-        lambda t: attend_tile_back(t, 3, patches, scale, q_ref, kvx_ref, e_ref, et_ref, probs_ref, gai_ref, gqb, gkv),
-    )
+    loads[0].wait()
+    for t in range(frames // 3):
+        attend_tile_back(t, 3, patches, scale, q_ref, kvx_ref, e_ref, et_ref, probs_ref, a_buf, gq_ref, gkv)
+        tick()
+    loads[1].start()
     place = jnp.where(y == 0, count, -1) + 1
     pick_slot(frames + 2, patches, place, gkv, halo_out)
-    copy = pltpu.make_async_remote_copy(
-        src_ref=halo_out, dst_ref=halo_in, send_sem=send, recv_sem=recv,
-        device_id=pos.dev(y=1 - pos.y), device_id_type=MESH,
-    )
+    copy = remote(halo_out, halo_in, send, recv, 0, pos.dev(y=1 - pos.y))
     copy.start()
     bsum_ref[...] = jnp.zeros(bsum_ref.shape, F32)
-    gp_ref[...] = jnp.zeros(gp_ref.shape, F32)
-    dw_s[:, :width] = dot_tn(nm_ref[...], gqb[...]).astype(BF)
-    load.wait()
-    ig_ref[...] = dot_nt(gqb[...], w_buf[:, :width])
+    loads[1].wait()
+    for low, high in ((0, 640), (640, width)):
+        tick()
+        dw_s[:, low:high] = dot_tn(a_buf[...], gq_ref[:, low:high]).astype(BF)
+    tick()
     copy.wait()
     mine = jnp.where(y == 0, count - 1, 0) + 1
 
@@ -1285,69 +1731,284 @@
         add = jnp.full(shape, (s + 1 == mine).astype(F32), F32)
         g = jnp.where(drop > 0.5, 0.0, gkv[r, :]) + jnp.where(add > 0.5, halo_in[...].astype(F32), 0.0)
         g = g.astype(BF)
-        gkb[o, :] = g[:, :width]
-        gvb[o, :] = g[:, width:]
-        bsum_ref[0:1, :] += jnp.sum(gqb[o, :].astype(F32), axis=0, keepdims=True)
+        gk_ref[o, :] = g[:, :width]
+        gv_ref[o, :] = g[:, width:]
+        bsum_ref[0:1, :] += jnp.sum(gq_ref[o, :].astype(F32), axis=0, keepdims=True)
         bsum_ref[1:2, :] += jnp.sum(g[:, width:].astype(F32), axis=0, keepdims=True)
 
     each(frames, settle)
-    late = pltpu.make_async_copy(gra_ref, gkv.at[pl.ds(0, rows), pl.ds(0, width)], sems.at[2])
-    late.start()
-    dw_s[:, width:] = dot_tn(nm_ref[...], gkb[:, :half]).astype(BF)
-    out = [pltpu.make_async_copy(dw_s, dw_ref.at[f], sems.at[1]) for f in range(2)]
+    tick()
+    dw_s[:, width:] = dot_tn(a_buf[...], gk_ref[:, :half]).astype(BF)
+    out = [pltpu.make_async_copy(dw_s, dw_ref.at[f], sems.at[f]) for f in range(2)]
     out[0].start()
-    ig_ref[...] += dot_nt(gkb[...], w_buf[:, width : 2 * width])
-    ig_ref[...] += dot_nt(gvb[...], w_buf[:, 2 * width :])
+    tick()
     out[0].wait()
-    dw_s[:, :half] = dot_tn(nm_ref[...], gkb[:, half:]).astype(BF)
-    dw_s[:, half:] = dot_tn(nm_ref[...], gvb[...]).astype(BF)
+    dw_s[:, :half] = dot_tn(a_buf[...], gk_ref[:, half:]).astype(BF)
+    tick()
+    for low, high in ((0, half), (half, width)):
+        dw_s[:, half + low : half + high] = dot_tn(a_buf[...], gv_ref[:, low:high]).astype(BF)
     out[1].start()
-    late.wait()
+    tick.drain()
+    out[1].wait()
+
+
+def attend_back_call(
+    patches, heads, gai, q, kvx, probs, e, et, info, nm, keeps, r2s, tail, tail_outs, parts, shard_shapes, units, kv_keep, kv_r2, kv_blocks, ident
+):
+    rows, width = q.shape
+    cols = 3 * width // 2
+    head = ScatterPlan(shard_shapes, units)
+    extra = ScatterPlan([kv_blocks], SCATTER_KV)
+    n, mt, mh = len(parts), tail.n, head.n
+    scratches = [tail.tail_scratch(), head.head_scratch(), extra.tail_scratch()]
+    S = jax.ShapeDtypeStruct
+    out = pl.pallas_call(
+        partial(attend_back_kernel, patches, heads, tail, head, extra, n, [len(s) for s in scratches]),
+        out_shape=[S((rows, width), BF)] * 3
+        + [S((8, width), F32), S((2, width, cols), BF)]
+        + [S(s, F32) for s in tail_outs]
+        + [S(kv_blocks, BF)]
+        + head.r1_shapes
+        + head.halves
+        + head.halves,
+        in_specs=[IN_ANY] + [IN_VMEM] * 5 + [IN_SMEM] + [IN_ANY] * (3 + 2 * mt + n),
+        out_specs=[IN_VMEM] * 4 + [IN_ANY] + [IN_VMEM] * 3 + [IN_ANY] * (3 * mh),
+        scratch_shapes=[
+            pltpu.VMEM(kvx.shape, F32), pltpu.VMEM((patches, 2 * width), BF), pltpu.VMEM((patches, 2 * width), BF),
+            pltpu.VMEM((width, cols), BF), pltpu.VMEM((rows, width), BF),
+            pltpu.SemaphoreType.DMA((4,)), pltpu.SemaphoreType.DMA((1,)), pltpu.SemaphoreType.DMA((1,)),
+        ]
+        + sum(scratches, []),
+        compiler_params=pltpu.CompilerParams(collective_id=ident, has_side_effects=True, vmem_limit_bytes=VMEM_LIMIT),
+        name="attend_back",
+    )(gai, q, kvx, probs, e, et, info, nm, *keeps, *r2s, *parts, kv_keep, kv_r2)
+    return out[:5], out[5:8], out[8 + mh : 8 + 2 * mh], out[8 + 2 * mh : 8 + 3 * mh]
+
+
+def close_kernel(
+    patches, tail, plan, gunits, cuts, gq_ref, gk_ref, gv_ref, x_ref, scale_ref, gpg_ref, gpm_ref,
+    ba_ref, bc_ref, bm_ref, hsum_ref, one_ref, used_ref,
+    gra_ref, wqkv_ref, wkv_ref, kvlow_ref, *refs
+):
+    mt, m = tail.n, plan.n
+    keeps_in, r2s_in, parts, outs6, tshards, shards, r1s, r2s, keeps, refs = take(refs, mt, mt, 1, 6, 3, 1, m, m, m)
+    ig_ref, sum_ref, last_ref, rows_ref, kvg_ref, kvfull_ref = outs6
+    mine_refs, t_refs, h_refs, c_refs, _ = take(refs, 15, *cuts)
+    w_buf, late, gp, kv_buf, lands, zland, lands2, zland2, sems, g_send, g_recv, s_send, s_recv, s_send2, s_recv2 = mine_refs
+    pos = Place()
+    rows, width = x_ref.shape
+    frames = rows // patches
+    clips = one_ref.shape[1]
+    loads = (
+        pltpu.make_async_copy(wqkv_ref, w_buf, sems.at[0]),
+        pltpu.make_async_copy(gra_ref, late, sems.at[1]),
+        pltpu.make_async_copy(wkv_ref.at[0], w_buf.at[:, pl.ds(0, width)], sems.at[2]),
+        pltpu.make_async_copy(wkv_ref.at[1], w_buf.at[:, pl.ds(width, width)], sems.at[4]),
+    )
+    loads[0].start()
+    loads[1].start()
+    barrier(pos)
+    tick = Ticker(
+        scatter_chain_process(
+            plan.head_bind(pos, parts, r1s, r2s, keeps, h_refs), plan.tail_bind(pos, keeps, r2s, shards, c_refs)
+        )
+    )
+    tick()
+    tails = tail.tail_bind(pos, keeps_in, r2s_in, tshards, t_refs)
+
+    def all_tails(step):
+        for u in tails:
+            getattr(u, step)()
+
+    all_tails("load")
+    gather = Ticker(gather_process(gather_units(pos, gunits, [kvlow_ref], [kvfull_ref], g_send, g_recv)))
+    gather()
+    gp[...] = jnp.zeros(gp.shape, F32)
+    tick()
+    all_tails("step1")
+    base = 4 * clips
+    sum_ref[...] = jnp.zeros(sum_ref.shape, F32)
+    sum_ref[base : base + 2, :] = ba_ref[0:2, :]
+    sum_ref[base + 2 : base + 3, :] = bc_ref[2:3, :]
+    sum_ref[base + 3 : base + 4, :] = bc_ref[1:2, :]
+    sum_ref[base + 5 : base + 6, :] = bc_ref[0:1, :]
+    sum_ref[base + 6 : base + 7, :] = bm_ref[0:1, :]
+    sum_ref[base + 7 : base + 11, :] = hsum_ref[...]
+
+    def clip_sums(ref, base, step, grads):
+        for k, g in enumerate(grads):
+            for c in range(clips):
+                at = base + c * step + k
+                ref[at : at + 1, :] = jnp.sum(one_ref[:, c : c + 1] * g, axis=0, keepdims=True)
+
+    clip_sums(sum_ref, 0, 4, (gpg_ref[...], gpm_ref[0], gpm_ref[1], gpm_ref[2]))
+    small = Ticker(sum_process(pos, sum_ref, [lands.at[i] for i in range(3)], zland, s_send, s_recv))
+    small()
+    loads[0].wait()
+    tick()
+    ig_ref[...] = dot_nt(gq_ref[...], w_buf[:, :width])
+    tick()
+    gather()
+    ig_ref[...] += dot_nt(gk_ref[...], w_buf[:, width : 2 * width])
+    tick()
+    small()
+    ig_ref[...] += dot_nt(gv_ref[...], w_buf[:, 2 * width :])
+    loads[2].start()
+    loads[3].start()
+    loads[1].wait()
+    gather()
+    tick()
+    small()
 
     def finish(s):
         r = rows_at(s * patches, patches)
         xhat, rstd = normalise(x_ref[r, :].astype(F32))
         g = ig_ref[r, :]
-        gp_ref[0] += g
-        gp_ref[1] += g * xhat
-        ig_ref[r, :] = gkv[r, :width] + normalise_back(xhat, rstd, g, scale_ref[...])
+        gp[0] += g
+        gp[1] += g * xhat
+        ig_ref[r, :] = late[r, :] + normalise_back(xhat, rstd, g, scale_ref[...])
 
     each(frames, finish)
-    out[1].wait()
-
-
-def attend_back_call(patches, heads, gai, q, kvx, probs, e, et, info, nm, x, scale, gra, wqkv, ident):
-    cols = 3 * x.shape[1] // 2
+    clip_sums(last_ref, 0, 2, (gp[0], gp[1]))
+    last = Ticker(sum_process(pos, last_ref, [lands2.at[i] for i in range(3)], zland2, s_send2, s_recv2))
+    last()
+    small()
+    tick()
+    all_tails("step2")
+    gather()
+    last()
+    tick()
+    small.drain()
+    last()
+    tick()
+    gather.drain()
+    full = pltpu.make_async_copy(kvfull_ref, kv_buf, sems.at[3])
+    full.start()
+    last()
+    tick()
+    loads[2].wait()
+    loads[3].wait()
+    full.wait()
+    kv0 = kv_buf[0].reshape(used_ref.shape[0], width)
+    kv1 = kv_buf[1].reshape(used_ref.shape[0], width)
+    rows_ref[...] = dot_nt(kv0, w_buf[:, :width]) + dot_nt(kv1, w_buf[:, width : 2 * width])
+    last.drain()
+    tick()
+    mine = kv_buf[pos.y].reshape(used_ref.shape[0], width)
+    kvg_ref[...] = dot_tn(used_ref[...], mine)
+    sum_ref[20:21, :] = sum_ref[20:21, :] + jnp.sum(kv1.astype(F32), axis=0, keepdims=True)
+    tick.drain()
+    all_tails("step3")
+
+
+def scatter_chain_process(heads, tails, lags=(1, 3, 4, 5, 6, 8)):
+    for u in heads:
+        u.send()
+    yield
+    total = len(heads)
+    order = (
+        (5, tails, "step3"), (4, tails, "step2"), (3, tails, "step1"), (2, tails, "load"), (1, heads, "step2"), (0, heads, "step1"),
+    )
+    for t in range(total + lags[5]):
+        for i, units, step in order:
+            if 0 <= t - lags[i] < total:
+                getattr(units[t - lags[i]], step)()
+        if t < total:
+            heads[t].load()
+        yield
+    for u in heads:
+        u.finish()
+
+
+def close_call(
+    patches, gq, gk, gv, x, scale, gpg, gpm, ba, bc, bm, hsum, one, used, gra, wqkv, wkv, kvlow, keeps, r2s, tail, tail_outs, part, shard_shape,
+    units, gunits, ident,
+):
     rows, width = x.shape
+    plan = ScatterPlan([shard_shape], units)
+    mt, m = tail.n, plan.n
+    scratches = [tail.tail_scratch(), plan.head_scratch(), plan.tail_scratch()]
     S = jax.ShapeDtypeStruct
-    return pl.pallas_call(
-        partial(attend_back_kernel, patches, heads),
-        out_shape=[S((rows, width), F32), S((8, width), F32), S((2, patches, width), F32), S((2, width, cols), BF)],
-        in_specs=[IN_VMEM] * 6 + [IN_SMEM] + [IN_VMEM] * 3 + [IN_ANY] * 2,
-        out_specs=[IN_VMEM] * 3 + [IN_ANY],
+    full = gather_shapes([kvlow])
+    least = (8, width)
+    most = (4 * one.shape[1] + 16, width)
+    out = pl.pallas_call(
+        partial(close_kernel, patches, tail, plan, gunits, [len(s) for s in scratches]),
+        out_shape=[
+            S((rows, width), F32), S(most, F32), S(least, F32), S((used.shape[0], width), F32), S((used.shape[1], width), F32),
+        ]
+        + full
+        + [S(s, F32) for s in tail_outs]
+        + [S(shard_shape, F32)]
+        + plan.r1_shapes
+        + plan.halves
+        + plan.halves,
+        in_specs=[IN_VMEM] * 13 + [IN_ANY] * (4 + 2 * mt + 1),
+        out_specs=[IN_VMEM] * 5 + [IN_ANY] + [IN_VMEM] * 4 + [IN_ANY] * (3 * m),
         scratch_shapes=[
-            pltpu.VMEM(wqkv.shape, BF), pltpu.VMEM((rows, width), BF), pltpu.VMEM((rows, width), BF), pltpu.VMEM((rows, width), BF),
-            pltpu.VMEM(kvx.shape, F32), pltpu.VMEM((patches, 2 * width), BF), pltpu.VMEM((patches, 2 * width), BF),
-            pltpu.VMEM((width, cols), BF),
-            pltpu.SemaphoreType.DMA((3,)), pltpu.SemaphoreType.DMA, pltpu.SemaphoreType.DMA,
-        ],
+            pltpu.VMEM(wqkv.shape, BF), pltpu.VMEM((rows, width), F32), pltpu.VMEM((2, patches, width), F32),
+            pltpu.VMEM(full[0].shape, BF), pltpu.VMEM((3,) + most, F32), pltpu.VMEM((4,) + most, F32),
+            pltpu.VMEM((3,) + least, F32), pltpu.VMEM((4,) + least, F32),
+            pltpu.SemaphoreType.DMA((5,)),
+        ]
+        + gather_sems(gunits)
+        + [pltpu.SemaphoreType.DMA((6,))] * 4
+        + sum(scratches, []),
         compiler_params=pltpu.CompilerParams(collective_id=ident, has_side_effects=True, vmem_limit_bytes=VMEM_LIMIT),
-        name="attend_back",
-    )(gai, q, kvx, probs, e, et, info, nm, x, scale, gra, wqkv)
-
-
-UNITS_ALL = (
-    (0, None, (0, 896), "x"),
-    (0, None, (896, 832), "y"),
-    (1, None, None, "x"),
-    (2, None, None, "y"),
-    (3, None, None, "x"),
-    (4, None, None, "y"),
-    (5, None, (0, 1152), "x"),
-    (5, None, (1152, 1152), "y"),
-    (6, (0, 144), None, "x"),
-    (6, (144, 144), None, "y"),
+        name="close",
+    )(gq, gk, gv, x, scale, gpg, gpm, ba, bc, bm, hsum, one, used, gra, wqkv, wkv, kvlow, *keeps, *r2s, part)
+    return out[:5], out[6:9], out[9]
+
+
+GATHER_OPEN = (
+    (0, None, (0, 512), "zxy"),
+    (0, None, (512, 512), "zyx"),
+    (0, None, (1024, 256), "zxy"),
+    (1, None, None, "zyx"),
+    (0, None, (1280, 448), "zxy"),
 )
+GATHER_ATTEND = (
+    (0, None, None, "zxy"),
+    (1, None, None, "zyx"),
+    (2, None, (0, 640), "zxy"),
+    (2, None, (640, 512), "zyx"),
+)
+GATHER_CROSS = (
+    (0, None, (0, 256), "xyz"),
+    (0, None, (256, 384), "zxy"),
+    (0, None, (640, 384), "zyx"),
+    (0, None, (1024, 384), "zxy"),
+    (0, None, (1408, 384), "zyx"),
+    (1, (0, 64), None, "xyz"),
+    (0, None, (1792, 256), "zxy"),
+    (0, None, (2048, 256), "zyx"),
+    (1, (64, 48), None, "zxy"),
+    (1, (112, 48), None, "zyx"),
+    (1, (160, 32), None, "zxy"),
+    (1, (192, 32), None, "zyx"),
+    (1, (224, 32), None, "zxy"),
+    (1, (256, 32), None, "zyx"),
+)
+SCATTER_EARLY = tuple((0, None, (384 * i, 384), ("xyz", "yxz")[i % 2], 0) for i in range(4))
+SCATTER_LATE = (
+    (0, None, (1920, 384), "yxz", 0),
+    (1, (0, 48), None, "yxz", 0),
+    (1, (48, 48), None, "xyz", 0),
+    (1, (96, 48), None, "yxz", 0),
+    (0, None, (1536, 384), "xyz", 0),
+    (1, (144, 48), None, "xyz", 0),
+    (1, (192, 48), None, "yxz", 0),
+    (1, (240, 48), None, "xyz", 0),
+)
+SCATTER_MID = (
+    (2, None, None, "xyz", 0),
+    (1, None, None, "yxz", 0),
+    (0, None, (0, 256), "xyz", 0),
+    (0, None, (256, 320), "yxz", 0),
+)
+SCATTER_CLOSE = tuple((0, None, (256 * i, 256 if i < 6 else 192), ("xyz", "yxz")[i % 2], 0) for i in range(7))
+SCATTER_KV = ((0, None, None, "xyz", 0),)
+GATHER_CLOSE = ((0, None, None, "zxy"),)
 
 
 def fast_body(
@@ -1373,12 +2034,7 @@
     time_rows, time_cols = time_proj.shape
     features = time_features(timesteps, time_rows * lax.axis_size("patches")).astype(BF)
     own_features = lax.dynamic_slice_in_dim(features, patch_index * time_rows, time_rows, 1)
-    time_part = lax.dynamic_update_slice(
-        jnp.zeros((clips, 6 * width), F32), forward_dot(own_features, time_proj), (0, frame_index * time_cols)
-    )
-    time_sum = lax.psum(time_part, ("frames", "patches"))
-    modulation = table.astype(F32) + time_sum.reshape(clips, 6, width)
-    mods = jnp.einsum("pc,ckd->kpd", onehot, modulation, precision=HIGH)
+    time_part = jnp.pad(forward_dot(own_features, time_proj), ((0, 8 - clips), (0, 0)))
     used = jnp.where(null_mask[:, None, None] == 1, null_embed[None], caption)
     used = jnp.pad(used, ((0, 0), (0, cap_pad - cap_len), (0, 0))).reshape(clips * cap_pad, width)
     key_ids = jnp.arange(clips * cap_pad, dtype=jnp.int32)
@@ -1390,40 +2046,52 @@
     info = jnp.stack([count, frame_index]).astype(jnp.int32)
     qkv_bias = jnp.concatenate([bias_f[0], jnp.zeros((width,), F32), bias_f[1]])[None]
 
-    got = gather_call([self_qkv, self_out, cross_q, cross_out, cross_kv, mlp_in, mlp_out], UNITS_ALL, 0)
-    w_qkv, w_out, w_q, w_co, w_kv, w_in, w_mo = [g.reshape(2, -1, g.shape[-1]) for g in got]
     x = tokens.reshape(rows, width)
     cot = cotangent.reshape(rows, width)
-    nm_a = norm_call(patches, x, mods)
-    wqkv, wo, q, kvx, probs, attn, ao, resid, residb = attend_call(
-        patches, heads, nm_a, x, mods, w_qkv, w_out, qkv_bias, bias_f[2:3], e, et, info, 3
-    )
-    wq, wco, cq, keys, vals, lse, mixb, rc, nm_m = cross_call(
-        patches, heads, resid, residb, mods, used, cmask, w_q, w_co, w_kv, bias_f[3:4], bias_f[4:5], bias_f[5:6]
-    )
-    block_out, grc, hsum, bsum_m, gp_m, dw_in, dw_mo = mlp_call(
-        patches, nm_m, cot, valid, rc, mods, hidden_bias.astype(F32), bias_f[6:7], w_in, w_mo
-    )
-    gra, gai, gkv, bsum_c, gp_g, dwo, dwq, dwco = cross_back_call(
-        patches, heads, grc, mixb, cq, keys, vals, lse, cmask, residb, attn, ao, mods[2], wco, wq, wo
-    )
-    input_grad, bsum_a, gp_a, dwqkv = attend_back_call(
-        patches, heads, gai, q, kvx, probs, e, et, info, nm_a, x, mods[1], gra, wqkv, 4
-    )
-    per_patch = jnp.stack([gp_a[0], gp_a[1], gp_g, gp_m[0], gp_m[1], gp_m[2]], axis=1)
-    mod_part = jnp.einsum("pc,pkd->ckd", onehot, per_patch, precision=HIGH)
-    bias_part = jnp.stack(
-        [bsum_a[0], bsum_a[1], bsum_c[2], bsum_c[1], jnp.zeros((width,), F32), bsum_c[0], bsum_m[0]]
-    )
-    kv_total, bias_total, hidden_total, mod_total = lax.psum(
-        (gkv.astype(F32), bias_part, hsum.reshape(-1), mod_part), ("frames", "patches")
-    )
-    kv_low = kv_total.astype(BF)
-    bias_cv = jnp.sum(kv_low[1].astype(F32), axis=0)
-    biases_grad = bias_total.at[4].add(bias_cv)
+    (nm_a, scale_a, gate_a, mods_m), (w_qkv, w_out), begun = open_call(
+        patches, x, time_part, table.astype(F32), onehot, [self_qkv, self_out], GATHER_OPEN,
+        [cross_q, cross_out, cross_kv], GATHER_ATTEND, 0,
+    )
+    (wqkv, wo, q, kvx, probs, attn, ao, resid, residb), (w_q, w_co, w_kv), begun = attend_call(
+        patches, heads, nm_a, x, gate_a, w_qkv, w_out, qkv_bias, bias_f[2:3], e, et, info,
+        [cross_q, cross_out, cross_kv], begun, GATHER_ATTEND, [mlp_in, mlp_out], GATHER_CROSS, 1,
+    )
+    (wq, wco, cq, keys, vals, lse, mixb, rc, nm_m), (w_in, w_mo) = cross_call(
+        patches, heads, resid, residb, mods_m, used, cmask, w_q, w_co, w_kv, bias_f[3:4], bias_f[4:5], bias_f[5:6],
+        [mlp_in, mlp_out], begun, GATHER_CROSS, 2,
+    )
+    mlp_shapes = [mlp_in.shape, mlp_out.shape]
+    early, late = ScatterPlan(mlp_shapes, SCATTER_EARLY, 4, 2), ScatterPlan(mlp_shapes, SCATTER_LATE, 4)
+    (block_out, grc, hsum, bsum_m, gp_m, dw_in, dw_mo), landed, kept = mlp_call(
+        patches, nm_m, cot, valid, rc, mods_m, hidden_bias.astype(F32), bias_f[6:7], w_in, w_mo, mlp_in.shape, early, 6
+    )
+
+    def blocks(part, shard):
+        return part.reshape((2, 4, 2, 2) + shard.shape)
+
+    (gra, gai, gkv, bsum_c, gp_g, dwo, dwq, dwco), in_first, landed, kept, (kv_keep, kv_r2) = cross_back_call(
+        patches, heads, grc, mixb, cq, keys, vals, lse, cmask, residb, attn, ao, gate_a, wco, wq, wo,
+        kept, landed, early, mlp_in.shape, [dw_in, blocks(dw_mo, mlp_out)], late, 3,
+    )
+    kv_rows = clips * cap_pad // 16
+    mid_shapes = [self_out.shape, cross_q.shape, cross_out.shape]
+    (gq, gk, gv, bsum_a, dwqkv), (in_rest, mo_shard, kv_low), landed, kept = attend_back_call(
+        patches, heads, gai, q, kvx, probs, e, et, info, nm_a, kept, landed, ScatterPlan(mlp_shapes, SCATTER_LATE), mlp_shapes,
+        [blocks(dwo, self_out), blocks(dwq, cross_q), blocks(dwco, cross_out)], mid_shapes, SCATTER_MID,
+        kv_keep, kv_r2, (kv_rows, width), 4,
+    )
+    in_shard = jnp.concatenate([in_first[:, :1536], in_rest[:, 1536:]], axis=1)
     own_used = lax.dynamic_slice_in_dim(used, patch_index * cross_kv.shape[0], cross_kv.shape[0], 1)
-    cross_kv_grad = outer_sum(own_used, kv_low[frame_index])
-    caption_rows = times_transposed(kv_low[0], w_kv[0]) + times_transposed(kv_low[1], w_kv[1])
+    (input_grad, totals, last_totals, caption_rows, cross_kv_grad), (out_shard, q_shard, co_shard), qkv_shard = close_call(
+        patches, gq, gk, gv, x, scale_a, gp_g, gp_m, bsum_a, bsum_c, bsum_m, hsum.reshape(-1, width), onehot, own_used, gra, wqkv, w_kv, kv_low,
+        kept, landed, ScatterPlan(mid_shapes, SCATTER_MID, 4, 4), mid_shapes, blocks(dwqkv, self_qkv), self_qkv.shape,
+        SCATTER_CLOSE, GATHER_CLOSE, 5,
+    )
+    mod_total = jnp.concatenate(
+        [last_totals.reshape(clips, 2, width), totals[: 4 * clips].reshape(clips, 4, width)], axis=1
+    )
+    biases_grad = totals[4 * clips : 4 * clips + 7]
+    hidden_total = totals[4 * clips + 7 : 4 * clips + 11].reshape(-1)
     caption_rows = caption_rows.reshape(clips, cap_pad, width)[:, :cap_len]
     dropped = (null_mask == 1)[:, None, None]
     caption_grad = jnp.where(dropped, 0.0, caption_rows)
@@ -1432,30 +2100,6 @@
     own_mod = lax.dynamic_slice_in_dim(mod_total.reshape(clips, 6 * width), frame_index * time_cols, time_cols, 1)
     time_proj_grad = jnp.dot(own_features.astype(F32).T, own_mod, precision=HIGH)
 
-    def blocks(part, shard):
-        return part.reshape((2, 4, 2, 2) + shard.shape)
-
-    in_shard, mo_shard = scatter_call(
-        [blocks(dw_in, mlp_in), blocks(dw_mo, mlp_out)],
-        (
-            (0, None, (0, 1152), "x"),
-            (0, None, (1152, 1152), "y"),
-            (1, (0, 144), None, "x"),
-            (1, (144, 144), None, "y"),
-        ),
-        1,
-    )
-    out_shard, q_shard, co_shard, qkv_shard = scatter_call(
-        [blocks(dwo, self_out), blocks(dwq, cross_q), blocks(dwco, cross_out), blocks(dwqkv, self_qkv)],
-        (
-            (0, None, None, "x"),
-            (1, None, None, "y"),
-            (2, None, None, "x"),
-            (3, None, (0, 896), "y"),
-            (3, None, (896, 832), "x"),
-        ),
-        2,
-    )
     return (
         block_out.reshape(tokens.shape),
         input_grad.reshape(tokens.shape),

time: 993 us -> 721 us (0.73)
  blocking collectives: 145 us -> 0 us
  Pallas kernels: 772 us -> 668 us
  between operations: 15.3 us -> 1.81 us
  matrix products: 11.7 us -> 1.3 us
    psum x2 -> x0, blocking collectives: 145 us -> none  [fast_body(): lax.psum((gkv.astype(F32), bias_part, hsum.reshape(-1), mod_part), ('fram...]
    pallas_call x9 -> x7, Pallas kernels: 772 us -> 668 us  [the longest x1 105 us: close_call(): pl.pallas_call(partial(close_kernel, patches, tail, plan, gunits, [len(s)...]
    dot_general x5 -> x0, matrix products: 10.4 us -> none  [the longest x2 5.16 us: times_transposed(): jnp.einsum('re,de->rd', grad, weight, preferred_element_type=jnp.float32)]
  transfers between devices with their start and end apart: 1 -> 0, of which waited for: 0 -> 0; matrix products, arithmetic and copies ran while one was open for 2% -> 0% of each run, Pallas kernels for 23% -> 0%
where the time goes in v3:
time: 721 us; the launch traced here: 710 us
  Pallas kernels  668 us (93%)
  local copies, waits for them, and re-layouts  23.4 us (3%)
  other arithmetic  15.1 us (2%)
    pallas_call x1, Pallas kernels, close_call(): pl.pallas_call(partial(close_kernel, patches, tail, plan, gunits, [len(s)...  105 us
    pallas_call x1, Pallas kernels, cross_call(): pl.pallas_call(partial(cross_kernel, patches, heads, units, n), out_shape...  104 us
    pallas_call x1, Pallas kernels, mlp_call(): pl.pallas_call(partial(mlp_kernel, chunk, patches, plan), out_shape=[S((r...  99.8 us
    pallas_call x1, Pallas kernels, attend_call(): pl.pallas_call(partial(attend_kernel, patches, heads, units, n, hunits, h...  93.2 us
    pallas_call x1, Pallas kernels, cross_back_call(): pl.pallas_call(partial(cross_back_kernel, patches, heads, tail, plan, ext...  92.5 us
    pallas_call x1, Pallas kernels, attend_back_call(): pl.pallas_call(partial(attend_back_kernel, patches, heads, tail, head, ex...  87.7 us
    pallas_call x1, Pallas kernels, open_call(): pl.pallas_call(partial(open_kernel, patches, units, count, hunits, hcount...  85.8 us

profile of v3, /device:TPU:0, one launch (start us, length us, event | category | flops | bytes accessed | tf_op | source)
XLA Modules:
  0.0 709.8 jit_solution(16833270130842162894)
XLA Ops:
  1.4 0.6 pad_add_fusion.info_ref
  2.1 0.7 broadcast_compare_fusion.1
  2.8 0.7 convert_element_type.32
  3.4 0.8 reduce-window.8
  4.3 0.7 broadcast_compare_fusion
  5.0 0.1 fusion.14
  5.2 1.5 fusion.24
  6.7 1.3 reshape.252.hb_ref
  8.1 1.3 convert_element_type.33.table_ref
  9.4 0.7 convert_element_type.36
  10.2 0.6 broadcast_in_dim.43.qb_ref
  10.8 0.7 fusion.5.one_ref
  11.5 0.2 fusion.21
  11.7 0.7 pad.8.part_ref
  12.5 0.8 and_select_fusion.cm_ref
  13.3 0.9 fusion.e_ref
  14.2 1.1 reshape.253.valid_ref
  15.3 0.9 add_convert_fusion.et_ref
  16.2 0.2 broadcast_select_fusion
  16.5 0.9 constant_dynamic-slice_fusion.used_ref
  17.4 85.8 %open.1 = (bf16[864,1152]{1,0:T(8,128)(2,1)}, f32[96,1152]{1,0:T(8,128)}, f32[96,1152]{1,0:T(8,128)}, f32[3,96,1152]{2,1,0:T(8,128)}, bf16[2,4,2,2,72,1728]{5,4,...) custom-call(bf16[864,1152]{1,0:T(8,128)(2,1)} %bitcast.31, ...), custom_call_target="tpu_custom_call" | custom-call | tf_op jit(solution)/shard_map/open/pallas_call | solution.py:1262
  103.2 93.2 %attend.1 = (bf16[1152,3456]{1,0:T(8,128)(2,1)}, bf16[1152,1152]{1,0:T(8,128)(2,1)}, bf16[864,1152]{1,0:T(8,128)(2,1)}, bf16[1056,2304]{1,0:T(8,128)(2,1)}, f32[...) custom-call(bf16[864,1152]{1,0:T(8,128)(2,1)} %get-tuple-element.115, ...), custom_call_target="tpu_custom_call", output_to_operand_aliasing={{9}: (13, {}), {10}: (14, {}), {11}: (15, {})} | custom-call | tf_op jit(solution)/shard_map/attend/pallas_call | solution.py:1189
  196.4 104.4 %cross.1 = (bf16[1152,1152]{1,0:T(8,128)(2,1)}, bf16[1152,1152]{1,0:T(8,128)(2,1)}, bf16[864,1152]{1,0:T(8,128)(2,1)}, bf16[512,1152]{1,0:T(8,128)(2,1)}, bf16[5...) custom-call(f32[864,1152]{1,0:T(8,128)} %get-tuple-element.122.resid, ...), custom_call_target="tpu_custom_call", output_to_operand_aliasing={{9}: (13, {}), {10}: (14, {})} | custom-call | tf_op jit(solution)/shard_map/cross/pallas_call | solution.py:1346
  300.9 99.8 %mlp.1 = (bf16[864,1152]{1,0:T(8,128)(2,1)}, f32[864,1152]{1,0:T(8,128)}, f32[6,768]{1,0:T(8,128)}, f32[8,1152]{1,0:T(8,128)}, f32[3,96,1152]{2,1,0:T(8,128)}, /...) custom-call(bf16[864,1152]{1,0:T(8,128)(2,1)} %get-tuple-element.130, ...), custom_call_target="tpu_custom_call" | custom-call | tf_op jit(solution)/shard_map/mlp/pallas_call | solution.py:1512
  400.7 1.4 reshape.242.hsum_ref
  402.0 92.5 %cross_back.1 = (f32[864,1152]{1,0:T(8,128)}, bf16[864,1152]{1,0:T(8,128)(2,1)}, bf16[2,4,2,2,32,1152]{5,4,3,2,1,0:T(8,128)(2,1)}, f32[8,1152]{1,0:T(8,128)}, f3...) custom-call(f32[864,1152]{1,0:T(8,128)} %get-tuple-element.135.grc_r, ...), custom_call_target="tpu_custom_call" | custom-call | tf_op jit(solution)/shard_map/cross_back/pallas_call | solution.py:1656
  494.6 87.7 %attend_back.1 = (bf16[864,1152]{1,0:T(8,128)(2,1)}, bf16[864,1152]{1,0:T(8,128)(2,1)}, bf16[864,1152]{1,0:T(8,128)(2,1)}, f32[8,1152]{1,0:T(8,128)}, bf16[2,115...) custom-call(bf16[864,1152]{1,0:T(8,128)(2,1)} %get-tuple-element.156, ...), custom_call_target="tpu_custom_call" | custom-call | tf_op jit(solution)/shard_map/attend_back/pallas_call | solution.py:1765
  582.3 104.7 %close.1 = (f32[864,1152]{1,0:T(8,128)}, f32[32,1152]{1,0:T(8,128)}, f32[8,1152]{1,0:T(8,128)}, f32[512,1152]{1,0:T(8,128)}, f32[72,1152]{1,0:T(8,128)}, /*index...) custom-call(bf16[864,1152]{1,0:T(8,128)(2,1)} %get-tuple-element.181, ...), custom_call_target="tpu_custom_call" | custom-call | tf_op jit(solution)/shard_map/close/pallas_call | solution.py:1935
  687.0 0.9 slice.51
  687.9 0.6 reshape.249
  688.6 0.8 reshape.246
  689.4 1.4 slice.50
  690.7 0.9 slice.47
  691.7 0.7 fusion.1
  692.3 1.1 fusion.3
  693.4 0.9 slice.49
  694.4 4.1 select_reduce_fusion
  698.6 0.9 pad_maximum_fusion
  699.5 0.9 copy-done.4
  700.3 1.3 copy.57
  701.6 1.6 copy-done.3
  703.2 1.9 copy.58
  705.2 0.8 copy.59
  706.0 0.7 copy.60
  706.6 0.7 copy.61
  707.3 0.7 copy.62
  708.0 0.7 copy.63
  708.7 0.9 copy.64
  (42 shorter events, 0.6 us)
Async XLA Ops:
  0.6 10.9 %copy-start = (bf16[16,3456]{1,0:T(8,128)(2,1)S(1)}, bf16[16,3456]{1,0:T(8,128)(2,1)}, u32[]{:S(2)}) copy-start(bf16[16,3456]{1,0:T(8,128)(2,1)} %param.30) | copy-start | bytes 331780
  0.7 15.5 %copy-start.10 = (bf16[120,1152]{1,0:T(8,128)(2,1)S(1)}, bf16[120,1152]{1,0:T(8,128)(2,1)}, u32[]{:S(2)}) copy-start(bf16[120,1152]{1,0:T(8,128)(2,1)} %param.23) | copy-start | bytes 829444
  0.7 15.5 %copy-start.5 = (bf16[4,120,1152]{2,1,0:T(8,128)(2,1)S(1)}, bf16[4,120,1152]{2,1,0:T(8,128)(2,1)}, u32[]{:S(2)}) copy-start(bf16[4,120,1152]{2,1,0:T(8,128)(2,1)} %param.22) | copy-start | bytes 3317764
  16.5 180.0 %copy-start.2 = (bf16[4,128,1152]{2,1,0:T(8,128)(2,1)}, bf16[4,128,1152]{2,1,0:T(8,128)(2,1)S(1)}, u32[]{:S(2)}) copy-start(bf16[4,128,1152]{2,1,0:T(8,128)(2,1)S(1)} %pad.9) | copy-start | bytes 3538948
  694.4 4.2 copy-start.9
  698.5 1.8 copy-start.4
  700.3 2.8 copy-start.3
  703.2 2.0 copy-start.7
  703.2 2.8 copy-start.13
  703.2 3.4 copy-start.12
  703.2 4.1 copy-start.8
  703.2 6.4 copy-start.1
  705.2 2.9 copy-start.11
  705.2 3.5 copy-start.6
